TPU v7x, 512 devices: a whole 4x8x8 slice. The times are simulated.
512 devices in a mesh: seq: 32 (over y_lo, x, core), fsdp: 16 (over y_hi, z).
Axes of the slice: x: 4, y: 8 (y_hi: 2, y_lo: 4; y = y_hi * 4 + y_lo), z: 8, core: 2. Of those that a mesh axis runs over, the one named last changes fastest.
Arguments:
- query_raw: bfloat16 [16, 4096, 4096], P('fsdp', 'seq'), may hold values from -8 to 8
- key_raw: bfloat16 [16, 4096, 1024], P('fsdp', 'seq'), may hold values from -8 to 8
- value_proj: bfloat16 [16, 4096, 1024], P('fsdp', 'seq'), may hold values from -6 to 6
- out_grad: bfloat16 [16, 4096, 4096], P('fsdp', 'seq'), may hold values from -6 to 6
- query_gain: float32 [128], P('fsdp'), may hold values from 0.5 to 3.8
- key_gain: float32 [128], P('fsdp'), may hold values from 0.5 to 3.8
- turn_lengths: int32 [16, 48], P('fsdp'), may hold values from 1 to 256, 4096 in all within a row
Outputs:
- query_raw_grad: bfloat16 [16, 4096, 4096], P('fsdp', 'seq')
- key_raw_grad: bfloat16 [16, 4096, 1024], P('fsdp', 'seq')
- value_grad: bfloat16 [16, 4096, 1024], P('fsdp', 'seq')
- query_gain_grad: float32 [128], P('fsdp')
- key_gain_grad: float32 [128], P('fsdp')
Inputs may be any that keep to these rules, and one draw needn't show every extreme that they name: `turn_lengths`: each row sums to 4096; no turn is longer than 256 tokens, and every trajectory has a turn of exactly 256.
All inputs are finite; a program needn't handle non-finite values.
Results may differ from a plain program's by a relative error of at most 0.0264.
The roundings to bfloat16 on the way count: a program that leaves them out, or rounds other values in their place, can miss the bound.
Values may be sent and summed in bfloat16 or wider, within the bound.
No kernel may reach another device: no remote copies, remote signals or barrier semaphores. Data moves between devices by JAX's collectives and lax.ppermute only.
A program may use at most 128 MiB of HBM per device.

v0:
```python
import jax
import jax.numpy as jnp
from jax import lax
from jax.sharding import PartitionSpec as P

HEADS = 32
KV_HEADS = 8
HEAD_DIM = 128


norm_epsilon = 1e-06
rope_base = 1000000.0


def rotary_tables(positions, head_size):
    half_size = head_size // 2
    freqs = rope_base ** (-(jnp.arange(half_size, dtype=jnp.float32) * 2.0 / head_size))
    angles = positions.astype(jnp.float32)[:, None] * freqs[None, :]
    angles = jnp.concatenate([angles, angles], axis=1)
    return (jnp.cos(angles)[:, None, :], jnp.sin(angles)[:, None, :])


def rotate_half(values):
    half_size = values.shape[-1] // 2
    return jnp.concatenate([-values[..., half_size:], values[..., :half_size]], axis=-1)


def rotate_back(values):
    half_size = values.shape[-1] // 2
    return jnp.concatenate([values[..., half_size:], -values[..., :half_size]], axis=-1)


def norm_forward(raw, gain, cosine, sine):
    values = raw.astype(jnp.float32)
    inverse = lax.rsqrt(jnp.mean(values * values, axis=-1, keepdims=True) + norm_epsilon)
    normed = values * inverse * gain
    rotated = normed * cosine + rotate_half(normed) * sine
    return (rotated.astype(jnp.bfloat16), values, inverse)


def norm_backward(grad_rot, values, inverse, gain, cosine, sine):
    grad_rot = grad_rot.astype(jnp.float32)
    grad_normed = grad_rot * cosine + rotate_back(grad_rot * sine)
    gain_part = jnp.sum(grad_normed * values * inverse, axis=(0, 1))
    scaled = grad_normed * gain
    grad_raw = inverse * (
        scaled - values * inverse * inverse * jnp.mean(scaled * values, axis=-1, keepdims=True)
    )
    return (grad_raw.astype(jnp.bfloat16), gain_part)


def turn_ids(lengths, seq_len):
    ends = jnp.cumsum(lengths)
    positions = jnp.arange(seq_len, dtype=jnp.int32)
    return jnp.sum((positions[:, None] >= ends[None, :]).astype(jnp.int32), axis=1)


def shift_blocks(values, count, fill):
    front = jnp.full((count,) + values.shape[1:], fill, values.dtype)
    return jnp.concatenate([front, values[:-count]], axis=0)


def unshift_blocks(values, count):
    back = jnp.zeros((count,) + values.shape[1:], values.dtype)
    return jnp.concatenate([values[count:], back], axis=0)


def window_of(blocks, fill):
    return jnp.concatenate(
        [shift_blocks(blocks, 2, fill), shift_blocks(blocks, 1, fill), blocks], axis=1
    )


def attend(query, keys, values, dout, segment, seq_len):
    count = 32
    block = seq_len // count
    scale = HEAD_DIM ** (-0.5)
    query_blocks = query.reshape((count, block) + query.shape[1:])
    dout_blocks = dout.reshape((count, block) + dout.shape[1:])
    key_window = window_of(keys.reshape((count, block) + keys.shape[1:]), 0.0)
    value_window = window_of(values.reshape((count, block) + values.shape[1:]), 0.0)
    positions = jnp.arange(seq_len, dtype=jnp.int32).reshape(count, block)
    position_window = jnp.concatenate([positions - 2 * block, positions - block, positions], axis=1)
    segment_blocks = segment.reshape(count, block)
    segment_window = window_of(segment_blocks, -1)
    allowed = (
        (position_window[:, None, :] <= positions[:, :, None])
        & (position_window[:, None, :] >= 0)
        & (segment_window[:, None, :] == segment_blocks[:, :, None])
    )
    allowed = allowed[:, None, None]
    scores = (
        jnp.einsum(
            "nqkgd,nwkd->nkgqw", query_blocks, key_window, preferred_element_type=jnp.float32
        )
        * scale
    )
    masked = jnp.where(allowed, scores, -jnp.inf)
    row_max = jnp.max(masked, axis=-1, keepdims=True)
    weights = jnp.where(allowed, jnp.exp(masked - row_max), 0.0)
    probs = weights / jnp.sum(weights, axis=-1, keepdims=True)
    probs_low = probs.astype(jnp.bfloat16)
    dprobs = jnp.einsum(
        "nqkgd,nwkd->nkgqw", dout_blocks, value_window, preferred_element_type=jnp.float32
    )
    delta = jnp.sum(probs * dprobs, axis=-1, keepdims=True)
    dscore = (probs * (dprobs - delta) * scale).astype(jnp.bfloat16)
    dquery = jnp.einsum(
        "nkgqw,nwkd->nqkgd", dscore, key_window, preferred_element_type=jnp.float32
    ).astype(jnp.bfloat16)
    dkey_window = jnp.einsum(
        "nkgqw,nqkgd->nwkd", dscore, query_blocks, preferred_element_type=jnp.float32
    )
    dvalue_window = jnp.einsum(
        "nkgqw,nqkgd->nwkd", probs_low, dout_blocks, preferred_element_type=jnp.float32
    )

    def fold_back(window):
        total = (
            window[:, 2 * block :]
            + unshift_blocks(window[:, block : 2 * block], 1)
            + unshift_blocks(window[:, :block], 2)
        )
        return total.reshape((seq_len,) + window.shape[2:])

    return (dquery.reshape(query.shape), fold_back(dkey_window), fold_back(dvalue_window))


def local(query_raw, key_raw, value_proj, out_grad, query_gain, key_gain, turn_lengths):
    tok_rows = query_raw.shape[1]
    seq_devices = lax.axis_size("seq")
    seq_len = tok_rows * seq_devices
    local_heads = HEADS // seq_devices
    group_size = HEADS // KV_HEADS
    q_gain, k_gain = (
        lax.all_gather(query_gain, "fsdp", axis=0, tiled=True),
        lax.all_gather(key_gain, "fsdp", axis=0, tiled=True),
    )
    positions = lax.axis_index("seq") * tok_rows + jnp.arange(tok_rows, dtype=jnp.int32)
    cosine, sine = rotary_tables(positions, HEAD_DIM)
    query, q_values, q_inverse = norm_forward(
        query_raw[0].reshape(tok_rows, HEADS, HEAD_DIM), q_gain, cosine, sine
    )
    keys, k_values, k_inverse = norm_forward(
        key_raw[0].reshape(tok_rows, KV_HEADS, HEAD_DIM), k_gain, cosine, sine
    )
    values = value_proj[0].reshape(tok_rows, KV_HEADS, HEAD_DIM)
    dout = out_grad[0].reshape(tok_rows, HEADS, HEAD_DIM)
    segment = turn_ids(turn_lengths[0], seq_len)
    keys_wide = jnp.repeat(keys, group_size, axis=1)
    values_wide = jnp.repeat(values, group_size, axis=1)
    query_heads, key_heads, value_heads, dout_heads = (
        lax.all_to_all(query, "seq", split_axis=1, concat_axis=0, tiled=True),
        lax.all_to_all(keys_wide, "seq", split_axis=1, concat_axis=0, tiled=True),
        lax.all_to_all(values_wide, "seq", split_axis=1, concat_axis=0, tiled=True),
        lax.all_to_all(dout, "seq", split_axis=1, concat_axis=0, tiled=True),
    )
    dquery, dkeys, dvalues = attend(
        query_heads.reshape(seq_len, local_heads, 1, HEAD_DIM),
        key_heads,
        value_heads,
        dout_heads.reshape(seq_len, local_heads, 1, HEAD_DIM),
        segment,
        seq_len,
    )
    grads_back = lax.all_to_all(
        jnp.stack([dkeys, dvalues]), "seq", split_axis=1, concat_axis=2, tiled=True
    )
    kv_grads = jnp.sum(grads_back.reshape(2, tok_rows, KV_HEADS, group_size, HEAD_DIM), axis=3)
    dquery_tok = lax.all_to_all(
        dquery.reshape(seq_len, local_heads, HEAD_DIM),
        "seq",
        split_axis=0,
        concat_axis=1,
        tiled=True,
    )
    q_grad, q_gain_part = norm_backward(dquery_tok, q_values, q_inverse, q_gain, cosine, sine)
    k_grad, k_gain_part = norm_backward(
        kv_grads[0].astype(jnp.bfloat16), k_values, k_inverse, k_gain, cosine, sine
    )
    v_grad = kv_grads[1].astype(jnp.bfloat16)
    gain_shard = (
        lax.psum_scatter(q_gain_part, "fsdp", scatter_dimension=0, tiled=True),
        lax.psum_scatter(k_gain_part, "fsdp", scatter_dimension=0, tiled=True),
    )
    q_gain_grad, k_gain_grad = lax.psum((gain_shard[0], gain_shard[1]), "seq")
    return (
        q_grad.reshape(1, tok_rows, HEADS * HEAD_DIM),
        k_grad.reshape(1, tok_rows, KV_HEADS * HEAD_DIM),
        v_grad.reshape(1, tok_rows, KV_HEADS * HEAD_DIM),
        q_gain_grad,
        k_gain_grad,
    )


def solution(mesh):
    return jax.shard_map(
        local,
        mesh=mesh,
        in_specs=(
            P("fsdp", "seq", None),
            P("fsdp", "seq", None),
            P("fsdp", "seq", None),
            P("fsdp", "seq", None),
            P("fsdp"),
            P("fsdp"),
            P("fsdp", None),
        ),
        out_specs=(
            P("fsdp", "seq", None),
            P("fsdp", "seq", None),
            P("fsdp", "seq", None),
            P("fsdp"),
            P("fsdp"),
        ),
        check_vma=False,
    )
```

profile of v0, /device:TPU:1, one launch (start us, length us, event | category | flops | bytes accessed | tf_op | source)
XLA Modules:
  0.0 499.3 jit_solution(8222790564165086541)
XLA Ops:
  5.2 54.1 %all-reduce.16 = (f32[128]{0:T(128)S(1)}, f32[128]{0:T(128)S(1)}) all-reduce(f32[128]{0:T(128)S(1)} %dynamic-update-slice.1, f32[128]{0:T(128)S(1)} %dynamic-update-slice), channel_id=1, replica_groups=mesh['seq'=32,'fsdp'=16] {'fsdp'}, use_global_device_ids=true, to_apply=%add.11 | all-reduce | flops 256 | bytes 2048
  60.0 2.7 slice_negate_fusion.1
  63.2 3.6 fusion.39
  66.8 12.7 %all-to-all-start.1 = ((bf16[128,32,128]{2,0,1:T(8,128)(2,1)}), bf16[128,32,128]{2,0,1:T(8,128)(2,1)S(1)}, u32[]{:S(2)}, u32[]{:S(2)}) async-start(bf16[128,32,128]{2,0,1:T(8,128)(2,1)} %fusion.39), calls=%async_computation.1 | async-start | bytes 2097152 | tf_op jit(solution)/shard_map/all_to_all | solution.py:153
  82.7 23.4 %all-to-all-done.1 = bf16[128,32,128]{2,0,1:T(8,128)(2,1)S(1)} async-done(((bf16[128,32,128]{2,0,1:T(8,128)(2,1)}), bf16[128,32,128]{2,0,1:T(8,128)(2,1)S(1)}, u32[]{:S(2)}, u32[]{:S(2)}) %all-to-all-start.1) | async-done | bytes 1048608 | tf_op jit(solution)/shard_map/all_to_all | solution.py:153
  106.1 2.4 broadcast_in_dim.10
  108.5 5.4 %all-to-all-start = ((bf16[128,32,128]{2,0,1:T(8,128)(2,1)}), bf16[128,32,128]{2,0,1:T(8,128)(2,1)S(1)}, u32[]{:S(2)}, u32[]{:S(2)}) async-start(bf16[128,32,128]{2,0,1:T(8,128)(2,1)} %bitcast.221), calls=%async_computation | async-start | bytes 2097152 | tf_op jit(solution)/shard_map/all_to_all | solution.py:154
  114.9 25.5 %all-to-all-done = bf16[128,32,128]{2,0,1:T(8,128)(2,1)S(1)} async-done(((bf16[128,32,128]{2,0,1:T(8,128)(2,1)}), bf16[128,32,128]{2,0,1:T(8,128)(2,1)S(1)}, u32[]{:S(2)}, u32[]{:S(2)}) %all-to-all-start) | async-done | bytes 1048608 | tf_op jit(solution)/shard_map/all_to_all | solution.py:154
  141.7 5.2 %all-to-all-start.2 = ((bf16[128,32,128]{2,0,1:T(8,128)(2,1)}), bf16[128,32,128]{2,0,1:T(8,128)(2,1)S(1)}, u32[]{:S(2)}, u32[]{:S(2)}) async-start(bf16[128,32,128]{2,0,1:T(8,128)(2,1)} %bitcast.220), calls=%async_computation.2 | async-start | bytes 2097152 | tf_op jit(solution)/shard_map/all_to_all | solution.py:155
  158.3 15.3 %all-to-all-done.2 = bf16[128,32,128]{2,0,1:T(8,128)(2,1)S(1)} async-done(((bf16[128,32,128]{2,0,1:T(8,128)(2,1)}), bf16[128,32,128]{2,0,1:T(8,128)(2,1)S(1)}, u32[]{:S(2)}, u32[]{:S(2)}) %all-to-all-start.2) | async-done | bytes 1048608 | tf_op jit(solution)/shard_map/all_to_all | solution.py:155
  173.6 5.3 %all-to-all-start.3 = ((bf16[128,32,128]{2,0,1:T(8,128)(2,1)}), bf16[128,32,128]{2,0,1:T(8,128)(2,1)}, u32[]{:S(2)}, u32[]{:S(2)}) async-start(bf16[128,32,128]{2,0,1:T(8,128)(2,1)} %copy.97), calls=%async_computation.3 | async-start | bytes 2097152 | tf_op jit(solution)/shard_map/all_to_all | solution.py:156
  183.5 9.9 %fusion.7 = (f32[32,128]{1,0:T(8,128)S(1)}, f32[32,384,128]{2,1,0:T(8,128)S(1)}) fusion(s32[32,128]{1,0:T(8,128)S(1)} %bitcast.227, s32[32,384]{1,0:T(8,128)S(1)} %fusion.57, pred[32,384]{1,0:T(8,128)(4,1)S(1)} %broadcast_compare_fusion, s32[32,128]{1,0:T(8,128)S(1)} %copy-done.26, s32[32,384]{1,0:T(8,128)S(1)} %pad_add_fusion, ...), kind=kOutput, calls=%fused_computation.15 | convolution fusion | flops 432533504 | bytes 10547200 | tf_op jit(solution)/shard_map/nqkgd,nwkd->nkgqw/dot_general | solution.py:93
  193.4 2.6 copy-done.2
  196.0 6.9 %fusion.11 = f32[32,128]{1,0:T(8,128)} fusion(f32[32,384,128]{2,1,0:T(8,128)S(1)} %get-tuple-element.52, f32[32,128]{1,0:T(8,128)S(1)} %get-tuple-element.51, s32[32,128]{1,0:T(8,128)S(1)} %bitcast.228, s32[32,384]{1,0:T(8,128)S(1)} %fusion.57, pred[32,384]{1,0:T(8,128)(4,1)S(1)} %broadcast_compare_fusion, s32[32,128]{1,0:T(8,128)S(1)} %copy-done.26, ...), kind=kLoop, calls=%fused_computation.23 | loop fusion | flops 14151680 | bytes 6467584 | tf_op jit(solution)/shard_map/reduce_sum | solution.py:101
  202.9 2.6 all-to-all-done.3
  205.5 8.3 %fusion.2 = (f32[32,128]{1,0:T(8,128)S(1)}, f32[32,384,128]{2,1,0:T(8,128)S(1)}) fusion(f32[32,128]{1,0:T(8,128)} %fusion.11, f32[32,128]{1,0:T(8,128)} %copy-done.34, f32[32,384,128]{2,1,0:T(8,128)} %copy-done.2, s32[32,128]{1,0:T(8,128)S(1)} %bitcast.229, s32[32,384]{1,0:T(8,128)} %copy-done.21, pred[32,384]{1,0:T(8,128)(4,1)} %copy-done.29, ...), kind=kOutput, calls=%fused_computation.8 | convolution fusion | flops 438824960 | bytes 16871424 | tf_op jit(solution)/shard_map/nqkgd,nwkd->nkgqw/dot_general | solution.py:103
  213.9 6.5 %fusion.20 = bf16[32,128,384]{1,2,0:T(8,128)(2,1)S(1)} fusion(f32[32,384,128]{2,1,0:T(8,128)S(1)} %get-tuple-element.54, f32[32,128]{1,0:T(8,128)S(1)} %get-tuple-element.53, f32[32,128]{1,0:T(8,128)S(1)} %copy-done.37, f32[32,128]{1,0:T(8,128)S(1)} %copy-done.35, f32[32,384,128]{2,1,0:T(8,128)S(1)} %copy-done.3, s32[32,128]{1,0:T(8,128)S(1)} %bitcast.230, ...), kind=kLoop, calls=%fused_computation.31 | loop fusion | flops 20447232 | bytes 15921152 | tf_op jit(solution)/shard_map/reshape.37
  225.3 5.3 %all-to-all-start.4 = ((bf16[32,2,8192]{2,1,0:T(2,128)(2,1)}), bf16[32,2,8192]{2,1,0:T(2,128)(2,1)}, u32[]{:S(2)}, u32[]{:S(2)}) async-start(bf16[32,2,8192]{2,1,0:T(2,128)(2,1)} %reshape.492), calls=%async_computation.4 | async-start | bytes 2097152 | tf_op jit(solution)/shard_map/all_to_all | solution.py:170
  230.7 9.3 %fusion.30 = f32[32,384,1,128]{3,1,0,2:T(8,128)S(1)} fusion(bf16[128,32,128]{2,0,1:T(8,128)(2,1)} %all-to-all-done.3, f32[32,384,128]{2,1,0:T(8,128)} %copy-done.2, f32[32,128]{1,0:T(8,128)S(1)} %copy-done.38, f32[32,128]{1,0:T(8,128)S(1)} %copy-done.36, s32[32,128]{1,0:T(8,128)S(1)} %bitcast.231, s32[32,384]{1,0:T(8,128)S(1)} %copy-done.23, ...), kind=kOutput, calls=%fused_computation.41 | convolution fusion | flops 418381824 | bytes 13807616 | tf_op jit(solution)/shard_map/nkgqw,nqkgd->nwkd/dot_general | solution.py:114
  241.4 2.7 copy-done.8
  251.3 3.3 fusion.36
  254.9 19.1 %copy.108 = f32[2,4096,1,128]{3,2,0,1:T(1,128)} copy(f32[2,4096,1,128]{3,1,2,0:T(8,128)S(1)} %pad_maximum_fusion) | data formatting | bytes 8388608 | tf_op jit(solution)/shard_map/stack | solution.py:167
  274.0 7.8 %all-to-all-start.5 = ((f32[2,4096,1,128]{3,2,0,1:T(1,128)}), f32[2,4096,1,128]{3,2,0,1:T(1,128)}, u32[]{:S(2)}, u32[]{:S(2)}) async-start(f32[2,4096,1,128]{3,2,0,1:T(1,128)} %copy.108), calls=%async_computation.5 | async-start | bytes 8388608 | tf_op jit(solution)/shard_map/all_to_all | solution.py:166
  284.4 5.8 %reshape.493 = bf16[4096,1,128]{2,1,0:T(2,128)(2,1)} reshape(bf16[32,2,8192]{2,1,0:T(2,128)(2,1)} %all-to-all-done.4) | data formatting | bytes 2097152
  290.2 3.8 convert_element_type.169
  295.8 3.3 multiply_reduce_fusion
  299.1 3.0 copy.102
  304.6 2.7 fusion.35
  308.6 66.6 %all-to-all-done.5 = f32[2,4096,1,128]{3,2,0,1:T(1,128)} async-done(((f32[2,4096,1,128]{3,2,0,1:T(1,128)}), f32[2,4096,1,128]{3,2,0,1:T(1,128)}, u32[]{:S(2)}, u32[]{:S(2)}) %all-to-all-start.5) | async-done | bytes 4194336 | tf_op jit(solution)/shard_map/all_to_all | solution.py:166
  375.1 5.0 %reduce.3 = bf16[2,128,8,1,128]{4,0,1,2,3:T(2,128)(2,1)S(1)} reduce(f32[2,128,8,4,1,128]{5,0,1,3,2,4:T(2,128)} %bitcast.63, f32[]{:T(128)} %constant.15.clone.1), dimensions={3}, to_apply=%region_8.9 | reduce | flops 786432 | bytes 4718596
  383.9 39.3 %all-reduce.15 = (f32[128]{0:T(128)S(1)}, f32[128]{0:T(128)S(1)}) all-reduce(f32[128]{0:T(128)S(1)} %copy-done.46, f32[128]{0:T(128)S(1)} %copy-done.47), channel_id=2, replica_groups=mesh['seq'=32,'fsdp'=16] {'fsdp'}, use_global_device_ids=true, to_apply=%region_11.12.clone | all-reduce | flops 256 | bytes 2048
  424.2 75.0 %all-reduce.14 = (f32[8]{0:T(128)}, f32[8]{0:T(128)}) all-reduce(f32[8]{0:T(128)S(1)} %dynamic-slice.3, f32[8]{0:T(128)S(1)} %dynamic-slice.5), channel_id=1, replica_groups=mesh['seq'=32,'fsdp'=16] {'seq'}, use_global_device_ids=true, to_apply=%region_12.13 | all-reduce | flops 16 | bytes 128 | tf_op jit(solution)/shard_map/psum | solution.py:186
  (178 shorter events, 52.1 us)
Async XLA Ops:
  2.8 60.3 %copy-start = (f32[128,32,128]{2,0,1:T(8,128)}, f32[128,32,128]{2,0,1:T(8,128)S(1)}, u32[]{:S(2)}) copy-start(f32[128,32,128]{2,0,1:T(8,128)S(1)} %copy.94) | copy-start | bytes 6291460
  3.1 60.0 %copy-start.24 = (f32[128,32]{0,1:T(8,128)}, f32[128,32]{0,1:T(8,128)S(1)}, u32[]{:S(2)}) copy-start(f32[128,32]{0,1:T(8,128)S(1)} %add_rsqrt_fusion) | copy-start | bytes 49156
  59.3 22.0 %copy-start.40 = (f32[128]{0:T(128)}, f32[128]{0:T(128)S(1)}, u32[]{:S(2)}) copy-start(f32[128]{0:T(128)S(1)} %get-tuple-element.34) | copy-start | bytes 1540
  66.8 39.3 %all-to-all-start.1 = ((bf16[128,32,128]{2,0,1:T(8,128)(2,1)}), bf16[128,32,128]{2,0,1:T(8,128)(2,1)S(1)}, u32[]{:S(2)}, u32[]{:S(2)}) async-start(bf16[128,32,128]{2,0,1:T(8,128)(2,1)} %fusion.39), calls=%async_computation.1 | async-start | bytes 2097152 | tf_op jit(solution)/shard_map/all_to_all | solution.py:153
  80.8 27.7 %copy-start.6 = (f32[128,8,128]{2,0,1:T(8,128)}, f32[128,8,128]{2,0,1:T(8,128)S(1)}, u32[]{:S(2)}) copy-start(f32[128,8,128]{2,0,1:T(8,128)S(1)} %copy.92) | copy-start | bytes 1572868
  108.5 38.5 %copy-start.49 = (s32[1,48]{1,0:T(1,128)S(1)}, s32[1,48]{1,0:T(1,128)}, u32[]{:S(2)}) copy-start(s32[1,48]{1,0:T(1,128)} %param.13) | copy-start | bytes 580
  108.5 32.0 %all-to-all-start = ((bf16[128,32,128]{2,0,1:T(8,128)(2,1)}), bf16[128,32,128]{2,0,1:T(8,128)(2,1)S(1)}, u32[]{:S(2)}, u32[]{:S(2)}) async-start(bf16[128,32,128]{2,0,1:T(8,128)(2,1)} %bitcast.221), calls=%async_computation | async-start | bytes 2097152 | tf_op jit(solution)/shard_map/all_to_all | solution.py:154
  141.7 31.8 %all-to-all-start.2 = ((bf16[128,32,128]{2,0,1:T(8,128)(2,1)}), bf16[128,32,128]{2,0,1:T(8,128)(2,1)S(1)}, u32[]{:S(2)}, u32[]{:S(2)}) async-start(bf16[128,32,128]{2,0,1:T(8,128)(2,1)} %bitcast.220), calls=%async_computation.2 | async-start | bytes 2097152 | tf_op jit(solution)/shard_map/all_to_all | solution.py:155
  173.6 31.9 %all-to-all-start.3 = ((bf16[128,32,128]{2,0,1:T(8,128)(2,1)}), bf16[128,32,128]{2,0,1:T(8,128)(2,1)}, u32[]{:S(2)}, u32[]{:S(2)}) async-start(bf16[128,32,128]{2,0,1:T(8,128)(2,1)} %copy.97), calls=%async_computation.3 | async-start | bytes 2097152 | tf_op jit(solution)/shard_map/all_to_all | solution.py:156
  179.6 13.8 %copy-start.29 = (pred[32,384]{1,0:T(8,128)(4,1)}, pred[32,384]{1,0:T(8,128)(4,1)S(1)}, u32[]{:S(2)}) copy-start(pred[32,384]{1,0:T(8,128)(4,1)S(1)} %broadcast_compare_fusion) | copy-start | bytes 36868
  180.4 13.0 %copy-start.18 = (s32[32,384]{1,0:T(8,128)}, s32[32,384]{1,0:T(8,128)S(1)}, u32[]{:S(2)}) copy-start(s32[32,384]{1,0:T(8,128)S(1)} %pad_add_fusion) | copy-start | bytes 147460
  181.1 12.3 %copy-start.21 = (s32[32,384]{1,0:T(8,128)}, s32[32,384]{1,0:T(8,128)S(1)}, u32[]{:S(2)}) copy-start(s32[32,384]{1,0:T(8,128)S(1)} %fusion.57) | copy-start | bytes 147460
  181.2 12.1 %copy-start.13 = (bf16[31,128,1,128]{3,1,0,2:T(8,128)(2,1)}, bf16[31,128,1,128]{3,1,0,2:T(8,128)(2,1)S(1)}, u32[]{:S(2)}) copy-start(bf16[31,128,1,128]{3,1,0,2:T(8,128)(2,1)S(1)} %slice.126) | copy-start | bytes 3047428
  181.3 12.0 %copy-start.15 = (bf16[30,128,1,128]{3,1,0,2:T(8,128)(2,1)}, bf16[30,128,1,128]{3,1,0,2:T(8,128)(2,1)S(1)}, u32[]{:S(2)}) copy-start(bf16[30,128,1,128]{3,1,0,2:T(8,128)(2,1)S(1)} %slice.125) | copy-start | bytes 2949124
  205.5 8.4 %copy-start.3 = (f32[32,384,128]{2,1,0:T(8,128)S(1)}, f32[32,384,128]{2,1,0:T(8,128)}, u32[]{:S(2)}) copy-start(f32[32,384,128]{2,1,0:T(8,128)} %copy-done.2) | copy-start | bytes 18874372
  205.5 8.4 %copy-start.19 = (s32[32,384]{1,0:T(8,128)S(1)}, s32[32,384]{1,0:T(8,128)}, u32[]{:S(2)}) copy-start(s32[32,384]{1,0:T(8,128)} %copy-done.18) | copy-start | bytes 147460
  205.5 8.4 %copy-start.22 = (s32[32,384]{1,0:T(8,128)S(1)}, s32[32,384]{1,0:T(8,128)}, u32[]{:S(2)}) copy-start(s32[32,384]{1,0:T(8,128)} %copy-done.21) | copy-start | bytes 147460
  205.5 8.4 %copy-start.27 = (s32[32,128]{1,0:T(8,128)S(1)}, s32[32,128]{1,0:T(8,128)}, u32[]{:S(2)}) copy-start(s32[32,128]{1,0:T(8,128)} %get-tuple-element.55) | copy-start | bytes 49156
  205.5 8.4 %copy-start.30 = (pred[32,384]{1,0:T(8,128)(4,1)S(1)}, pred[32,384]{1,0:T(8,128)(4,1)}, u32[]{:S(2)}) copy-start(pred[32,384]{1,0:T(8,128)(4,1)} %copy-done.29) | copy-start | bytes 36868
  205.5 8.4 %copy-start.35 = (f32[32,128]{1,0:T(8,128)S(1)}, f32[32,128]{1,0:T(8,128)}, u32[]{:S(2)}) copy-start(f32[32,128]{1,0:T(8,128)} %copy-done.34) | copy-start | bytes 49156
  205.5 8.4 %copy-start.37 = (f32[32,128]{1,0:T(8,128)S(1)}, f32[32,128]{1,0:T(8,128)}, u32[]{:S(2)}) copy-start(f32[32,128]{1,0:T(8,128)} %fusion.11) | copy-start | bytes 49156
  213.9 6.5 %copy-start.14 = (bf16[31,128,1,128]{3,1,0,2:T(8,128)(2,1)S(1)}, bf16[31,128,1,128]{3,1,0,2:T(8,128)(2,1)}, u32[]{:S(2)}) copy-start(bf16[31,128,1,128]{3,1,0,2:T(8,128)(2,1)} %copy-done.13) | copy-start | bytes 3047428
  213.9 6.5 %copy-start.16 = (bf16[30,128,1,128]{3,1,0,2:T(8,128)(2,1)S(1)}, bf16[30,128,1,128]{3,1,0,2:T(8,128)(2,1)}, u32[]{:S(2)}) copy-start(bf16[30,128,1,128]{3,1,0,2:T(8,128)(2,1)} %copy-done.15) | copy-start | bytes 2949124
  224.1 6.5 %copy-start.20 = (s32[32,384]{1,0:T(8,128)S(1)}, s32[32,384]{1,0:T(8,128)}, u32[]{:S(2)}) copy-start(s32[32,384]{1,0:T(8,128)} %copy-done.18) | copy-start | bytes 147460
  224.2 6.5 %copy-start.23 = (s32[32,384]{1,0:T(8,128)S(1)}, s32[32,384]{1,0:T(8,128)}, u32[]{:S(2)}) copy-start(s32[32,384]{1,0:T(8,128)} %copy-done.21) | copy-start | bytes 147460
  224.2 6.5 %copy-start.28 = (s32[32,128]{1,0:T(8,128)S(1)}, s32[32,128]{1,0:T(8,128)}, u32[]{:S(2)}) copy-start(s32[32,128]{1,0:T(8,128)} %get-tuple-element.55) | copy-start | bytes 49156
  224.2 6.5 %copy-start.31 = (pred[32,384]{1,0:T(8,128)(4,1)S(1)}, pred[32,384]{1,0:T(8,128)(4,1)}, u32[]{:S(2)}) copy-start(pred[32,384]{1,0:T(8,128)(4,1)} %copy-done.29) | copy-start | bytes 36868
  224.2 6.5 %copy-start.36 = (f32[32,128]{1,0:T(8,128)S(1)}, f32[32,128]{1,0:T(8,128)}, u32[]{:S(2)}) copy-start(f32[32,128]{1,0:T(8,128)} %copy-done.34) | copy-start | bytes 49156
  225.3 48.7 %all-to-all-start.4 = ((bf16[32,2,8192]{2,1,0:T(2,128)(2,1)}), bf16[32,2,8192]{2,1,0:T(2,128)(2,1)}, u32[]{:S(2)}, u32[]{:S(2)}) async-start(bf16[32,2,8192]{2,1,0:T(2,128)(2,1)} %reshape.492), calls=%async_computation.4 | async-start | bytes 2097152 | tf_op jit(solution)/shard_map/all_to_all | solution.py:170
  274.0 9.2 %copy-start.41 = (f32[128]{0:T(128)S(1)}, f32[128]{0:T(128)}, u32[]{:S(2)}) copy-start(f32[128]{0:T(128)} %copy-done.40) | copy-start | bytes 1540
  274.0 9.8 %copy-start.44 = (f32[128]{0:T(128)S(1)}, f32[128]{0:T(128)}, u32[]{:S(2)}) copy-start(f32[128]{0:T(128)} %copy-done.43) | copy-start | bytes 1540
  274.0 101.1 %all-to-all-start.5 = ((f32[2,4096,1,128]{3,2,0,1:T(1,128)}), f32[2,4096,1,128]{3,2,0,1:T(1,128)}, u32[]{:S(2)}, u32[]{:S(2)}) async-start(f32[2,4096,1,128]{3,2,0,1:T(1,128)} %copy.108), calls=%async_computation.5 | async-start | bytes 8388608 | tf_op jit(solution)/shard_map/all_to_all | solution.py:166
  (26 other events, 68.5 us)
where the time goes:
time: 501 us; the launch traced here: 499 us
  blocking collectives  168 us (34%)
  waiting for transfers between devices  133 us (27%)
  local copies, waits for them, and re-layouts  67.4 us (13%)
  other arithmetic  55.1 us (11%)
  starting transfers between devices  41.7 us (8%)
  matrix products  30.3 us (6%)
    unnamed x2, blocking collectives  93.4 us
    psum x1, blocking collectives, local(): q_gain_grad, k_gain_grad = lax.psum((gain_shard[0], gain_shard[1]), 'seq')  75 us
    all_to_all x1, waiting for transfers between devices, local(): lax.all_to_all(jnp.stack([dkeys, dvalues]), 'seq', split_axis=1, concat_a...  66.6 us
    all_to_all x1, waiting for transfers between devices, local(): lax.all_to_all(keys_wide, 'seq', split_axis=1, concat_axis=0, tiled=True)  25.5 us
    unnamed x122, local copies, waits for them, and re-layouts  25.1 us
    all_to_all x1, waiting for transfers between devices, local(): lax.all_to_all(query, 'seq', split_axis=1, concat_axis=0, tiled=True)  23.4 us
    another operation x1, local copies, waits for them, and re-layouts, local(): jnp.stack([dkeys, dvalues])  19.1 us
    all_to_all x1, waiting for transfers between devices, local(): lax.all_to_all(values_wide, 'seq', split_axis=1, concat_axis=0, tiled=True)  15.3 us
  transfers between devices with their start and end apart: 6, of which 5 were waited for; matrix products, arithmetic and copies ran while one was open for 20% of the time, Pallas kernels for 0%

commit v1 on v0

v1 whole, which is shorter than its diff:
```python
import jax
import jax.numpy as jnp
from jax import lax
from jax.experimental import pallas as pl
from jax.experimental.pallas import tpu as pltpu
from jax.sharding import PartitionSpec as P

HEADS = 32
KV_HEADS = 8
GROUP = HEADS // KV_HEADS
HEAD_DIM = 128
HALF = HEAD_DIM // 2
ROWS = 128

norm_epsilon = 1e-06
rope_base = 1000000.0
MASKED = -1e30

NT = (((1,), (1,)), ((), ()))
NN = (((1,), (0,)), ((), ()))
TN = (((0,), (0,)), ((), ()))


def dot(a, b, dims):
    return lax.dot_general(a, b, dims, preferred_element_type=jnp.float32)


def roll_half(x):
    return pltpu.roll(x, HALF, axis=1)


def forward_norm(raw, gain, cosine, sine):
    x = raw.astype(jnp.float32)
    inverse = lax.rsqrt(jnp.mean(x * x, axis=-1, keepdims=True) + norm_epsilon)
    y = x * inverse * gain
    return x, inverse, (y * cosine + roll_half(y) * sine).astype(jnp.bfloat16)


def unrotate(grad, cosine, sine):
    return grad * cosine - roll_half(grad) * sine


def fold8(x):
    return jnp.sum(x.reshape(x.shape[0] // 8, 8, x.shape[1]), axis=0)


def stack_heads(x):
    return jnp.concatenate([x[:, h * HEAD_DIM:(h + 1) * HEAD_DIM] for h in range(GROUP)], axis=0)


def table_kernel(len_ref, place_ref, bias_ref, late_ref, take_ref):
    shape = (ROWS, ROWS)
    base = place_ref[0]
    row = lax.broadcasted_iota(jnp.int32, shape, 0)
    lane = lax.broadcasted_iota(jnp.int32, shape, 1)
    here = lax.broadcasted_iota(jnp.int32, (8, ROWS), 1)
    first = jnp.zeros((8, ROWS), jnp.int32) - base
    end = -base
    for k in range(len_ref.shape[0] - 1):
        end = end + len_ref[k]
        first = jnp.where(here >= end, end, first)
    first = jnp.concatenate([first] * (ROWS // 8), axis=0)
    bias_ref[0] = jnp.where(row >= first + ROWS, 0.0, MASKED)
    own = (row <= lane) & (row >= first)
    bias_ref[1] = jnp.where(own | (row >= first + 2 * ROWS), 0.0, MASKED)
    late_ref[...] = jnp.where(first < -ROWS, 1.0, 0.0).T
    head = jnp.broadcast_to(first[:, 0:1], shape)
    take_ref[...] = jnp.where(row >= head + 2 * ROWS, 1.0, 0.0)


def block_tables(lengths, place):
    tile = jax.ShapeDtypeStruct((ROWS, ROWS), jnp.float32)
    smem = pl.BlockSpec(memory_space=pltpu.SMEM)
    return pl.pallas_call(
        table_kernel,
        in_specs=[smem, smem],
        out_shape=[jax.ShapeDtypeStruct((2, ROWS, ROWS), jnp.float32), tile, tile],
        name="tables",
    )(lengths, place)


def attend_kernel(
    q_ref, do_ref, own_k, own_v, one_k, one_v, two_k, two_v,
    cos_ref, sin_ref, bias_ref, late_ref, take_ref, gain_ref,
    dq_ref, ret1_ref, ret2_ref, keep_ref, gains_ref, total_ref,
):
    scale = HEAD_DIM ** (-0.5)
    step = pl.program_id(0)
    gain = jnp.sum(gain_ref[...], axis=0)
    qg, kg = gain[0:1], gain[1:2]
    cos0, sin0 = cos_ref[0], sin_ref[0]
    cos4 = jnp.concatenate([cos0] * GROUP, axis=0)
    sin4 = jnp.concatenate([sin0] * GROUP, axis=0)
    late = late_ref[...] > 0.0
    take = take_ref[...] > 0.0
    late4 = jnp.concatenate([late] * GROUP, axis=0)
    cos2 = jnp.where(take, cos_ref[2], cos0)
    sin2 = jnp.where(take, sin_ref[2], sin0)

    x, inv_q, q = forward_norm(stack_heads(q_ref[...]), qg, cos4, sin4)
    do = stack_heads(do_ref[...])
    zero = jnp.zeros_like(q)
    q_wide = jnp.concatenate([jnp.where(late4, zero, q), jnp.where(late4, q, zero)], axis=1)
    do_wide = jnp.concatenate([jnp.where(late4, zero, do), jnp.where(late4, do, zero)], axis=1)

    v0, v1 = own_v[...], one_v[...]
    xk0, inv0, k0 = forward_norm(own_k[...], kg, cos0, sin0)
    xk1, inv1, k1 = forward_norm(one_k[...], kg, cos_ref[1], sin_ref[1])
    xk2, inv2, k2 = forward_norm(jnp.where(take, two_k[...], own_k[...]), kg, cos2, sin2)
    k_wide = jnp.concatenate([k0, k2], axis=1)
    v_wide = jnp.concatenate([v0, jnp.where(take, two_v[...], v0)], axis=1)

    bias_a = jnp.concatenate([bias_ref[0]] * GROUP, axis=1)
    bias_b = jnp.concatenate([bias_ref[1]] * GROUP, axis=1)
    s_a = dot(k1, q, NT) * scale + bias_a
    s_b = dot(k_wide, q_wide, NT) * scale + bias_b
    top = jnp.maximum(jnp.max(s_a, axis=0, keepdims=True), jnp.max(s_b, axis=0, keepdims=True))
    w_a, w_b = jnp.exp(s_a - top), jnp.exp(s_b - top)
    inv_sum = 1.0 / (jnp.sum(w_a, axis=0, keepdims=True) + jnp.sum(w_b, axis=0, keepdims=True))
    p_a, p_b = w_a * inv_sum, w_b * inv_sum
    dp_a = dot(v1, do, NT)
    dp_b = dot(v_wide, do_wide, NT)
    delta = jnp.sum(p_a * dp_a, axis=0, keepdims=True) + jnp.sum(p_b * dp_b, axis=0, keepdims=True)
    ds_a = (p_a * (dp_a - delta) * scale).astype(jnp.bfloat16)
    ds_b = (p_b * (dp_b - delta) * scale).astype(jnp.bfloat16)

    dv1 = dot(p_a.astype(jnp.bfloat16), do, NN)
    dv_wide = dot(p_b.astype(jnp.bfloat16), do_wide, NN)
    dk1 = dot(ds_a, q, NN)
    dk_wide = dot(ds_b, q_wide, NN)
    dk0, dk2 = dk_wide[:, :HEAD_DIM], dk_wide[:, HEAD_DIM:]
    dv0, dv2 = dv_wide[:, :HEAD_DIM], dv_wide[:, HEAD_DIM:]

    dq_wide = dot(ds_b, k_wide, TN)
    dq = dot(ds_a, k1, TN) + jnp.where(late4, dq_wide[:, HEAD_DIM:], dq_wide[:, :HEAD_DIM])
    dq = dq.astype(jnp.bfloat16).astype(jnp.float32)
    dy = unrotate(dq, cos4, sin4)
    e = dy * qg
    mean = jnp.mean(e * x, axis=-1, keepdims=True)
    dx = (inv_q * (e - x * (inv_q * inv_q * mean))).astype(jnp.bfloat16)
    for h in range(GROUP):
        dq_ref[:, h * HEAD_DIM:(h + 1) * HEAD_DIM] = dx[h * ROWS:(h + 1) * ROWS]

    gk = unrotate(dk0, cos0, sin0) * (xk0 * inv0)
    gk = gk + unrotate(dk1, cos_ref[1], sin_ref[1]) * (xk1 * inv1)
    gk = gk + unrotate(dk2, cos2, sin2) * (xk2 * inv2)
    parts = (fold8(dy * (x * inv_q)), fold8(gk))

    @pl.when(step == 0)
    def _():
        total_ref[0], total_ref[1] = parts

    @pl.when(step > 0)
    def _():
        total_ref[0] += parts[0]
        total_ref[1] += parts[1]

    @pl.when(step == pl.num_programs(0) - 1)
    def _():
        gains_ref[...] = jnp.broadcast_to(jnp.sum(total_ref[...], axis=1)[None], gains_ref.shape)

    ret1_ref[:, :HEAD_DIM] = dk1.astype(jnp.bfloat16)
    ret1_ref[:, HEAD_DIM:] = dv1.astype(jnp.bfloat16)
    ret2_ref[:, :HEAD_DIM] = jnp.where(take, dk2, 0.0).astype(jnp.bfloat16)
    ret2_ref[:, HEAD_DIM:] = jnp.where(take, dv2, 0.0).astype(jnp.bfloat16)
    keep_ref[:, :HEAD_DIM] = dk0 + jnp.where(take, 0.0, dk2)
    keep_ref[:, HEAD_DIM:] = dv0 + jnp.where(take, 0.0, dv2)


def blocks(width, index):
    return pl.BlockSpec((ROWS, width), lambda g: (0, index(g)))


def fixed(a):
    return pl.BlockSpec(a.shape, lambda g: (0,) * a.ndim)


def attend(q, do, own, one, two, tables, peers):
    wide, pair = GROUP * HEAD_DIM, 2 * HEAD_DIM
    here = lambda g: g
    beside = lambda g: g + KV_HEADS
    kv = [blocks(HEAD_DIM, here), blocks(HEAD_DIM, beside)]
    return pl.pallas_call(
        attend_kernel,
        grid=(KV_HEADS,),
        in_specs=[blocks(wide, here), blocks(wide, here)] + kv * 3 + [fixed(t) for t in tables],
        out_specs=[
            blocks(wide, here), blocks(pair, here), blocks(pair, here), blocks(pair, here),
            pl.BlockSpec((peers, 2, HEAD_DIM), lambda g: (0, 0, 0)),
        ],
        out_shape=[
            jax.ShapeDtypeStruct((ROWS, KV_HEADS * wide), jnp.bfloat16),
            jax.ShapeDtypeStruct((ROWS, KV_HEADS * pair), jnp.bfloat16),
            jax.ShapeDtypeStruct((ROWS, KV_HEADS * pair), jnp.bfloat16),
            jax.ShapeDtypeStruct((ROWS, KV_HEADS * pair), jnp.float32),
            jax.ShapeDtypeStruct((peers, 2, HEAD_DIM), jnp.float32),
        ],
        scratch_shapes=[pltpu.VMEM((2, 8, HEAD_DIM), jnp.float32)],
        compiler_params=pltpu.CompilerParams(vmem_limit_bytes=40 * 1024 * 1024),
        name="attend",
    )(q, do, own, own, one, one, two, two, *tables)


def finish_kernel(k_ref, keep_ref, one_ref, two_ref, cos_ref, sin_ref, gain_ref, dk_ref, dv_ref):
    gain = jnp.sum(gain_ref[...], axis=0)[1:2]
    total = keep_ref[...] + one_ref[...].astype(jnp.float32) + two_ref[...].astype(jnp.float32)
    for h in range(k_ref.shape[1] // HEAD_DIM):
        at = slice(h * HEAD_DIM, (h + 1) * HEAD_DIM)
        x = k_ref[:, at].astype(jnp.float32)
        inverse = lax.rsqrt(jnp.mean(x * x, axis=-1, keepdims=True) + norm_epsilon)
        dk = total[:, 2 * h * HEAD_DIM:(2 * h + 1) * HEAD_DIM].astype(jnp.bfloat16).astype(jnp.float32)
        e = unrotate(dk, cos_ref[0], sin_ref[0]) * gain
        mean = jnp.mean(e * x, axis=-1, keepdims=True)
        dk_ref[:, at] = (inverse * (e - x * (inverse * inverse * mean))).astype(jnp.bfloat16)
        dv_ref[:, at] = total[:, (2 * h + 1) * HEAD_DIM:(2 * h + 2) * HEAD_DIM].astype(jnp.bfloat16)


def finish(k, keep, one, two, cosine, sine, gain):
    steps = max(KV_HEADS // 2, 1)
    width = KV_HEADS * HEAD_DIM // steps
    here = lambda g: g
    out = jax.ShapeDtypeStruct((ROWS, KV_HEADS * HEAD_DIM), jnp.bfloat16)
    return pl.pallas_call(
        finish_kernel,
        grid=(steps,),
        in_specs=[blocks(width, here)] + [blocks(2 * width, here)] * 3 + [fixed(t) for t in (cosine, sine, gain)],
        out_specs=[blocks(width, here)] * 2,
        out_shape=[out, out],
        compiler_params=pltpu.CompilerParams(vmem_limit_bytes=40 * 1024 * 1024),
        name="finish",
    )(k, keep, one, two, cosine, sine, gain)


def rotary_tables(base):
    positions = base + jnp.arange(ROWS, dtype=jnp.int32)
    positions = positions[None, :] - ROWS * jnp.arange(3, dtype=jnp.int32)[:, None]
    freqs = rope_base ** (-(jnp.arange(HALF, dtype=jnp.float32) * 2.0 / HEAD_DIM))
    angles = positions.astype(jnp.float32)[:, :, None] * freqs
    cosine, sine = jnp.cos(angles), jnp.sin(angles)
    return jnp.concatenate([cosine, cosine], axis=2), jnp.concatenate([-sine, sine], axis=2)


AXES = ("seq", "fsdp")


def device_at(y, z, x, core):
    return ((y % 4 * 4 + x) * 2 + core) * 16 + y // 4 * 8 + z


def gain_groups():
    return [
        [device_at(a, z, x, c) for z in range(8)] + [device_at(4 + (a + 2) % 4, z, x, c) for z in range(8)]
        for a in range(4) for x in range(4) for c in range(2)
    ]


def plane_groups():
    return [[device_at(y, z, x, c) for z in range(8) for x in range(4) for c in range(2)] for y in range(8)]


def column_groups():
    return [[device_at(y, z, x, c) for y in range(8)] for z in range(8) for x in range(4) for c in range(2)]


def swap(rows, groups):
    return lax.all_to_all(rows, AXES, 0, 0, axis_index_groups=groups, tiled=True)


def local(query_raw, key_raw, value_proj, out_grad, query_gain, key_gain, turn_lengths):
    me, shard = lax.axis_index("seq"), lax.axis_index("fsdp")
    seq, shards = lax.axis_size("seq"), lax.axis_size("fsdp")
    base = me * ROWS

    own = jnp.concatenate([key_raw[0], value_proj[0]], axis=1)
    two = lax.ppermute(own, "seq", [(i, i + 2) for i in range(seq - 2)])
    one = lax.ppermute(own, "seq", [(i, i + 1) for i in range(seq - 1)])

    gain = jnp.tile(jnp.stack([query_gain, key_gain]), (1, shards))
    mine = jnp.arange(HEAD_DIM, dtype=jnp.int32) // query_gain.shape[0] == shard
    gain = jnp.where(mine, gain, 0.0)
    gain = swap(jnp.broadcast_to(gain[None], (shards, 2, HEAD_DIM)), gain_groups())

    cosine, sine = rotary_tables(base)
    bias, late, take = block_tables(turn_lengths[0], base[None])
    tables = (cosine, sine, bias, late, take, gain)
    q_grad, ret1, ret2, keep, parts = attend(query_raw[0], out_grad[0], own, one, two, tables, 64)

    back2 = lax.ppermute(ret2, "seq", [(i + 2, i) for i in range(seq - 2)])
    back1 = lax.ppermute(ret1, "seq", [(i + 1, i) for i in range(seq - 1)])

    part = jnp.sum(swap(parts, plane_groups()), axis=0)
    total = jnp.sum(swap(jnp.broadcast_to(part[None], (8, 2, HEAD_DIM)), column_groups()), axis=0)
    shard_rows = total.reshape(2, shards, HEAD_DIM // shards)
    gain_grad = lax.dynamic_slice_in_dim(shard_rows, shard, 1, axis=1)

    k_grad, v_grad = finish(key_raw[0], keep, back1, back2, cosine, sine, gain)
    return q_grad[None], k_grad[None], v_grad[None], gain_grad[0, 0], gain_grad[1, 0]


def solution(mesh):
    return jax.shard_map(
        local,
        mesh=mesh,
        in_specs=(
            P("fsdp", "seq", None),
            P("fsdp", "seq", None),
            P("fsdp", "seq", None),
            P("fsdp", "seq", None),
            P("fsdp"),
            P("fsdp"),
            P("fsdp", None),
        ),
        out_specs=(
            P("fsdp", "seq", None),
            P("fsdp", "seq", None),
            P("fsdp", "seq", None),
            P("fsdp"),
            P("fsdp"),
        ),
        check_vma=False,
    )
```

time: 501 us -> 94.4 us (0.19)
  blocking collectives: 168 us -> 19.3 us
  waiting for transfers between devices: 133 us -> 13.7 us
  local copies, waits for them, and re-layouts: 67.4 us -> 7.61 us
  other arithmetic: 55.1 us -> 2.21 us
  matrix products: 30.3 us -> 0 us
  Pallas kernels: 0 us -> 19.6 us
  starting transfers between devices: 41.7 us -> 30.6 us
    all_to_all x6 -> x2, waiting for transfers between devices: 133 us -> 13.7 us  [swap(): lax.all_to_all(rows, AXES, 0, 0, axis_index_groups=groups, tiled=True)]
    unnamed x2 -> x0, blocking collectives: 93.4 us -> none
    psum x1 -> x0, blocking collectives: 75 us -> none  [local(): q_gain_grad, k_gain_grad = lax.psum((gain_shard[0], gain_shard[1]), 'seq')]
    dot_general x5 -> x0, matrix products: 30.3 us -> none  [the longest x1 9.85 us: attend(): jnp.einsum('nqkgd,nwkd->nkgqw', query_blocks, key_window, preferred_eleme...]
    another operation x5 -> x2, local copies, waits for them, and re-layouts: 22.7 us -> 0.09 us  [local(): gain = jnp.tile(jnp.stack([query_gain, key_gain]), (1, shards))]
    all_to_all x6 -> x2, starting transfers between devices: 41.7 us -> 19.3 us  [swap(): lax.all_to_all(rows, AXES, 0, 0, axis_index_groups=groups, tiled=True)]
    pallas_call x0 -> x3, Pallas kernels: none -> 19.6 us  [the longest x1 16 us: attend(): pl.pallas_call(attend_kernel, grid=(KV_HEADS,), in_specs=[blocks(wide, he...]
    unnamed x122 -> x16, local copies, waits for them, and re-layouts: 25.1 us -> 5.69 us
  transfers between devices with their start and end apart: 6 -> 6, of which waited for: 5 -> 2; matrix products, arithmetic and copies ran while one was open for 20% -> 3% of each run, Pallas kernels for 0% -> 2%
where the time goes in v1:
time: 94.4 us; the launch traced here: 93.8 us
  starting transfers between devices  30.6 us (32%)
  Pallas kernels  19.6 us (21%)
  blocking collectives  19.3 us (20%)
  waiting for transfers between devices  13.7 us (15%)
  local copies, waits for them, and re-layouts  7.61 us (8%)
  other arithmetic  2.21 us (2%)
    all_to_all x1, blocking collectives, swap(): lax.all_to_all(rows, AXES, 0, 0, axis_index_groups=groups, tiled=True)  19.3 us
    all_to_all x2, starting transfers between devices, swap(): lax.all_to_all(rows, AXES, 0, 0, axis_index_groups=groups, tiled=True)  19.3 us
    pallas_call x1, Pallas kernels, attend(): pl.pallas_call(attend_kernel, grid=(KV_HEADS,), in_specs=[blocks(wide, he...  16 us
    all_to_all x2, waiting for transfers between devices, swap(): lax.all_to_all(rows, AXES, 0, 0, axis_index_groups=groups, tiled=True)  13.7 us
    unnamed x16, local copies, waits for them, and re-layouts  5.69 us
    ppermute x1, starting transfers between devices, local(): one = lax.ppermute(own, 'seq', [(i, i + 1) for i in range(seq - 1)])  4.51 us
    ppermute x1, starting transfers between devices, local(): two = lax.ppermute(own, 'seq', [(i, i + 2) for i in range(seq - 2)])  3.15 us
    ppermute x1, starting transfers between devices, local(): back1 = lax.ppermute(ret1, 'seq', [(i + 1, i) for i in range(seq - 1)])  2.42 us
  transfers between devices with their start and end apart: 6, of which 2 were waited for; matrix products, arithmetic and copies ran while one was open for 3% of the time, Pallas kernels for 2%

profile of v1, /device:TPU:1, one launch (start us, length us, event | category | flops | bytes accessed | tf_op | source)
XLA Modules:
  0.0 93.8 jit_solution(17673281027968002926)
XLA Ops:
  0.6 1.1 %pad_maximum_fusion.own_k.own_v = bf16[128,2048]{1,0:T(8,128)(2,1)S(1)} fusion(bf16[128,1024]{1,0:T(8,128)(2,1)} %bitcast.19, bf16[128,1024]{1,0:T(8,128)(2,1)} %bitcast.17), kind=kLoop, calls=%fused_computation | loop fusion | flops 1048576 | bytes 1048576 | tf_op jit(solution)/shard_map/concatenate | solution.py:274
  1.7 4.5 %collective-permute-start = (bf16[128,2048]{1,0:T(8,128)(2,1)S(1)}, bf16[128,2048]{1,0:T(8,128)(2,1)S(1)}, u32[]{:S(2)}, u32[]{:S(2)}) collective-permute-start(bf16[128,2048]{1,0:T(8,128)(2,1)S(1)} %pad_maximum_fusion.own_k.own_v), channel_id=1, source_target_pairs={{0,16},{16,32},{32,48},{48,64},{64,80},{80,96},{96,112},{112,128},... | collective-permute-start | bytes 1572872 | tf_op jit(solution)/shard_map/ppermute | solution.py:276
  6.2 3.1 %collective-permute-start.1 = (bf16[128,2048]{1,0:T(8,128)(2,1)S(1)}, bf16[128,2048]{1,0:T(8,128)(2,1)S(1)}, u32[]{:S(2)}, u32[]{:S(2)}) collective-permute-start(bf16[128,2048]{1,0:T(8,128)(2,1)S(1)} %pad_maximum_fusion.own_k.own_v), channel_id=1, source_target_pairs={{0,32},{16,48},{32,64},{48,80},{64,96},{80,112},{96,128},{112,144}... | collective-permute-start | bytes 1572872 | tf_op jit(solution)/shard_map/ppermute | solution.py:275
  9.4 0.0 copy-start.6
  9.4 0.0 copy-start.7
  9.4 0.6 copy-done.6
  10.0 0.0 copy-done.7
  10.1 0.1 tile.10
  10.2 0.6 broadcast_in_dim.39
  10.8 13.8 %all-to-all-start = ((f32[16,2,128]{2,1,0:T(2,128)}), f32[16,2,128]{2,1,0:T(2,128)S(1)}, u32[]{:S(2)}, u32[]{:S(2)}) async-start(f32[16,2,128]{2,1,0:T(2,128)} %broadcast_in_dim.39), calls=%async_computation | async-start | bytes 32768 | tf_op jit(solution)/shard_map/all_to_all | solution.py:266
  24.6 0.1 subtract_convert_fusion
  24.7 0.8 fusion
  25.5 0.2 pad_maximum_fusion.1
  25.7 1.5 %tables.1 = (f32[2,128,128]{2,1,0:T(8,128)}, f32[128,128]{1,0:T(8,128)}, f32[128,128]{1,0:T(8,128)}) custom-call(s32[48]{0:T(128)} %bitcast.25, s32[1]{0:T(128)} %bitcast.5.place_ref), custom_call_target="tpu_custom_call" | custom-call | tf_op jit(solution)/shard_map/tables/pallas_call | solution.py:74
  27.1 7.1 %all-to-all-done.gain_ref = f32[16,2,128]{2,1,0:T(2,128)S(1)} async-done(((f32[16,2,128]{2,1,0:T(2,128)}), f32[16,2,128]{2,1,0:T(2,128)S(1)}, u32[]{:S(2)}, u32[]{:S(2)}) %all-to-all-start) | async-done | bytes 16416 | tf_op jit(solution)/shard_map/all_to_all | solution.py:266
  34.3 0.0 collective-permute-done.1.two_k.two_v
  34.3 1.2 %copy-done = bf16[1,128,4096]{2,1,0:T(8,128)(2,1)S(1)} copy-done((bf16[1,128,4096]{2,1,0:T(8,128)(2,1)S(1)}, bf16[1,128,4096]{2,1,0:T(8,128)(2,1)}, u32[]{:S(2)}) %copy-start) | copy-done | bytes 1048600
  35.5 1.2 %copy-done.1 = bf16[1,128,4096]{2,1,0:T(8,128)(2,1)S(1)} copy-done((bf16[1,128,4096]{2,1,0:T(8,128)(2,1)S(1)}, bf16[1,128,4096]{2,1,0:T(8,128)(2,1)}, u32[]{:S(2)}) %copy-start.1) | copy-done | bytes 1048600
  36.7 0.9 copy-done.3
  37.6 0.8 copy-done.4
  38.5 0.8 copy-done.5
  39.3 16.0 %attend.1 = (bf16[128,4096]{1,0:T(8,128)(2,1)}, bf16[128,2048]{1,0:T(8,128)(2,1)}, bf16[128,2048]{1,0:T(8,128)(2,1)S(1)}, f32[128,2048]{1,0:T(8,128)S(1)}, f32[64,2,128]{2,1,0:T(2,128)S(1)}) custom-call(bf16[128,4096]{1,0:T(8,128)(2,1)S(1)} %bitcast.15, bf16[128,4096]{1,0:T(8,128)(2,1)S(1)} %bitcast.16, bf16[128,2048]{1,0:T(8,128)(2,1)S(1)} %pad_maximum_fusion.own_k.own_v, ...), custom_call_target="tpu_custom_call" | custom-call | tf_op jit(solution)/shard_map/attend/pallas_call | solution.py:183
  55.3 2.4 %collective-permute-start.2 = (bf16[128,2048]{1,0:T(8,128)(2,1)}, bf16[128,2048]{1,0:T(8,128)(2,1)S(1)}, u32[]{:S(2)}, u32[]{:S(2)}) collective-permute-start(bf16[128,2048]{1,0:T(8,128)(2,1)} %get-tuple-element.20), channel_id=1, source_target_pairs={{16,0},{32,16},{48,32},{64,48},{80,64},{96,80},{112,96},{128,112},... | collective-permute-start | bytes 1572872 | tf_op jit(solution)/shard_map/ppermute | solution.py:289
  57.7 1.3 %collective-permute-start.3 = (bf16[128,2048]{1,0:T(8,128)(2,1)S(1)}, bf16[128,2048]{1,0:T(8,128)(2,1)S(1)}, u32[]{:S(2)}, u32[]{:S(2)}) collective-permute-start(bf16[128,2048]{1,0:T(8,128)(2,1)S(1)} %get-tuple-element.21), channel_id=1, source_target_pairs={{32,0},{48,16},{64,32},{80,48},{96,64},{112,80},{128,96},{144,112}... | collective-permute-start | bytes 1572872 | tf_op jit(solution)/shard_map/ppermute | solution.py:288
  59.0 19.3 %all_to_all.15 = f32[64,2,128]{2,1,0:T(2,128)S(1)} all-to-all(f32[64,2,128]{2,1,0:T(2,128)S(1)} %get-tuple-element.24), channel_id=1, replica_groups={{0,16,32,48,64,80,96,112,1,17,33,49,65,81,97,113,2,18,34,50,66,82,98,11..., dimensions={0} | all-to-all | bytes 131072 | tf_op jit(solution)/shard_map/all_to_all | solution.py:266
  78.3 0.1 reduce_sum.18
  78.4 0.6 broadcast_in_dim.43
  79.0 5.5 %all-to-all-start.2 = ((f32[8,2,128]{2,1,0:T(2,128)}), f32[8,2,128]{2,1,0:T(2,128)S(1)}, u32[]{:S(2)}, u32[]{:S(2)}) async-start(f32[8,2,128]{2,1,0:T(2,128)} %broadcast_in_dim.43), calls=%async_computation.2 | async-start | bytes 16384 | tf_op jit(solution)/shard_map/all_to_all | solution.py:266
  84.5 6.6 %all-to-all-done.2 = f32[8,2,128]{2,1,0:T(2,128)S(1)} async-done(((f32[8,2,128]{2,1,0:T(2,128)}), f32[8,2,128]{2,1,0:T(2,128)S(1)}, u32[]{:S(2)}, u32[]{:S(2)}) %all-to-all-start.2) | async-done | bytes 8224 | tf_op jit(solution)/shard_map/all_to_all | solution.py:266
  91.1 0.1 reshape.81
  91.2 0.5 dynamic-slice_bitcast_fusion
  91.7 2.1 %finish.1 = (bf16[128,1024]{1,0:T(8,128)(2,1)}, bf16[128,1024]{1,0:T(8,128)(2,1)}) custom-call(bf16[128,1024]{1,0:T(8,128)(2,1)S(1)} %bitcast.18, f32[128,2048]{1,0:T(8,128)S(1)} %get-tuple-element.19.keep_ref, bf16[128,2048]{1,0:T(8,128)(2,1)S(1)} %collective-permute-done.2.one_ref, bf16[128,2048]{1,0:T(8,128)(2,1)S(1)} %collective-permute-done.3.two_ref, ...), custom_call_target="tpu_custom_call" | custom-call | tf_op jit(solution)/shard_map/finish/pallas_call | solution.py:223
  (18 shorter events, 0.1 us)
Async XLA Ops:
  1.7 32.6 %collective-permute-start = (bf16[128,2048]{1,0:T(8,128)(2,1)S(1)}, bf16[128,2048]{1,0:T(8,128)(2,1)S(1)}, u32[]{:S(2)}, u32[]{:S(2)}) collective-permute-start(bf16[128,2048]{1,0:T(8,128)(2,1)S(1)} %pad_maximum_fusion.own_k.own_v), channel_id=1, source_target_pairs={{0,16},{16,32},{32,48},{48,64},{64,80},{80,96},{96,112},{112,128},... | collective-permute-start | bytes 1572872 | tf_op jit(solution)/shard_map/ppermute | solution.py:276
  6.2 28.1 %collective-permute-start.1 = (bf16[128,2048]{1,0:T(8,128)(2,1)S(1)}, bf16[128,2048]{1,0:T(8,128)(2,1)S(1)}, u32[]{:S(2)}, u32[]{:S(2)}) collective-permute-start(bf16[128,2048]{1,0:T(8,128)(2,1)S(1)} %pad_maximum_fusion.own_k.own_v), channel_id=1, source_target_pairs={{0,32},{16,48},{32,64},{48,80},{64,96},{80,112},{96,128},{112,144}... | collective-permute-start | bytes 1572872 | tf_op jit(solution)/shard_map/ppermute | solution.py:275
  9.4 0.7 copy-start.6
  9.4 0.7 copy-start.7
  10.8 23.5 %all-to-all-start = ((f32[16,2,128]{2,1,0:T(2,128)}), f32[16,2,128]{2,1,0:T(2,128)S(1)}, u32[]{:S(2)}, u32[]{:S(2)}) async-start(f32[16,2,128]{2,1,0:T(2,128)} %broadcast_in_dim.39), calls=%async_computation | async-start | bytes 32768 | tf_op jit(solution)/shard_map/all_to_all | solution.py:266
  34.3 1.2 %copy-start = (bf16[1,128,4096]{2,1,0:T(8,128)(2,1)S(1)}, bf16[1,128,4096]{2,1,0:T(8,128)(2,1)}, u32[]{:S(2)}) copy-start(bf16[1,128,4096]{2,1,0:T(8,128)(2,1)} %param.7) | copy-start | bytes 3145732
  35.5 1.2 %copy-start.1 = (bf16[1,128,4096]{2,1,0:T(8,128)(2,1)S(1)}, bf16[1,128,4096]{2,1,0:T(8,128)(2,1)}, u32[]{:S(2)}) copy-start(bf16[1,128,4096]{2,1,0:T(8,128)(2,1)} %param.10) | copy-start | bytes 3145732
  36.7 0.9 copy-start.3
  37.6 0.8 copy-start.4
  38.5 0.8 copy-start.5
  55.3 36.4 %copy-start.2 = (bf16[1,128,1024]{2,1,0:T(8,128)(2,1)S(1)}, bf16[1,128,1024]{2,1,0:T(8,128)(2,1)}, u32[]{:S(2)}) copy-start(bf16[1,128,1024]{2,1,0:T(8,128)(2,1)} %param.8) | copy-start | bytes 786436
  55.3 36.4 %collective-permute-start.2 = (bf16[128,2048]{1,0:T(8,128)(2,1)}, bf16[128,2048]{1,0:T(8,128)(2,1)S(1)}, u32[]{:S(2)}, u32[]{:S(2)}) collective-permute-start(bf16[128,2048]{1,0:T(8,128)(2,1)} %get-tuple-element.20), channel_id=1, source_target_pairs={{16,0},{32,16},{48,32},{64,48},{80,64},{96,80},{112,96},{128,112},... | collective-permute-start | bytes 1572872 | tf_op jit(solution)/shard_map/ppermute | solution.py:289
  57.7 34.0 %collective-permute-start.3 = (bf16[128,2048]{1,0:T(8,128)(2,1)S(1)}, bf16[128,2048]{1,0:T(8,128)(2,1)S(1)}, u32[]{:S(2)}, u32[]{:S(2)}) collective-permute-start(bf16[128,2048]{1,0:T(8,128)(2,1)S(1)} %get-tuple-element.21), channel_id=1, source_target_pairs={{32,0},{48,16},{64,32},{80,48},{96,64},{112,80},{128,96},{144,112}... | collective-permute-start | bytes 1572872 | tf_op jit(solution)/shard_map/ppermute | solution.py:288
  79.0 12.0 %all-to-all-start.2 = ((f32[8,2,128]{2,1,0:T(2,128)}), f32[8,2,128]{2,1,0:T(2,128)S(1)}, u32[]{:S(2)}, u32[]{:S(2)}) async-start(f32[8,2,128]{2,1,0:T(2,128)} %broadcast_in_dim.43), calls=%async_computation.2 | async-start | bytes 16384 | tf_op jit(solution)/shard_map/all_to_all | solution.py:266

commit v2 on v1

v2 whole, which is shorter than its diff:
```python
import jax
import jax.numpy as jnp
import numpy as np
from jax import lax
from jax.experimental import pallas as pl
from jax.experimental.pallas import tpu as pltpu
from jax.sharding import PartitionSpec as P

HEADS = 32
KV_HEADS = 8
GROUP = HEADS // KV_HEADS
HEAD_DIM = 128
HALF = HEAD_DIM // 2
ROWS = 128

norm_epsilon = 1e-06
rope_base = 1000000.0
MASKED = -1e30
LOG2E = 1.4426950408889634
STEP_HEADS = 4
VMEM = 24 * 1024 * 1024

NT = (((1,), (1,)), ((), ()))
NN = (((1,), (0,)), ((), ()))
TN = (((0,), (0,)), ((), ()))


def dot(a, b, dims):
    return lax.dot_general(a, b, dims, preferred_element_type=jnp.float32)


def roll_half(x):
    return pltpu.roll(x, HALF, axis=1)


def forward_norm(raw, gain, cosine, sine):
    x = raw.astype(jnp.float32)
    inverse = lax.rsqrt(jnp.mean(x * x, axis=-1, keepdims=True) + norm_epsilon)
    y = x * inverse * gain
    return x, inverse, (y * cosine + roll_half(y) * sine).astype(jnp.bfloat16)


def unrotate(grad, cosine, sine):
    return grad * cosine - roll_half(grad) * sine


def swap_halves(x):
    return jnp.concatenate([x[HALF:], x[:HALF]], axis=0)


def beside_heads(x):
    return jnp.concatenate([x[h * HEAD_DIM:(h + 1) * HEAD_DIM] for h in range(GROUP)], axis=1)


def over_heads(x):
    return jnp.concatenate([x[:, h * ROWS:(h + 1) * ROWS] for h in range(GROUP)], axis=0)


def fold8(x):
    return jnp.sum(x.reshape(x.shape[0] // 8, 8, x.shape[1]), axis=0)


def stack_heads(x):
    return jnp.concatenate([x[:, h * HEAD_DIM:(h + 1) * HEAD_DIM] for h in range(GROUP)], axis=0)


def table_kernel(len_ref, place_ref, freq_ref, table_ref, late_ref):
    shape = (ROWS, ROWS)
    base = place_ref[0]
    row = lax.broadcasted_iota(jnp.int32, shape, 0)
    lane = lax.broadcasted_iota(jnp.int32, shape, 1)
    for back in range(3):
        angles = (base - back * ROWS + row).astype(jnp.float32) * freq_ref[...]
        cosine, sine = jnp.cos(angles), jnp.sin(angles)
        sine = jnp.where(lane < HALF, -sine, sine)
        table_ref[back], table_ref[3 + back] = cosine, sine
        if back == 0:
            table_ref[6], table_ref[7] = cosine.T, sine.T

    here = lax.broadcasted_iota(jnp.int32, (8, ROWS), 1)
    first = jnp.zeros((8, ROWS), jnp.int32) - base
    end = -base
    for k in range(len_ref.shape[0] - 1):
        end = end + len_ref[k]
        first = jnp.where(here >= end, end, first)
    first = jnp.concatenate([first] * (ROWS // 8), axis=0)
    table_ref[8] = jnp.where(row >= first + ROWS, 0.0, MASKED)
    own = (row <= lane) & (row >= first)
    table_ref[9] = jnp.where(own | (row >= first + 2 * ROWS), 0.0, MASKED)
    head = jnp.broadcast_to(first[:, 0:1], shape)
    table_ref[10] = jnp.where(row >= head + 2 * ROWS, 1.0, 0.0)
    late = jnp.where(first < -ROWS, 1.0, 0.0)
    late_ref[0] = late.T.astype(jnp.bfloat16)
    late_ref[1] = (1.0 - late).T.astype(jnp.bfloat16)
    late_ref[2] = late.astype(jnp.bfloat16)
    late_ref[3] = (1.0 - late).astype(jnp.bfloat16)


SMEM_IN = pl.BlockSpec(memory_space=pltpu.SMEM)
VMEM_IN = pl.BlockSpec(memory_space=pltpu.VMEM)
HBM_IN = pl.BlockSpec(memory_space=pltpu.HBM)


def in_hbm(*arrays):
    return [pltpu.with_memory_space_constraint(a, pltpu.HBM) for a in arrays]


def block_tables(lengths, place):
    half = rope_base ** (-np.arange(HALF) * 2.0 / HEAD_DIM)
    freqs = jnp.asarray(np.concatenate([half, half])[None], jnp.float32)
    return pl.pallas_call(
        table_kernel,
        in_specs=[SMEM_IN, SMEM_IN, VMEM_IN],
        out_specs=[VMEM_IN] * 2,
        out_shape=[
            pltpu.VMEM((11, ROWS, ROWS), jnp.float32),
            pltpu.VMEM((4, ROWS, ROWS), jnp.bfloat16),
        ],
        compiler_params=pltpu.CompilerParams(vmem_limit_bytes=VMEM),
        name="tables",
    )(lengths, place, freqs)


def pack_kernel(k_ref, v_ref, qg_in, kg_in, shard_ref, own_ref, gain_ref, qg_ref, kg_ref, sems):
    copies = [
        pltpu.make_async_copy(
            ref.at[:, pl.ds(h * HEAD_DIM, HEAD_DIM)],
            own_ref.at[:, pl.ds((2 * h + n) * HEAD_DIM, HEAD_DIM)],
            sems.at[2 * h + n],
        )
        for h in range(KV_HEADS) for n, ref in enumerate((k_ref, v_ref))
    ]
    gains = [
        pltpu.make_async_copy(source, target, sems.at[2 * KV_HEADS + n])
        for n, (source, target) in enumerate(((qg_in, qg_ref), (kg_in, kg_ref)))
    ]
    for copy in gains + copies:
        copy.start()
    for copy in gains:
        copy.wait()
    width = qg_ref.shape[0]
    lane = lax.broadcasted_iota(jnp.int32, (2, HEAD_DIM), 1) - shard_ref[0] * width
    row = lax.broadcasted_iota(jnp.int32, (2, HEAD_DIM), 0)
    both = jnp.zeros((2, HEAD_DIM), jnp.float32)
    for i in range(width):
        both = jnp.where(lane == i, jnp.where(row == 0, qg_ref[i], kg_ref[i]), both)
    gain_ref[...] = jnp.broadcast_to(both[None], gain_ref.shape)
    for copy in copies:
        copy.wait()


def pack(k, v, q_gain, k_gain, shard, shards):
    return pl.pallas_call(
        pack_kernel,
        in_specs=[HBM_IN] * 4 + [SMEM_IN],
        out_specs=[VMEM_IN, VMEM_IN],
        out_shape=[
            pltpu.VMEM((ROWS, 2 * KV_HEADS * HEAD_DIM), jnp.bfloat16),
            pltpu.VMEM((shards, 2, HEAD_DIM), jnp.float32),
        ],
        scratch_shapes=[
            pltpu.SMEM(q_gain.shape, jnp.float32),
            pltpu.SMEM(k_gain.shape, jnp.float32),
            pltpu.SemaphoreType.DMA((2 * KV_HEADS + 2,)),
        ],
        compiler_params=pltpu.CompilerParams(vmem_limit_bytes=VMEM),
        name="pack",
    )(*in_hbm(k, v, q_gain, k_gain), shard)


def forward_keys(raw, gain, cosine, sine):
    x = raw.astype(jnp.float32)
    unit = x * lax.rsqrt(jnp.mean(x * x, axis=-1, keepdims=True) + norm_epsilon)
    straight, across = unit * cosine, roll_half(unit) * sine
    return straight, across, (straight * gain + across * roll_half(gain)).astype(jnp.bfloat16)


def over(a, b):
    return jnp.concatenate([a, b], axis=0)


def beside(a, b):
    return jnp.concatenate([a, b], axis=1)


def wide(a):
    return jnp.concatenate([a] * GROUP, axis=1)


def tall(a):
    return jnp.concatenate([a] * GROUP, axis=0)


def attend_kernel(
    q_in, do_in, own_ref, one_ref, two_ref, table_ref, late_ref, gain_ref,
    dq_out, ret1_out, ret2_out, keep_ref, gains_ref, q_ref, do_ref, dq_ref, ret1_ref, ret2_ref, q_total, k_total, in_sems, sems,
):
    group, pair = GROUP * HEAD_DIM, 2 * HEAD_DIM

    def fetch(step):
        width = STEP_HEADS * group
        at = pl.ds(pl.multiple_of(step * width, HEAD_DIM), width)
        return [
            pltpu.make_async_copy(source.at[:, at], target.at[:, at], in_sems.at[n, step])
            for n, (source, target) in enumerate(((q_in, q_ref), (do_in, do_ref)))
        ]

    for step in range(KV_HEADS // STEP_HEADS):
        for copy in fetch(step):
            copy.start()
    gain = jnp.sum(gain_ref[...], axis=0)
    kg = gain[1:2]
    qgt = jnp.broadcast_to(gain[0:1], (HEAD_DIM, HEAD_DIM)).T
    cost, sint = table_ref[6], table_ref[7]
    turn, cross, uncross = wide(qgt * cost), wide(swap_halves(qgt) * sint), wide(qgt * sint)
    late, on_time = tall(late_ref[0]), tall(late_ref[1])
    latet, on_timet = wide(late_ref[2]), wide(late_ref[3])
    take = table_ref[10] > 0.0
    cos0, sin0 = table_ref[0], table_ref[3]
    cos1, sin1 = table_ref[1], table_ref[4]
    cos2 = jnp.where(take, table_ref[2], cos0)
    sin2 = jnp.where(take, table_ref[5], sin0)
    bias = over(wide(table_ref[8]), wide(table_ref[9]))
    q_total[...] = jnp.zeros_like(q_total)
    k_total[...] = jnp.zeros_like(k_total)

    def out(step):
        copies = []
        for n, (source, target) in enumerate(((dq_ref, dq_out), (ret1_ref, ret1_out), (ret2_ref, ret2_out))):
            width = STEP_HEADS * (group if n == 0 else pair)
            at = pl.ds(pl.multiple_of(step * width, HEAD_DIM), width)
            copies.append(pltpu.make_async_copy(source.at[:, at], target.at[:, at], sems.at[n, step]))
        return copies

    def one_head(head):
        heads = pl.ds(pl.multiple_of(head * group, group), group)
        at_k = pl.ds(pl.multiple_of(head * pair, HEAD_DIM), HEAD_DIM)
        at_v = pl.ds(pl.multiple_of(head * pair + HEAD_DIM, HEAD_DIM), HEAD_DIM)
        xt = beside_heads(q_ref[:, heads].T).astype(jnp.float32)
        inv_q = lax.rsqrt(jnp.mean(xt * xt, axis=0, keepdims=True) + norm_epsilon)
        qt = ((xt * turn + swap_halves(xt) * cross) * inv_q).astype(jnp.bfloat16)
        q = jnp.concatenate([qt[:, h * ROWS:(h + 1) * ROWS].T for h in range(GROUP)], axis=0)
        do = stack_heads(do_ref[:, heads])
        dot_ = beside_heads(do_ref[:, heads].T)
        qt_wide = over(qt * on_timet, qt * latet)
        dot_wide = over(dot_ * on_timet, dot_ * latet)
        q_wide = beside(q * on_time, q * late)
        do_wide = beside(do * on_time, do * late)

        v0, v1 = own_ref[:, at_v], one_ref[:, at_v]
        v2 = jnp.where(take, two_ref[:, at_v], v0)
        straight0, across0, k0 = forward_keys(own_ref[:, at_k], kg, cos0, sin0)
        straight1, across1, k1 = forward_keys(one_ref[:, at_k], kg, cos1, sin1)
        straight2, across2, k2 = forward_keys(jnp.where(take, two_ref[:, at_k], own_ref[:, at_k]), kg, cos2, sin2)
        k_all = over(beside(k1, k1), beside(k0, k2))
        v_all = over(beside(v1, v1), beside(v0, v2))
        k1t = k1.T
        kt_all = over(beside(k1t, k0.T), beside(k1t, k2.T))

        s = dot(k_all, qt_wide, NN) * (HEAD_DIM ** (-0.5) * LOG2E) + bias
        w = jnp.exp2(s - jnp.max(s, axis=0, keepdims=True))
        p = w * (1.0 / jnp.sum(w, axis=0, keepdims=True))
        dp = dot(v_all, dot_wide, NN)
        delta = jnp.sum(p * dp, axis=0, keepdims=True)
        ds = (p * (dp - delta) * (HEAD_DIM ** (-0.5))).astype(jnp.bfloat16)

        dv = dot(p.astype(jnp.bfloat16), do_wide, NN)
        dk = dot(ds, q_wide, NN)
        dk1, dv1 = dk[:ROWS, :HEAD_DIM] + dk[:ROWS, HEAD_DIM:], dv[:ROWS, :HEAD_DIM] + dv[:ROWS, HEAD_DIM:]
        dk0, dk2 = dk[ROWS:, :HEAD_DIM], dk[ROWS:, HEAD_DIM:]
        dv0, dv2 = dv[ROWS:, :HEAD_DIM], dv[ROWS:, HEAD_DIM:]

        dqt = dot(kt_all, ds, NN)
        dqt = jnp.where(latet > 0.0, dqt[HEAD_DIM:], dqt[:HEAD_DIM])
        dqt = dqt.astype(jnp.bfloat16).astype(jnp.float32)
        et = dqt * turn - swap_halves(dqt) * uncross
        ext = et * xt
        mean = jnp.mean(ext, axis=0, keepdims=True)
        dxt = (et * inv_q - xt * (inv_q * inv_q * inv_q * mean)).astype(jnp.bfloat16)
        dq_ref[:, heads] = over_heads(dxt).T
        ext = ext * inv_q
        q_total[...] += sum(ext[:, h * ROWS:(h + 1) * ROWS] for h in range(GROUP))
        k_total[0] += fold8(dk0 * straight0 + dk1 * straight1 + dk2 * straight2)
        k_total[1] += fold8(dk0 * across0 + dk1 * across1 + dk2 * across2)

        ret1_ref[:, at_k] = dk1.astype(jnp.bfloat16)
        ret1_ref[:, at_v] = dv1.astype(jnp.bfloat16)
        ret2_ref[:, at_k] = jnp.where(take, dk2, 0.0).astype(jnp.bfloat16)
        ret2_ref[:, at_v] = jnp.where(take, dv2, 0.0).astype(jnp.bfloat16)
        keep_ref[:, at_k] = dk0 + jnp.where(take, 0.0, dk2)
        keep_ref[:, at_v] = dv0 + jnp.where(take, 0.0, dv2)

    @pl.loop(0, KV_HEADS // STEP_HEADS)
    def _(step):
        for copy in fetch(step):
            copy.wait()
        for n in range(STEP_HEADS):
            one_head(step * STEP_HEADS + n)
        for copy in out(step):
            copy.start()

    q_gain_grad = jnp.sum(q_total[...].T, axis=0, keepdims=True) / gain[0:1]
    k_gain_grad = jnp.sum(k_total[0] + roll_half(k_total[1]), axis=0, keepdims=True)
    gains_ref[...] = jnp.broadcast_to(over(q_gain_grad, k_gain_grad)[None], gains_ref.shape)

    @pl.loop(0, KV_HEADS // STEP_HEADS)
    def _(step):
        for copy in out(step):
            copy.wait()


def attend(q, do, own, one, two, tables, peers):
    pair = (ROWS, 2 * KV_HEADS * HEAD_DIM)
    return pl.pallas_call(
        attend_kernel,
        in_specs=[HBM_IN] * 2 + [VMEM_IN] * 6,
        out_specs=[HBM_IN] * 3 + [VMEM_IN] * 2,
        out_shape=[
            pltpu.HBM(q.shape, jnp.bfloat16),
            pltpu.HBM(pair, jnp.bfloat16),
            pltpu.HBM(pair, jnp.bfloat16),
            pltpu.VMEM(pair, jnp.float32),
            pltpu.VMEM((peers, 2, HEAD_DIM), jnp.float32),
        ],
        scratch_shapes=[
            pltpu.VMEM(q.shape, jnp.bfloat16),
            pltpu.VMEM(q.shape, jnp.bfloat16),
            pltpu.VMEM(q.shape, jnp.bfloat16),
            pltpu.VMEM(pair, jnp.bfloat16),
            pltpu.VMEM(pair, jnp.bfloat16),
            pltpu.VMEM((HEAD_DIM, HEAD_DIM), jnp.float32),
            pltpu.VMEM((2, 8, HEAD_DIM), jnp.float32),
            pltpu.SemaphoreType.DMA((2, KV_HEADS // STEP_HEADS)),
            pltpu.SemaphoreType.DMA((3, KV_HEADS // STEP_HEADS)),
        ],
        compiler_params=pltpu.CompilerParams(vmem_limit_bytes=VMEM),
        name="attend",
    )(*in_hbm(q, do), own, one, two, *tables)


def finish_kernel(own_ref, keep_ref, one_ref, two_ref, table_ref, gain_ref, dk_ref, dv_ref, stage, sems):
    gain = jnp.sum(gain_ref[...], axis=0)[1:2]
    copies = []
    for h in range(KV_HEADS):
        at_k, at_v = pl.ds(2 * h * HEAD_DIM, HEAD_DIM), pl.ds((2 * h + 1) * HEAD_DIM, HEAD_DIM)
        dk, dv = (keep_ref[:, at] + one_ref[:, at] + two_ref[:, at] for at in (at_k, at_v))
        x = own_ref[:, at_k].astype(jnp.float32)
        inverse = lax.rsqrt(jnp.mean(x * x, axis=-1, keepdims=True) + norm_epsilon)
        dk = dk.astype(jnp.bfloat16).astype(jnp.float32)
        e = unrotate(dk, table_ref[0], table_ref[3]) * gain
        mean = jnp.mean(e * x, axis=-1, keepdims=True)
        stage[0, h] = (inverse * (e - x * (inverse * inverse * mean))).astype(jnp.bfloat16)
        stage[1, h] = dv.astype(jnp.bfloat16)
        for n, ref in enumerate((dk_ref, dv_ref)):
            at = pl.ds(h * HEAD_DIM, HEAD_DIM)
            copies.append(pltpu.make_async_copy(stage.at[n, h], ref.at[:, at], sems.at[n, h]))
            copies[-1].start()
    for copy in copies:
        copy.wait()


def finish(own, keep, one, two, table, gain):
    out = jax.ShapeDtypeStruct((ROWS, KV_HEADS * HEAD_DIM), jnp.bfloat16)
    return pl.pallas_call(
        finish_kernel,
        in_specs=[VMEM_IN] * 6,
        out_specs=[HBM_IN] * 2,
        out_shape=[out, out],
        scratch_shapes=[
            pltpu.VMEM((2, KV_HEADS, ROWS, HEAD_DIM), jnp.bfloat16),
            pltpu.SemaphoreType.DMA((2, KV_HEADS)),
        ],
        compiler_params=pltpu.CompilerParams(vmem_limit_bytes=VMEM),
        name="finish",
    )(own, keep, one, two, table, gain)


AXES = ("seq", "fsdp")


def device_at(y, z, x, core):
    return ((y % 4 * 4 + x) * 2 + core) * 16 + y // 4 * 8 + z


def gain_groups():
    return [
        [device_at(a, z, x, c) for z in range(8)] + [device_at(4 + (a + 2) % 4, z, x, c) for z in range(8)]
        for a in range(4) for x in range(4) for c in range(2)
    ]


def plane_groups():
    return [[device_at(y, z, x, c) for z in range(8) for x in range(4) for c in range(2)] for y in range(8)]


def column_groups():
    return [[device_at(y, z, x, c) for y in range(8)] for z in range(8) for x in range(4) for c in range(2)]


def swap(rows, groups):
    return lax.all_to_all(rows, AXES, 0, 0, axis_index_groups=groups, tiled=True)


def local(query_raw, key_raw, value_proj, out_grad, query_gain, key_gain, turn_lengths):
    me, shard = lax.axis_index("seq"), lax.axis_index("fsdp")
    seq, shards = lax.axis_size("seq"), lax.axis_size("fsdp")
    base = me * ROWS

    own, gain = pack(key_raw[0], value_proj[0], query_gain, key_gain, shard[None], shards)
    table, late = block_tables(turn_lengths[0], base[None])
    two = lax.ppermute(own, "seq", [(i, i + 2) for i in range(seq - 2)])
    gain = swap(gain, gain_groups())
    one, gain, table = lax.optimization_barrier((jnp.where(me % 2 == 1, two, own), gain, table))
    one = lax.ppermute(one, "seq", [(i, i ^ 1) for i in range(seq)])
    q_grad, ret1, ret2, keep, parts = attend(query_raw[0], out_grad[0], own, one, two, (table, late, gain), 64)

    back2 = lax.ppermute(ret2, "seq", [(i + 2, i) for i in range(seq - 2)])
    part = jnp.sum(swap(parts, plane_groups()), axis=0)
    ret1, part = lax.optimization_barrier((ret1, part))
    back1 = lax.ppermute(ret1, "seq", [(i + 1, i) for i in range(seq - 1)])
    total = swap(jnp.broadcast_to(part[None], (8, 2, HEAD_DIM)), column_groups())
    k_grad, v_grad = finish(own, keep, back1, back2, table, gain)
    total, k_grad, v_grad = lax.optimization_barrier((total, k_grad, v_grad))
    total = jnp.sum(total, axis=0)
    shard_rows = total.reshape(2, shards, HEAD_DIM // shards)
    gain_grad = lax.dynamic_slice_in_dim(shard_rows, shard, 1, axis=1)

    return q_grad[None], k_grad[None], v_grad[None], gain_grad[0, 0], gain_grad[1, 0]


def solution(mesh):
    return jax.shard_map(
        local,
        mesh=mesh,
        in_specs=(
            P("fsdp", "seq", None),
            P("fsdp", "seq", None),
            P("fsdp", "seq", None),
            P("fsdp", "seq", None),
            P("fsdp"),
            P("fsdp"),
            P("fsdp", None),
        ),
        out_specs=(
            P("fsdp", "seq", None),
            P("fsdp", "seq", None),
            P("fsdp", "seq", None),
            P("fsdp"),
            P("fsdp"),
        ),
        check_vma=False,
    )
```

time: 94.4 us -> 77.8 us (0.82)
  blocking collectives: 19.3 us -> 0 us
  waiting for transfers between devices: 13.7 us -> 22.9 us
  local copies, waits for them, and re-layouts: 7.61 us -> 1.87 us
  starting transfers between devices: 30.6 us -> 36 us
  Pallas kernels: 19.6 us -> 14.9 us
  other arithmetic: 2.21 us -> 0.15 us
    all_to_all x1 -> x0, blocking collectives: 19.3 us -> none  [swap(): lax.all_to_all(rows, AXES, 0, 0, axis_index_groups=groups, tiled=True)]
    ppermute x1, waiting for transfers between devices: 0.01 us -> 5.27 us  [local(): back1 = lax.ppermute(ret1, 'seq', [(i + 1, i) for i in range(seq - 1)])]
    unnamed x16 -> x4, local copies, waits for them, and re-layouts: 5.69 us -> 0.66 us
    all_to_all x2 -> x3, starting transfers between devices: 19.3 us -> 24.2 us  [swap(): lax.all_to_all(rows, AXES, 0, 0, axis_index_groups=groups, tiled=True)]
    pallas_call x3 -> x4, Pallas kernels: 19.6 us -> 14.9 us  [the longest x1 10 us: attend(): pl.pallas_call(attend_kernel, in_specs=[HBM_IN] * 2 + [VMEM_IN] * 6, out_...]
    all_to_all x2 -> x3, waiting for transfers between devices: 13.7 us -> 16.1 us  [swap(): lax.all_to_all(rows, AXES, 0, 0, axis_index_groups=groups, tiled=True)]
    ppermute x1, waiting for transfers between devices: 0.01 us -> 1.51 us  [local(): one = lax.ppermute(one, 'seq', [(i, i ^ 1) for i in range(seq)])]
    concatenate x2 -> x0, other arithmetic: 1.24 us -> none  [the longest x1 1.07 us: local(): own = jnp.concatenate([key_raw[0], value_proj[0]], axis=1)]
  transfers between devices with their start and end apart: 6 -> 7, of which waited for: 2 -> 4; matrix products, arithmetic and copies ran while one was open for 3% -> 1% of each run, Pallas kernels for 2% -> 4%
where the time goes in v2:
time: 77.8 us; the launch traced here: 76.6 us
  starting transfers between devices  36 us (46%)
  waiting for transfers between devices  22.9 us (29%)
  Pallas kernels  14.9 us (19%)
  local copies, waits for them, and re-layouts  1.87 us (2%)
  between operations  0.78 us (1%)
    all_to_all x3, starting transfers between devices, swap(): lax.all_to_all(rows, AXES, 0, 0, axis_index_groups=groups, tiled=True)  24.2 us
    all_to_all x3, waiting for transfers between devices, swap(): lax.all_to_all(rows, AXES, 0, 0, axis_index_groups=groups, tiled=True)  16.1 us
    pallas_call x1, Pallas kernels, attend(): pl.pallas_call(attend_kernel, in_specs=[HBM_IN] * 2 + [VMEM_IN] * 6, out_...  10 us
    ppermute x1, waiting for transfers between devices, local(): back1 = lax.ppermute(ret1, 'seq', [(i + 1, i) for i in range(seq - 1)])  5.27 us
    ppermute x1, starting transfers between devices, local(): one = lax.ppermute(one, 'seq', [(i, i ^ 1) for i in range(seq)])  4.28 us
    ppermute x1, starting transfers between devices, local(): two = lax.ppermute(own, 'seq', [(i, i + 2) for i in range(seq - 2)])  3.98 us
    ppermute x1, starting transfers between devices, local(): back1 = lax.ppermute(ret1, 'seq', [(i + 1, i) for i in range(seq - 1)])  2.29 us
    pallas_call x1, Pallas kernels, pack(): pl.pallas_call(pack_kernel, in_specs=[HBM_IN] * 4 + [SMEM_IN], out_specs=...  1.77 us
  transfers between devices with their start and end apart: 7, of which 4 were waited for; matrix products, arithmetic and copies ran while one was open for 1% of the time, Pallas kernels for 4%

profile of v2, /device:TPU:1, one launch (start us, length us, event | category | flops | bytes accessed | tf_op | source)
XLA Modules:
  0.0 76.6 jit_solution(8110028992625030740)
XLA Ops:
  0.6 1.8 %pack.1 = (bf16[128,2048]{1,0:T(8,128)(2,1)S(1)}, f32[16,2,128]{2,1,0:T(2,128)}) custom-call(bf16[128,1024]{1,0:T(8,128)(2,1)} %bitcast.17, bf16[128,1024]{1,0:T(8,128)(2,1)} %bitcast.18, f32[8]{0:T(128)} %qg_in.1, f32[8]{0:T(128)} %kg_in.1, s32[1]{0:T(128)} %bitcast.4.shard_ref), custom_call_target="tpu_custom_call" | custom-call | tf_op jit(solution)/shard_map/pack/pallas_call | solution.py:153
  2.4 4.0 %collective-permute-start = (bf16[128,2048]{1,0:T(8,128)(2,1)S(1)}, bf16[128,2048]{1,0:T(8,128)(2,1)S(1)}, u32[]{:S(2)}, u32[]{:S(2)}) collective-permute-start(bf16[128,2048]{1,0:T(8,128)(2,1)S(1)} %get-tuple-element.24.own_ref), channel_id=1, source_target_pairs={{0,32},{16,48},{32,64},{48,80},{64,96},{80,112},{96,128},{112,144}... | collective-permute-start | bytes 1572872 | tf_op jit(solution)/shard_map/ppermute | solution.py:411
  6.4 13.8 %all-to-all-start = ((f32[16,2,128]{2,1,0:T(2,128)}), f32[16,2,128]{2,1,0:T(2,128)S(1)}, u32[]{:S(2)}, u32[]{:S(2)}) async-start(f32[16,2,128]{2,1,0:T(2,128)} %get-tuple-element.25), calls=%async_computation | async-start | bytes 32768 | tf_op jit(solution)/shard_map/all_to_all | solution.py:401
  20.2 0.0 copy-start
  20.3 0.0 copy-start.1
  20.3 0.6 copy-done
  20.9 0.0 copy-done.1
  20.9 1.4 %tables.1 = (f32[11,128,128]{2,1,0:T(8,128)S(1)}, bf16[4,128,128]{2,1,0:T(8,128)(2,1)S(1)}) custom-call(s32[48]{0:T(128)S(1)} %bitcast.14, s32[1]{0:T(128)} %bitcast.6.place_ref, f32[1,128]{1,0:T(1,128)S(1)} %copy-done.1), custom_call_target="tpu_custom_call" | custom-call | tf_op jit(solution)/shard_map/tables/pallas_call | solution.py:111
  22.3 0.0 collective-permute-done.two_ref
  22.3 0.1 broadcast_select_fusion
  22.4 7.3 %all-to-all-done.gain_ref = f32[16,2,128]{2,1,0:T(2,128)S(1)} async-done(((f32[16,2,128]{2,1,0:T(2,128)}), f32[16,2,128]{2,1,0:T(2,128)S(1)}, u32[]{:S(2)}, u32[]{:S(2)}) %all-to-all-start) | async-done | bytes 16416 | tf_op jit(solution)/shard_map/all_to_all | solution.py:401
  29.7 4.3 %collective-permute-start.1 = (bf16[128,2048]{1,0:T(8,128)(2,1)S(1)}, bf16[128,2048]{1,0:T(8,128)(2,1)S(1)}, u32[]{:S(2)}, u32[]{:S(2)}) collective-permute-start(bf16[128,2048]{1,0:T(8,128)(2,1)S(1)} %broadcast_select_fusion), channel_id=1, source_target_pairs={{0,16},{16,0},{32,48},{48,32},{64,80},{80,64},{96,112},{112,96},{1... | collective-permute-start | bytes 1572872 | tf_op jit(solution)/shard_map/ppermute | solution.py:414
  34.0 1.5 %collective-permute-done.1.one_ref = bf16[128,2048]{1,0:T(8,128)(2,1)S(1)} collective-permute-done((bf16[128,2048]{1,0:T(8,128)(2,1)S(1)}, bf16[128,2048]{1,0:T(8,128)(2,1)S(1)}, u32[]{:S(2)}, u32[]{:S(2)}) %collective-permute-start.1) | collective-permute-done | bytes 524320 | tf_op jit(solution)/shard_map/ppermute | solution.py:414
  35.5 10.0 %attend.1 = (bf16[128,4096]{1,0:T(8,128)(2,1)}, bf16[128,2048]{1,0:T(8,128)(2,1)}, bf16[128,2048]{1,0:T(8,128)(2,1)}, f32[128,2048]{1,0:T(8,128)S(1)}, f32[64,2,128]{2,1,0:T(2,128)}) custom-call(bf16[128,4096]{1,0:T(8,128)(2,1)} %bitcast.15, bf16[128,4096]{1,0:T(8,128)(2,1)} %bitcast.16, bf16[128,2048]{1,0:T(8,128)(2,1)S(1)} %get-tuple-element.24.own_ref, ...), custom_call_target="tpu_custom_call" | custom-call | tf_op jit(solution)/shard_map/attend/pallas_call | solution.py:314
  45.5 6.5 %all-to-all-start.1 = ((f32[64,2,128]{2,1,0:T(2,128)}), f32[64,2,128]{2,1,0:T(2,128)S(1)}, u32[]{:S(2)}, u32[]{:S(2)}) async-start(f32[64,2,128]{2,1,0:T(2,128)} %get-tuple-element.33), calls=%async_computation.1 | async-start | bytes 131072 | tf_op jit(solution)/shard_map/all_to_all | solution.py:401
  52.1 1.3 %collective-permute-start.3 = (bf16[128,2048]{1,0:T(8,128)(2,1)}, bf16[128,2048]{1,0:T(8,128)(2,1)S(1)}, u32[]{:S(2)}, u32[]{:S(2)}) collective-permute-start(bf16[128,2048]{1,0:T(8,128)(2,1)} %get-tuple-element.37), channel_id=1, source_target_pairs={{32,0},{48,16},{64,32},{80,48},{96,64},{112,80},{128,96},{144,112}... | collective-permute-start | bytes 1572872 | tf_op jit(solution)/shard_map/ppermute | solution.py:417
  53.4 8.8 %all-to-all-done.1 = f32[64,2,128]{2,1,0:T(2,128)S(1)} async-done(((f32[64,2,128]{2,1,0:T(2,128)}), f32[64,2,128]{2,1,0:T(2,128)S(1)}, u32[]{:S(2)}, u32[]{:S(2)}) %all-to-all-start.1) | async-done | bytes 65568 | tf_op jit(solution)/shard_map/all_to_all | solution.py:401
  62.2 0.1 reduce_sum.18
  62.2 2.3 %collective-permute-start.2 = (bf16[128,2048]{1,0:T(8,128)(2,1)}, bf16[128,2048]{1,0:T(8,128)(2,1)S(1)}, u32[]{:S(2)}, u32[]{:S(2)}) collective-permute-start(bf16[128,2048]{1,0:T(8,128)(2,1)} %get-tuple-element.36), channel_id=1, source_target_pairs={{16,0},{32,16},{48,32},{64,48},{80,64},{96,80},{112,96},{128,112},... | collective-permute-start | bytes 1572872 | tf_op jit(solution)/shard_map/ppermute | solution.py:420
  64.5 0.6 broadcast_in_dim.24
  65.1 3.8 %all-to-all-start.2 = ((f32[8,2,128]{2,1,0:T(2,128)}), f32[8,2,128]{2,1,0:T(2,128)S(1)}, u32[]{:S(2)}, u32[]{:S(2)}) async-start(f32[8,2,128]{2,1,0:T(2,128)} %broadcast_in_dim.24), calls=%async_computation.2 | async-start | bytes 16384 | tf_op jit(solution)/shard_map/all_to_all | solution.py:401
  68.9 0.0 collective-permute-done.3.two_ref
  68.9 5.3 %collective-permute-done.2.one_ref = bf16[128,2048]{1,0:T(8,128)(2,1)S(1)} collective-permute-done((bf16[128,2048]{1,0:T(8,128)(2,1)}, bf16[128,2048]{1,0:T(8,128)(2,1)S(1)}, u32[]{:S(2)}, u32[]{:S(2)}) %collective-permute-start.2) | collective-permute-done | bytes 524320 | tf_op jit(solution)/shard_map/ppermute | solution.py:420
  74.2 1.7 %finish.1 = (bf16[128,1024]{1,0:T(8,128)(2,1)}, bf16[128,1024]{1,0:T(8,128)(2,1)}) custom-call(bf16[128,2048]{1,0:T(8,128)(2,1)S(1)} %get-tuple-element.24.own_ref, f32[128,2048]{1,0:T(8,128)S(1)} %get-tuple-element.35.keep_ref, bf16[128,2048]{1,0:T(8,128)(2,1)S(1)} %collective-permute-done.2.one_ref, bf16[128,2048]{1,0:T(8,128)(2,1)S(1)} %collective-permute-done.3.two_ref, ...), custom_call_target="tpu_custom_call" | custom-call | tf_op jit(solution)/shard_map/finish/pallas_call | solution.py:364
  76.0 0.0 all-to-all-done.2
  76.0 0.1 reshape.14
  76.1 0.5 dynamic-slice_bitcast_fusion
  (1 shorter events, 0.0 us)
Async XLA Ops:
  2.4 19.9 %collective-permute-start = (bf16[128,2048]{1,0:T(8,128)(2,1)S(1)}, bf16[128,2048]{1,0:T(8,128)(2,1)S(1)}, u32[]{:S(2)}, u32[]{:S(2)}) collective-permute-start(bf16[128,2048]{1,0:T(8,128)(2,1)S(1)} %get-tuple-element.24.own_ref), channel_id=1, source_target_pairs={{0,32},{16,48},{32,64},{48,80},{64,96},{80,112},{96,128},{112,144}... | collective-permute-start | bytes 1572872 | tf_op jit(solution)/shard_map/ppermute | solution.py:411
  6.4 23.3 %all-to-all-start = ((f32[16,2,128]{2,1,0:T(2,128)}), f32[16,2,128]{2,1,0:T(2,128)S(1)}, u32[]{:S(2)}, u32[]{:S(2)}) async-start(f32[16,2,128]{2,1,0:T(2,128)} %get-tuple-element.25), calls=%async_computation | async-start | bytes 32768 | tf_op jit(solution)/shard_map/all_to_all | solution.py:401
  20.2 0.7 copy-start
  20.3 0.7 copy-start.1
  29.7 5.8 %collective-permute-start.1 = (bf16[128,2048]{1,0:T(8,128)(2,1)S(1)}, bf16[128,2048]{1,0:T(8,128)(2,1)S(1)}, u32[]{:S(2)}, u32[]{:S(2)}) collective-permute-start(bf16[128,2048]{1,0:T(8,128)(2,1)S(1)} %broadcast_select_fusion), channel_id=1, source_target_pairs={{0,16},{16,0},{32,48},{48,32},{64,80},{80,64},{96,112},{112,96},{1... | collective-permute-start | bytes 1572872 | tf_op jit(solution)/shard_map/ppermute | solution.py:414
  45.5 16.6 %all-to-all-start.1 = ((f32[64,2,128]{2,1,0:T(2,128)}), f32[64,2,128]{2,1,0:T(2,128)S(1)}, u32[]{:S(2)}, u32[]{:S(2)}) async-start(f32[64,2,128]{2,1,0:T(2,128)} %get-tuple-element.33), calls=%async_computation.1 | async-start | bytes 131072 | tf_op jit(solution)/shard_map/all_to_all | solution.py:401
  52.1 16.9 %collective-permute-start.3 = (bf16[128,2048]{1,0:T(8,128)(2,1)}, bf16[128,2048]{1,0:T(8,128)(2,1)S(1)}, u32[]{:S(2)}, u32[]{:S(2)}) collective-permute-start(bf16[128,2048]{1,0:T(8,128)(2,1)} %get-tuple-element.37), channel_id=1, source_target_pairs={{32,0},{48,16},{64,32},{80,48},{96,64},{112,80},{128,96},{144,112}... | collective-permute-start | bytes 1572872 | tf_op jit(solution)/shard_map/ppermute | solution.py:417
  62.2 12.0 %collective-permute-start.2 = (bf16[128,2048]{1,0:T(8,128)(2,1)}, bf16[128,2048]{1,0:T(8,128)(2,1)S(1)}, u32[]{:S(2)}, u32[]{:S(2)}) collective-permute-start(bf16[128,2048]{1,0:T(8,128)(2,1)} %get-tuple-element.36), channel_id=1, source_target_pairs={{16,0},{32,16},{48,32},{64,48},{80,64},{96,80},{112,96},{128,112},... | collective-permute-start | bytes 1572872 | tf_op jit(solution)/shard_map/ppermute | solution.py:420
  65.1 10.8 %all-to-all-start.2 = ((f32[8,2,128]{2,1,0:T(2,128)}), f32[8,2,128]{2,1,0:T(2,128)S(1)}, u32[]{:S(2)}, u32[]{:S(2)}) async-start(f32[8,2,128]{2,1,0:T(2,128)} %broadcast_in_dim.24), calls=%async_computation.2 | async-start | bytes 16384 | tf_op jit(solution)/shard_map/all_to_all | solution.py:401

commit v3 on v2

--- a/solution.py
+++ b/solution.py
@@ -17,7 +17,8 @@
 rope_base = 1000000.0
 MASKED = -1e30
 LOG2E = 1.4426950408889634
-STEP_HEADS = 4
+OUT_HEADS = 2
+FIRST_HEADS = 2
 VMEM = 24 * 1024 * 1024
 
 NT = (((1,), (1,)), ((), ()))
@@ -64,18 +65,19 @@
     return jnp.concatenate([x[:, h * HEAD_DIM:(h + 1) * HEAD_DIM] for h in range(GROUP)], axis=0)
 
 
-def table_kernel(len_ref, place_ref, freq_ref, table_ref, late_ref):
-    shape = (ROWS, ROWS)
+def table_kernel(len_ref, place_ref, freq_ref, q_in, do_in, table_ref, row_ref, q_ref, do_ref, sems):
+    copies = [
+        pltpu.make_async_copy(source.at[:, pl.ds(0, target.shape[1])], target, sems.at[n])
+        for n, (source, target) in enumerate(((q_in, q_ref), (do_in, do_ref)))
+    ]
+    for copy in copies:
+        copy.start()
     base = place_ref[0]
-    row = lax.broadcasted_iota(jnp.int32, shape, 0)
-    lane = lax.broadcasted_iota(jnp.int32, shape, 1)
-    for back in range(3):
-        angles = (base - back * ROWS + row).astype(jnp.float32) * freq_ref[...]
-        cosine, sine = jnp.cos(angles), jnp.sin(angles)
-        sine = jnp.where(lane < HALF, -sine, sine)
-        table_ref[back], table_ref[3 + back] = cosine, sine
-        if back == 0:
-            table_ref[6], table_ref[7] = cosine.T, sine.T
+    freqs = freq_ref[...]
+    token = lax.broadcasted_iota(jnp.int32, (ROWS, HEAD_DIM), 0) + base
+    angles = token.astype(jnp.float32) * freqs
+    table_ref[0] = jnp.cos(angles)
+    table_ref[1] = signed(jnp.sin(angles))
 
     here = lax.broadcasted_iota(jnp.int32, (8, ROWS), 1)
     first = jnp.zeros((8, ROWS), jnp.int32) - base
@@ -83,17 +85,18 @@
     for k in range(len_ref.shape[0] - 1):
         end = end + len_ref[k]
         first = jnp.where(here >= end, end, first)
-    first = jnp.concatenate([first] * (ROWS // 8), axis=0)
-    table_ref[8] = jnp.where(row >= first + ROWS, 0.0, MASKED)
-    own = (row <= lane) & (row >= first)
-    table_ref[9] = jnp.where(own | (row >= first + 2 * ROWS), 0.0, MASKED)
-    head = jnp.broadcast_to(first[:, 0:1], shape)
-    table_ref[10] = jnp.where(row >= head + 2 * ROWS, 1.0, 0.0)
-    late = jnp.where(first < -ROWS, 1.0, 0.0)
-    late_ref[0] = late.T.astype(jnp.bfloat16)
-    late_ref[1] = (1.0 - late).T.astype(jnp.bfloat16)
-    late_ref[2] = late.astype(jnp.bfloat16)
-    late_ref[3] = (1.0 - late).astype(jnp.bfloat16)
+    row_ref[0] = first.astype(jnp.float32)
+    for n in (1, 2):
+        angle = jnp.broadcast_to(freqs * float(n * ROWS), (8, HEAD_DIM))
+        row_ref[2 * n - 1] = jnp.cos(angle)
+        row_ref[2 * n] = signed(jnp.sin(angle))
+    for copy in copies:
+        copy.wait()
+
+
+def signed(sine):
+    lane = lax.broadcasted_iota(jnp.int32, sine.shape, 1)
+    return jnp.where(lane < HALF, -sine, sine)
 
 
 SMEM_IN = pl.BlockSpec(memory_space=pltpu.SMEM)
@@ -105,20 +108,23 @@
     return [pltpu.with_memory_space_constraint(a, pltpu.HBM) for a in arrays]
 
 
-def block_tables(lengths, place):
+def block_tables(lengths, place, q, do):
     half = rope_base ** (-np.arange(HALF) * 2.0 / HEAD_DIM)
     freqs = jnp.asarray(np.concatenate([half, half])[None], jnp.float32)
     return pl.pallas_call(
         table_kernel,
-        in_specs=[SMEM_IN, SMEM_IN, VMEM_IN],
-        out_specs=[VMEM_IN] * 2,
+        in_specs=[SMEM_IN, SMEM_IN, VMEM_IN, HBM_IN, HBM_IN],
+        out_specs=[VMEM_IN] * 4,
         out_shape=[
-            pltpu.VMEM((11, ROWS, ROWS), jnp.float32),
-            pltpu.VMEM((4, ROWS, ROWS), jnp.bfloat16),
-        ],
+            pltpu.VMEM((2, ROWS, HEAD_DIM), jnp.float32),
+            pltpu.VMEM((5, 8, HEAD_DIM), jnp.float32),
+            pltpu.VMEM((ROWS, FIRST_HEADS * GROUP * HEAD_DIM), q.dtype),
+            pltpu.VMEM((ROWS, FIRST_HEADS * GROUP * HEAD_DIM), q.dtype),
+        ],
+        scratch_shapes=[pltpu.SemaphoreType.DMA((2,))],
         compiler_params=pltpu.CompilerParams(vmem_limit_bytes=VMEM),
         name="tables",
-    )(lengths, place, freqs)
+    )(lengths, place, freqs, *in_hbm(q, do))
 
 
 def pack_kernel(k_ref, v_ref, qg_in, kg_in, shard_ref, own_ref, gain_ref, qg_ref, kg_ref, sems):
@@ -192,56 +198,75 @@
 
 
 def attend_kernel(
-    q_in, do_in, own_ref, one_ref, two_ref, table_ref, late_ref, gain_ref,
-    dq_out, ret1_out, ret2_out, keep_ref, gains_ref, q_ref, do_ref, dq_ref, ret1_ref, ret2_ref, q_total, k_total, in_sems, sems,
+    q_first, do_first, q_in, do_in, own_ref, one_ref, two_ref, table_ref, row_ref, gain_ref,
+    dq_out, ret1_out, ret2_out, keep_ref, gains_ref, q_rest, do_rest, dq_ref, ret1_ref, ret2_ref, q_total, k_total, in_sems, sems,
 ):
     group, pair = GROUP * HEAD_DIM, 2 * HEAD_DIM
 
-    def fetch(step):
-        width = STEP_HEADS * group
-        at = pl.ds(pl.multiple_of(step * width, HEAD_DIM), width)
-        return [
-            pltpu.make_async_copy(source.at[:, at], target.at[:, at], in_sems.at[n, step])
-            for n, (source, target) in enumerate(((q_in, q_ref), (do_in, do_ref)))
-        ]
-
-    for step in range(KV_HEADS // STEP_HEADS):
-        for copy in fetch(step):
-            copy.start()
+    ahead = q_first.shape[1]
+    fetch = [
+        pltpu.make_async_copy(source.at[:, pl.ds(ahead, target.shape[1])], target, in_sems.at[n])
+        for n, (source, target) in enumerate(((q_in, q_rest), (do_in, do_rest)))
+    ]
+    for copy in fetch:
+        copy.start()
+
     gain = jnp.sum(gain_ref[...], axis=0)
     kg = gain[1:2]
     qgt = jnp.broadcast_to(gain[0:1], (HEAD_DIM, HEAD_DIM)).T
-    cost, sint = table_ref[6], table_ref[7]
+    cos0, sin0 = table_ref[0], table_ref[1]
+    cost, sint = cos0.T, sin0.T
     turn, cross, uncross = wide(qgt * cost), wide(swap_halves(qgt) * sint), wide(qgt * sint)
-    late, on_time = tall(late_ref[0]), tall(late_ref[1])
-    latet, on_timet = wide(late_ref[2]), wide(late_ref[3])
-    take = table_ref[10] > 0.0
-    cos0, sin0 = table_ref[0], table_ref[3]
-    cos1, sin1 = table_ref[1], table_ref[4]
-    cos2 = jnp.where(take, table_ref[2], cos0)
-    sin2 = jnp.where(take, table_ref[5], sin0)
-    bias = over(wide(table_ref[8]), wide(table_ref[9]))
+
+    row = lax.broadcasted_iota(jnp.int32, (ROWS, ROWS), 0).astype(jnp.float32)
+    lane = lax.broadcasted_iota(jnp.int32, (ROWS, ROWS), 1).astype(jnp.float32)
+    first = jnp.concatenate([row_ref[0]] * (ROWS // 8), axis=0)
+    late_f = jnp.where(first < -ROWS, 1.0, 0.0)
+    latet = wide(late_f.astype(jnp.bfloat16))
+    on_timet = wide((1.0 - late_f).astype(jnp.bfloat16))
+    late_f = late_f.T
+    late = tall(late_f.astype(jnp.bfloat16))
+    on_time = tall((1.0 - late_f).astype(jnp.bfloat16))
+    take = row >= jnp.broadcast_to(first[:, 0:1], row.shape) + 2 * ROWS
+    own = (row <= lane) & (row >= first)
+    bias = over(
+        wide(jnp.where(row >= first + ROWS, 0.0, MASKED)),
+        wide(jnp.where(own | (row >= first + 2 * ROWS), 0.0, MASKED)),
+    )
+
+    def back(n):
+        cosine, sine = row_ref[2 * n - 1][0:1], row_ref[2 * n][0:1]
+        return cos0 * cosine + sin0 * sine, sin0 * cosine - cos0 * sine
+
+    cos1, sin1 = back(1)
+    cos2, sin2 = back(2)
+    cos2, sin2 = jnp.where(take, cos2, cos0), jnp.where(take, sin2, sin0)
     q_total[...] = jnp.zeros_like(q_total)
     k_total[...] = jnp.zeros_like(k_total)
 
     def out(step):
         copies = []
         for n, (source, target) in enumerate(((dq_ref, dq_out), (ret1_ref, ret1_out), (ret2_ref, ret2_out))):
-            width = STEP_HEADS * (group if n == 0 else pair)
-            at = pl.ds(pl.multiple_of(step * width, HEAD_DIM), width)
+            width = OUT_HEADS * (group if n == 0 else pair)
+            at = pl.ds(step * width, width)
             copies.append(pltpu.make_async_copy(source.at[:, at], target.at[:, at], sems.at[n, step]))
         return copies
 
     def one_head(head):
-        heads = pl.ds(pl.multiple_of(head * group, group), group)
-        at_k = pl.ds(pl.multiple_of(head * pair, HEAD_DIM), HEAD_DIM)
-        at_v = pl.ds(pl.multiple_of(head * pair + HEAD_DIM, HEAD_DIM), HEAD_DIM)
-        xt = beside_heads(q_ref[:, heads].T).astype(jnp.float32)
+        heads = slice(head * group, (head + 1) * group)
+        at_k = slice(head * pair, head * pair + HEAD_DIM)
+        at_v = slice(head * pair + HEAD_DIM, (head + 1) * pair)
+        among = heads
+        q_ref, do_ref = q_first, do_first
+        if head >= FIRST_HEADS:
+            among = slice(head * group - ahead, (head + 1) * group - ahead)
+            q_ref, do_ref = q_rest, do_rest
+        xt = beside_heads(q_ref[:, among].T).astype(jnp.float32)
         inv_q = lax.rsqrt(jnp.mean(xt * xt, axis=0, keepdims=True) + norm_epsilon)
         qt = ((xt * turn + swap_halves(xt) * cross) * inv_q).astype(jnp.bfloat16)
         q = jnp.concatenate([qt[:, h * ROWS:(h + 1) * ROWS].T for h in range(GROUP)], axis=0)
-        do = stack_heads(do_ref[:, heads])
-        dot_ = beside_heads(do_ref[:, heads].T)
+        do = stack_heads(do_ref[:, among])
+        dot_ = beside_heads(do_ref[:, among].T)
         qt_wide = over(qt * on_timet, qt * latet)
         dot_wide = over(dot_ * on_timet, dot_ * latet)
         q_wide = beside(q * on_time, q * late)
@@ -290,30 +315,29 @@
         keep_ref[:, at_k] = dk0 + jnp.where(take, 0.0, dk2)
         keep_ref[:, at_v] = dv0 + jnp.where(take, 0.0, dv2)
 
-    @pl.loop(0, KV_HEADS // STEP_HEADS)
-    def _(step):
-        for copy in fetch(step):
-            copy.wait()
-        for n in range(STEP_HEADS):
-            one_head(step * STEP_HEADS + n)
-        for copy in out(step):
-            copy.start()
+    for head in range(KV_HEADS):
+        if head == FIRST_HEADS:
+            for copy in fetch:
+                copy.wait()
+        one_head(head)
+        if head % OUT_HEADS == OUT_HEADS - 1:
+            for copy in out(head // OUT_HEADS):
+                copy.start()
 
     q_gain_grad = jnp.sum(q_total[...].T, axis=0, keepdims=True) / gain[0:1]
     k_gain_grad = jnp.sum(k_total[0] + roll_half(k_total[1]), axis=0, keepdims=True)
     gains_ref[...] = jnp.broadcast_to(over(q_gain_grad, k_gain_grad)[None], gains_ref.shape)
 
-    @pl.loop(0, KV_HEADS // STEP_HEADS)
-    def _(step):
+    for step in range(KV_HEADS // OUT_HEADS):
         for copy in out(step):
             copy.wait()
 
 
-def attend(q, do, own, one, two, tables, peers):
+def attend(q_first, do_first, q, do, own, one, two, tables, peers):
     pair = (ROWS, 2 * KV_HEADS * HEAD_DIM)
     return pl.pallas_call(
         attend_kernel,
-        in_specs=[HBM_IN] * 2 + [VMEM_IN] * 6,
+        in_specs=[VMEM_IN] * 2 + [HBM_IN] * 2 + [VMEM_IN] * 6,
         out_specs=[HBM_IN] * 3 + [VMEM_IN] * 2,
         out_shape=[
             pltpu.HBM(q.shape, jnp.bfloat16),
@@ -323,19 +347,35 @@
             pltpu.VMEM((peers, 2, HEAD_DIM), jnp.float32),
         ],
         scratch_shapes=[
-            pltpu.VMEM(q.shape, jnp.bfloat16),
-            pltpu.VMEM(q.shape, jnp.bfloat16),
+            pltpu.VMEM((ROWS, q.shape[1] - q_first.shape[1]), jnp.bfloat16),
+            pltpu.VMEM((ROWS, q.shape[1] - q_first.shape[1]), jnp.bfloat16),
             pltpu.VMEM(q.shape, jnp.bfloat16),
             pltpu.VMEM(pair, jnp.bfloat16),
             pltpu.VMEM(pair, jnp.bfloat16),
             pltpu.VMEM((HEAD_DIM, HEAD_DIM), jnp.float32),
             pltpu.VMEM((2, 8, HEAD_DIM), jnp.float32),
-            pltpu.SemaphoreType.DMA((2, KV_HEADS // STEP_HEADS)),
-            pltpu.SemaphoreType.DMA((3, KV_HEADS // STEP_HEADS)),
+            pltpu.SemaphoreType.DMA((2,)),
+            pltpu.SemaphoreType.DMA((3, KV_HEADS // OUT_HEADS)),
         ],
         compiler_params=pltpu.CompilerParams(vmem_limit_bytes=VMEM),
         name="attend",
-    )(*in_hbm(q, do), own, one, two, *tables)
+    )(q_first, do_first, *in_hbm(q, do), own, one, two, *tables)
+
+
+def add_up_kernel(parts_ref, out_ref):
+    total = jnp.sum(parts_ref[...], axis=0, keepdims=True)
+    out_ref[...] = jnp.broadcast_to(total, out_ref.shape)
+
+
+def add_up(parts, peers):
+    return pl.pallas_call(
+        add_up_kernel,
+        in_specs=[VMEM_IN],
+        out_specs=VMEM_IN,
+        out_shape=jax.ShapeDtypeStruct((peers,) + parts.shape[1:], parts.dtype),
+        compiler_params=pltpu.CompilerParams(vmem_limit_bytes=VMEM),
+        name="add_up",
+    )(parts)
 
 
 def finish_kernel(own_ref, keep_ref, one_ref, two_ref, table_ref, gain_ref, dk_ref, dv_ref, stage, sems):
@@ -347,7 +387,7 @@
         x = own_ref[:, at_k].astype(jnp.float32)
         inverse = lax.rsqrt(jnp.mean(x * x, axis=-1, keepdims=True) + norm_epsilon)
         dk = dk.astype(jnp.bfloat16).astype(jnp.float32)
-        e = unrotate(dk, table_ref[0], table_ref[3]) * gain
+        e = unrotate(dk, table_ref[0], table_ref[1]) * gain
         mean = jnp.mean(e * x, axis=-1, keepdims=True)
         stage[0, h] = (inverse * (e - x * (inverse * inverse * mean))).astype(jnp.bfloat16)
         stage[1, h] = dv.astype(jnp.bfloat16)
@@ -407,18 +447,17 @@
     base = me * ROWS
 
     own, gain = pack(key_raw[0], value_proj[0], query_gain, key_gain, shard[None], shards)
-    table, late = block_tables(turn_lengths[0], base[None])
+    table, rows, q_first, do_first = block_tables(turn_lengths[0], base[None], query_raw[0], out_grad[0])
     two = lax.ppermute(own, "seq", [(i, i + 2) for i in range(seq - 2)])
+    one = lax.ppermute(own, "seq", [(i, i + 1) for i in range(seq - 1)])
     gain = swap(gain, gain_groups())
-    one, gain, table = lax.optimization_barrier((jnp.where(me % 2 == 1, two, own), gain, table))
-    one = lax.ppermute(one, "seq", [(i, i ^ 1) for i in range(seq)])
-    q_grad, ret1, ret2, keep, parts = attend(query_raw[0], out_grad[0], own, one, two, (table, late, gain), 64)
+    q_grad, ret1, ret2, keep, parts = attend(q_first, do_first, query_raw[0], out_grad[0], own, one, two, (table, rows, gain), 64)
 
     back2 = lax.ppermute(ret2, "seq", [(i + 2, i) for i in range(seq - 2)])
-    part = jnp.sum(swap(parts, plane_groups()), axis=0)
+    part = add_up(swap(parts, plane_groups()), 8)
     ret1, part = lax.optimization_barrier((ret1, part))
     back1 = lax.ppermute(ret1, "seq", [(i + 1, i) for i in range(seq - 1)])
-    total = swap(jnp.broadcast_to(part[None], (8, 2, HEAD_DIM)), column_groups())
+    total = swap(part, column_groups())
     k_grad, v_grad = finish(own, keep, back1, back2, table, gain)
     total, k_grad, v_grad = lax.optimization_barrier((total, k_grad, v_grad))
     total = jnp.sum(total, axis=0)

time: 77.8 us -> 78.1 us (level)
  starting transfers between devices: 36 us -> 39.1 us
  waiting for transfers between devices: 22.9 us -> 21.5 us
    all_to_all x3, starting transfers between devices: 24.2 us -> 27.9 us  [swap(): lax.all_to_all(rows, AXES, 0, 0, axis_index_groups=groups, tiled=True)]
    ppermute x1, waiting for transfers between devices: 1.51 us -> 0.01 us  [local(): one = lax.ppermute(own, 'seq', [(i, i + 1) for i in range(seq - 1)])]
    ppermute x1, starting transfers between devices: 3.98 us -> 3.15 us  [local(): two = lax.ppermute(own, 'seq', [(i, i + 2) for i in range(seq - 2)])]
    pallas_call x2 -> x3, Pallas kernels: 11.4 us -> 10.7 us  [the longest x1 8.47 us: attend(): pl.pallas_call(attend_kernel, in_specs=[VMEM_IN] * 2 + [HBM_IN] * 2 + [VM...]
  transfers between devices with their start and end apart: 7 -> 7, of which waited for: 4 -> 3; matrix products, arithmetic and copies ran while one was open for 1% -> 0% of each run, Pallas kernels for 4% -> 5%
where the time goes in v3:
time: 78.1 us; the launch traced here: 76.9 us
  starting transfers between devices  39.1 us (50%)
  waiting for transfers between devices  21.5 us (28%)
  Pallas kernels  14.2 us (18%)
  local copies, waits for them, and re-layouts  1.27 us (2%)
    all_to_all x3, starting transfers between devices, swap(): lax.all_to_all(rows, AXES, 0, 0, axis_index_groups=groups, tiled=True)  27.9 us
    all_to_all x3, waiting for transfers between devices, swap(): lax.all_to_all(rows, AXES, 0, 0, axis_index_groups=groups, tiled=True)  16.2 us
    pallas_call x1, Pallas kernels, attend(): pl.pallas_call(attend_kernel, in_specs=[VMEM_IN] * 2 + [HBM_IN] * 2 + [VM...  8.47 us
    ppermute x1, waiting for transfers between devices, local(): back1 = lax.ppermute(ret1, 'seq', [(i + 1, i) for i in range(seq - 1)])  5.28 us
    ppermute x1, starting transfers between devices, local(): one = lax.ppermute(own, 'seq', [(i, i + 1) for i in range(seq - 1)])  4.51 us
    ppermute x1, starting transfers between devices, local(): two = lax.ppermute(own, 'seq', [(i, i + 2) for i in range(seq - 2)])  3.15 us
    ppermute x1, starting transfers between devices, local(): back1 = lax.ppermute(ret1, 'seq', [(i + 1, i) for i in range(seq - 1)])  2.29 us
    pallas_call x1, Pallas kernels, pack(): pl.pallas_call(pack_kernel, in_specs=[HBM_IN] * 4 + [SMEM_IN], out_specs=...  1.77 us
  transfers between devices with their start and end apart: 7, of which 3 were waited for; matrix products, arithmetic and copies ran while one was open for 0% of the time, Pallas kernels for 5%

profile of v3, /device:TPU:1, one launch (start us, length us, event | category | flops | bytes accessed | tf_op | source)
XLA Modules:
  0.0 76.9 jit_solution(595236707039765115)
XLA Ops:
  0.6 1.8 %pack.1 = (bf16[128,2048]{1,0:T(8,128)(2,1)S(1)}, f32[16,2,128]{2,1,0:T(2,128)}) custom-call(bf16[128,1024]{1,0:T(8,128)(2,1)} %bitcast.19, bf16[128,1024]{1,0:T(8,128)(2,1)} %bitcast.20, f32[8]{0:T(128)} %qg_in.1, f32[8]{0:T(128)} %kg_in.1, s32[1]{0:T(128)} %bitcast.6.shard_ref), custom_call_target="tpu_custom_call" | custom-call | tf_op jit(solution)/shard_map/pack/pallas_call | solution.py:159
  2.4 4.5 %collective-permute-start = (bf16[128,2048]{1,0:T(8,128)(2,1)S(1)}, bf16[128,2048]{1,0:T(8,128)(2,1)S(1)}, u32[]{:S(2)}, u32[]{:S(2)}) collective-permute-start(bf16[128,2048]{1,0:T(8,128)(2,1)S(1)} %get-tuple-element.25.own_ref), channel_id=1, source_target_pairs={{0,16},{16,32},{32,48},{48,64},{64,80},{80,96},{96,112},{112,128},... | collective-permute-start | bytes 1572872 | tf_op jit(solution)/shard_map/ppermute | solution.py:452
  6.9 3.1 %collective-permute-start.1 = (bf16[128,2048]{1,0:T(8,128)(2,1)S(1)}, bf16[128,2048]{1,0:T(8,128)(2,1)S(1)}, u32[]{:S(2)}, u32[]{:S(2)}) collective-permute-start(bf16[128,2048]{1,0:T(8,128)(2,1)S(1)} %get-tuple-element.25.own_ref), channel_id=1, source_target_pairs={{0,32},{16,48},{32,64},{48,80},{64,96},{80,112},{96,128},{112,144}... | collective-permute-start | bytes 1572872 | tf_op jit(solution)/shard_map/ppermute | solution.py:451
  10.1 13.8 %all-to-all-start = ((f32[16,2,128]{2,1,0:T(2,128)}), f32[16,2,128]{2,1,0:T(2,128)S(1)}, u32[]{:S(2)}, u32[]{:S(2)}) async-start(f32[16,2,128]{2,1,0:T(2,128)} %get-tuple-element.28), calls=%async_computation | async-start | bytes 32768 | tf_op jit(solution)/shard_map/all_to_all | solution.py:441
  23.9 0.0 copy-start
  23.9 0.0 copy-start.1
  23.9 0.6 copy-done
  24.6 0.0 copy-done.1
  24.6 1.6 %tables.1 = (f32[2,128,128]{2,1,0:T(8,128)S(1)}, f32[5,8,128]{2,1,0:T(8,128)S(1)}, bf16[128,1024]{1,0:T(8,128)(2,1)S(1)}, bf16[128,1024]{1,0:T(8,128)(2,1)S(1)}) custom-call(s32[48]{0:T(128)S(1)} %bitcast.14, s32[1]{0:T(128)} %bitcast.1.place_ref, f32[1,128]{1,0:T(1,128)S(1)} %copy-done.1, bf16[128,4096]{1,0:T(8,128)(2,1)} %bitcast.15, ...), custom_call_target="tpu_custom_call" | custom-call | tf_op jit(solution)/shard_map/tables/pallas_call | solution.py:114
  26.2 7.4 %all-to-all-done.gain_ref = f32[16,2,128]{2,1,0:T(2,128)S(1)} async-done(((f32[16,2,128]{2,1,0:T(2,128)}), f32[16,2,128]{2,1,0:T(2,128)S(1)}, u32[]{:S(2)}, u32[]{:S(2)}) %all-to-all-start) | async-done | bytes 16416 | tf_op jit(solution)/shard_map/all_to_all | solution.py:441
  33.6 0.0 collective-permute-done.one_ref
  33.6 0.0 collective-permute-done.1.two_ref
  33.6 8.5 %attend.1 = (bf16[128,4096]{1,0:T(8,128)(2,1)}, bf16[128,2048]{1,0:T(8,128)(2,1)}, bf16[128,2048]{1,0:T(8,128)(2,1)}, f32[128,2048]{1,0:T(8,128)S(1)}, f32[64,2,128]{2,1,0:T(2,128)}) custom-call(bf16[128,1024]{1,0:T(8,128)(2,1)S(1)} %get-tuple-element.23.q_first, bf16[128,1024]{1,0:T(8,128)(2,1)S(1)} %get-tuple-element.24.do_first, ...), custom_call_target="tpu_custom_call" | custom-call | tf_op jit(solution)/shard_map/attend/pallas_call | solution.py:338
  42.1 10.2 %all-to-all-start.1 = ((f32[64,2,128]{2,1,0:T(2,128)}), f32[64,2,128]{2,1,0:T(2,128)S(1)}, u32[]{:S(2)}, u32[]{:S(2)}) async-start(f32[64,2,128]{2,1,0:T(2,128)} %get-tuple-element.31), calls=%async_computation.1 | async-start | bytes 131072 | tf_op jit(solution)/shard_map/all_to_all | solution.py:441
  52.3 1.3 %collective-permute-start.3 = (bf16[128,2048]{1,0:T(8,128)(2,1)}, bf16[128,2048]{1,0:T(8,128)(2,1)S(1)}, u32[]{:S(2)}, u32[]{:S(2)}) collective-permute-start(bf16[128,2048]{1,0:T(8,128)(2,1)} %get-tuple-element.35), channel_id=1, source_target_pairs={{32,0},{48,16},{64,32},{80,48},{96,64},{112,80},{128,96},{144,112}... | collective-permute-start | bytes 1572872 | tf_op jit(solution)/shard_map/ppermute | solution.py:456
  53.6 8.8 %all-to-all-done.1.parts_ref = f32[64,2,128]{2,1,0:T(2,128)S(1)} async-done(((f32[64,2,128]{2,1,0:T(2,128)}), f32[64,2,128]{2,1,0:T(2,128)S(1)}, u32[]{:S(2)}, u32[]{:S(2)}) %all-to-all-start.1) | async-done | bytes 65568 | tf_op jit(solution)/shard_map/all_to_all | solution.py:441
  62.4 0.7 add_up.1
  63.1 2.3 %collective-permute-start.2 = (bf16[128,2048]{1,0:T(8,128)(2,1)}, bf16[128,2048]{1,0:T(8,128)(2,1)S(1)}, u32[]{:S(2)}, u32[]{:S(2)}) collective-permute-start(bf16[128,2048]{1,0:T(8,128)(2,1)} %get-tuple-element.34), channel_id=1, source_target_pairs={{16,0},{32,16},{48,32},{64,48},{80,64},{96,80},{112,96},{128,112},... | collective-permute-start | bytes 1572872 | tf_op jit(solution)/shard_map/ppermute | solution.py:459
  65.4 3.8 %all-to-all-start.2 = ((f32[8,2,128]{2,1,0:T(2,128)}), f32[8,2,128]{2,1,0:T(2,128)S(1)}, u32[]{:S(2)}, u32[]{:S(2)}) async-start(f32[8,2,128]{2,1,0:T(2,128)} %add_up.1), calls=%async_computation.2 | async-start | bytes 16384 | tf_op jit(solution)/shard_map/all_to_all | solution.py:441
  69.2 0.0 collective-permute-done.3.two_ref
  69.2 5.3 %collective-permute-done.2.one_ref = bf16[128,2048]{1,0:T(8,128)(2,1)S(1)} collective-permute-done((bf16[128,2048]{1,0:T(8,128)(2,1)}, bf16[128,2048]{1,0:T(8,128)(2,1)S(1)}, u32[]{:S(2)}, u32[]{:S(2)}) %collective-permute-start.2) | collective-permute-done | bytes 524320 | tf_op jit(solution)/shard_map/ppermute | solution.py:459
  74.5 1.8 %finish.1 = (bf16[128,1024]{1,0:T(8,128)(2,1)}, bf16[128,1024]{1,0:T(8,128)(2,1)}) custom-call(bf16[128,2048]{1,0:T(8,128)(2,1)S(1)} %get-tuple-element.25.own_ref, f32[128,2048]{1,0:T(8,128)S(1)} %get-tuple-element.33.keep_ref, bf16[128,2048]{1,0:T(8,128)(2,1)S(1)} %collective-permute-done.2.one_ref, bf16[128,2048]{1,0:T(8,128)(2,1)S(1)} %collective-permute-done.3.two_ref, ...), custom_call_target="tpu_custom_call" | custom-call | tf_op jit(solution)/shard_map/finish/pallas_call | solution.py:404
  76.2 0.0 all-to-all-done.2
  76.3 0.1 reshape.13
  76.3 0.5 dynamic-slice_bitcast_fusion
  (1 shorter events, 0.0 us)
Async XLA Ops:
  2.4 31.2 %collective-permute-start = (bf16[128,2048]{1,0:T(8,128)(2,1)S(1)}, bf16[128,2048]{1,0:T(8,128)(2,1)S(1)}, u32[]{:S(2)}, u32[]{:S(2)}) collective-permute-start(bf16[128,2048]{1,0:T(8,128)(2,1)S(1)} %get-tuple-element.25.own_ref), channel_id=1, source_target_pairs={{0,16},{16,32},{32,48},{48,64},{64,80},{80,96},{96,112},{112,128},... | collective-permute-start | bytes 1572872 | tf_op jit(solution)/shard_map/ppermute | solution.py:452
  6.9 26.7 %collective-permute-start.1 = (bf16[128,2048]{1,0:T(8,128)(2,1)S(1)}, bf16[128,2048]{1,0:T(8,128)(2,1)S(1)}, u32[]{:S(2)}, u32[]{:S(2)}) collective-permute-start(bf16[128,2048]{1,0:T(8,128)(2,1)S(1)} %get-tuple-element.25.own_ref), channel_id=1, source_target_pairs={{0,32},{16,48},{32,64},{48,80},{64,96},{80,112},{96,128},{112,144}... | collective-permute-start | bytes 1572872 | tf_op jit(solution)/shard_map/ppermute | solution.py:451
  10.1 23.5 %all-to-all-start = ((f32[16,2,128]{2,1,0:T(2,128)}), f32[16,2,128]{2,1,0:T(2,128)S(1)}, u32[]{:S(2)}, u32[]{:S(2)}) async-start(f32[16,2,128]{2,1,0:T(2,128)} %get-tuple-element.28), calls=%async_computation | async-start | bytes 32768 | tf_op jit(solution)/shard_map/all_to_all | solution.py:441
  23.9 0.7 copy-start
  23.9 0.7 copy-start.1
  42.1 20.3 %all-to-all-start.1 = ((f32[64,2,128]{2,1,0:T(2,128)}), f32[64,2,128]{2,1,0:T(2,128)S(1)}, u32[]{:S(2)}, u32[]{:S(2)}) async-start(f32[64,2,128]{2,1,0:T(2,128)} %get-tuple-element.31), calls=%async_computation.1 | async-start | bytes 131072 | tf_op jit(solution)/shard_map/all_to_all | solution.py:441
  52.3 16.9 %collective-permute-start.3 = (bf16[128,2048]{1,0:T(8,128)(2,1)}, bf16[128,2048]{1,0:T(8,128)(2,1)S(1)}, u32[]{:S(2)}, u32[]{:S(2)}) collective-permute-start(bf16[128,2048]{1,0:T(8,128)(2,1)} %get-tuple-element.35), channel_id=1, source_target_pairs={{32,0},{48,16},{64,32},{80,48},{96,64},{112,80},{128,96},{144,112}... | collective-permute-start | bytes 1572872 | tf_op jit(solution)/shard_map/ppermute | solution.py:456
  63.1 11.4 %collective-permute-start.2 = (bf16[128,2048]{1,0:T(8,128)(2,1)}, bf16[128,2048]{1,0:T(8,128)(2,1)S(1)}, u32[]{:S(2)}, u32[]{:S(2)}) collective-permute-start(bf16[128,2048]{1,0:T(8,128)(2,1)} %get-tuple-element.34), channel_id=1, source_target_pairs={{16,0},{32,16},{48,32},{64,48},{80,64},{96,80},{112,96},{128,112},... | collective-permute-start | bytes 1572872 | tf_op jit(solution)/shard_map/ppermute | solution.py:459
  65.4 10.9 %all-to-all-start.2 = ((f32[8,2,128]{2,1,0:T(2,128)}), f32[8,2,128]{2,1,0:T(2,128)S(1)}, u32[]{:S(2)}, u32[]{:S(2)}) async-start(f32[8,2,128]{2,1,0:T(2,128)} %add_up.1), calls=%async_computation.2 | async-start | bytes 16384 | tf_op jit(solution)/shard_map/all_to_all | solution.py:441

commit v4 on v3

--- a/solution.py
+++ b/solution.py
@@ -20,6 +20,7 @@
 OUT_HEADS = 2
 FIRST_HEADS = 2
 VMEM = 24 * 1024 * 1024
+FILL = 3
 
 NT = (((1,), (1,)), ((), ()))
 NN = (((1,), (0,)), ((), ()))
@@ -199,7 +200,7 @@
 
 def attend_kernel(
     q_first, do_first, q_in, do_in, own_ref, one_ref, two_ref, table_ref, row_ref, gain_ref,
-    dq_out, ret1_out, ret2_out, keep_ref, gains_ref, q_rest, do_rest, dq_ref, ret1_ref, ret2_ref, q_total, k_total, in_sems, sems,
+    dq_out, ret1_out, ret2_out, keep_ref, gains_out, gains_ref, q_rest, do_rest, dq_ref, ret1_ref, ret2_ref, q_total, k_total, in_sems, sems,
 ):
     group, pair = GROUP * HEAD_DIM, 2 * HEAD_DIM
 
@@ -327,10 +328,13 @@
     q_gain_grad = jnp.sum(q_total[...].T, axis=0, keepdims=True) / gain[0:1]
     k_gain_grad = jnp.sum(k_total[0] + roll_half(k_total[1]), axis=0, keepdims=True)
     gains_ref[...] = jnp.broadcast_to(over(q_gain_grad, k_gain_grad)[None], gains_ref.shape)
+    gains = pltpu.make_async_copy(gains_ref, gains_out, in_sems.at[2])
+    gains.start()
 
     for step in range(KV_HEADS // OUT_HEADS):
         for copy in out(step):
             copy.wait()
+    gains.wait()
 
 
 def attend(q_first, do_first, q, do, own, one, two, tables, peers):
@@ -338,15 +342,16 @@
     return pl.pallas_call(
         attend_kernel,
         in_specs=[VMEM_IN] * 2 + [HBM_IN] * 2 + [VMEM_IN] * 6,
-        out_specs=[HBM_IN] * 3 + [VMEM_IN] * 2,
+        out_specs=[HBM_IN] * 3 + [VMEM_IN, HBM_IN],
         out_shape=[
             pltpu.HBM(q.shape, jnp.bfloat16),
             pltpu.HBM(pair, jnp.bfloat16),
             pltpu.HBM(pair, jnp.bfloat16),
             pltpu.VMEM(pair, jnp.float32),
+            pltpu.HBM((peers, 2, HEAD_DIM), jnp.float32),
+        ],
+        scratch_shapes=[
             pltpu.VMEM((peers, 2, HEAD_DIM), jnp.float32),
-        ],
-        scratch_shapes=[
             pltpu.VMEM((ROWS, q.shape[1] - q_first.shape[1]), jnp.bfloat16),
             pltpu.VMEM((ROWS, q.shape[1] - q_first.shape[1]), jnp.bfloat16),
             pltpu.VMEM(q.shape, jnp.bfloat16),
@@ -354,12 +359,16 @@
             pltpu.VMEM(pair, jnp.bfloat16),
             pltpu.VMEM((HEAD_DIM, HEAD_DIM), jnp.float32),
             pltpu.VMEM((2, 8, HEAD_DIM), jnp.float32),
-            pltpu.SemaphoreType.DMA((2,)),
+            pltpu.SemaphoreType.DMA((3,)),
             pltpu.SemaphoreType.DMA((3, KV_HEADS // OUT_HEADS)),
         ],
         compiler_params=pltpu.CompilerParams(vmem_limit_bytes=VMEM),
         name="attend",
     )(q_first, do_first, *in_hbm(q, do), own, one, two, *tables)
+
+
+def hint(work):
+    return pl.CostEstimate(flops=work * 20_000_000_000, bytes_accessed=work * 40_000_000, transcendentals=0)
 
 
 def add_up_kernel(parts_ref, out_ref):
@@ -367,23 +376,85 @@
     out_ref[...] = jnp.broadcast_to(total, out_ref.shape)
 
 
-def add_up(parts, peers):
+def add_up(parts, peers, ahead):
     return pl.pallas_call(
         add_up_kernel,
         in_specs=[VMEM_IN],
         out_specs=VMEM_IN,
         out_shape=jax.ShapeDtypeStruct((peers,) + parts.shape[1:], parts.dtype),
         compiler_params=pltpu.CompilerParams(vmem_limit_bytes=VMEM),
+        cost_estimate=hint(ahead),
         name="add_up",
     )(parts)
 
 
-def finish_kernel(own_ref, keep_ref, one_ref, two_ref, table_ref, gain_ref, dk_ref, dv_ref, stage, sems):
+def parity_kernel(odd_ref, parts_ref, mask_ref):
+    mask_ref[...] = jnp.zeros_like(mask_ref) + odd_ref[0].astype(jnp.float32)
+
+
+def parity(odd, parts):
+    return pl.pallas_call(
+        parity_kernel,
+        in_specs=[SMEM_IN, HBM_IN],
+        out_specs=VMEM_IN,
+        out_shape=jax.ShapeDtypeStruct((8, HEAD_DIM), jnp.float32),
+        compiler_params=pltpu.CompilerParams(vmem_limit_bytes=VMEM),
+        cost_estimate=hint(FILL),
+        name="parity",
+    )(odd.astype(jnp.int32)[None], *in_hbm(parts))
+
+
+def merge_kernel(odd_ref, near_ref, ret_in, keep_in, far_out, keep_ref, ret_ref, far_ref, in_sems, sems):
+    pieces = sems.shape[0]
+    width = near_ref.shape[1] // pieces
+    odd = jnp.concatenate([odd_ref[0:1]] * (width // HEAD_DIM), axis=1)
+
+    def fetch(n):
+        at = pl.ds(n * width, width)
+        return pltpu.make_async_copy(ret_in.at[:, at], ret_ref.at[:, at], in_sems.at[n])
+
+    def out(n):
+        at = pl.ds(n * width, width)
+        return pltpu.make_async_copy(far_ref.at[:, at], far_out.at[:, at], sems.at[n])
+
+    for n in range(pieces):
+        fetch(n).start()
+    for n in range(pieces):
+        at = pl.ds(n * width, width)
+        near = near_ref[:, at].astype(jnp.float32)
+        fetch(n).wait()
+        far_ref[:, at] = (ret_ref[:, at] + near * odd).astype(jnp.bfloat16)
+        out(n).start()
+        keep_ref[:, at] = keep_in[:, at] + near * (1.0 - odd)
+    for n in range(pieces):
+        out(n).wait()
+
+
+def merge(odd, near, ret, keep):
+    pieces = 4
+    return pl.pallas_call(
+        merge_kernel,
+        in_specs=[VMEM_IN, VMEM_IN, HBM_IN, VMEM_IN],
+        out_specs=[HBM_IN, VMEM_IN],
+        out_shape=[pltpu.HBM(ret.shape, ret.dtype), pltpu.VMEM(keep.shape, keep.dtype)],
+        input_output_aliases={3: 1},
+        scratch_shapes=[
+            pltpu.VMEM(ret.shape, ret.dtype),
+            pltpu.VMEM(ret.shape, ret.dtype),
+            pltpu.SemaphoreType.DMA((pieces,)),
+            pltpu.SemaphoreType.DMA((pieces,)),
+        ],
+        compiler_params=pltpu.CompilerParams(vmem_limit_bytes=VMEM),
+        name="merge",
+    )(odd, near, *in_hbm(ret), keep)
+
+
+def finish_kernel(own_ref, keep_ref, far_ref, table_ref, gain_ref, dk_ref, dv_ref, stage, sems):
     gain = jnp.sum(gain_ref[...], axis=0)[1:2]
     copies = []
     for h in range(KV_HEADS):
         at_k, at_v = pl.ds(2 * h * HEAD_DIM, HEAD_DIM), pl.ds((2 * h + 1) * HEAD_DIM, HEAD_DIM)
-        dk, dv = (keep_ref[:, at] + one_ref[:, at] + two_ref[:, at] for at in (at_k, at_v))
+        dk, dv = (keep_ref[:, at] + far_ref[:, at] for at in (at_k, at_v))
         x = own_ref[:, at_k].astype(jnp.float32)
         inverse = lax.rsqrt(jnp.mean(x * x, axis=-1, keepdims=True) + norm_epsilon)
         dk = dk.astype(jnp.bfloat16).astype(jnp.float32)
@@ -399,11 +470,11 @@
         copy.wait()
 
 
-def finish(own, keep, one, two, table, gain):
+def finish(own, keep, far, table, gain):
     out = jax.ShapeDtypeStruct((ROWS, KV_HEADS * HEAD_DIM), jnp.bfloat16)
     return pl.pallas_call(
         finish_kernel,
-        in_specs=[VMEM_IN] * 6,
+        in_specs=[VMEM_IN] * 5,
         out_specs=[HBM_IN] * 2,
         out_shape=[out, out],
         scratch_shapes=[
@@ -412,7 +483,7 @@
         ],
         compiler_params=pltpu.CompilerParams(vmem_limit_bytes=VMEM),
         name="finish",
-    )(own, keep, one, two, table, gain)
+    )(own, keep, far, table, gain)
 
 
 AXES = ("seq", "fsdp")
@@ -445,20 +516,23 @@
     me, shard = lax.axis_index("seq"), lax.axis_index("fsdp")
     seq, shards = lax.axis_size("seq"), lax.axis_size("fsdp")
     base = me * ROWS
+    odd = me % 2 == 1
 
     own, gain = pack(key_raw[0], value_proj[0], query_gain, key_gain, shard[None], shards)
     table, rows, q_first, do_first = block_tables(turn_lengths[0], base[None], query_raw[0], out_grad[0])
     two = lax.ppermute(own, "seq", [(i, i + 2) for i in range(seq - 2)])
-    one = lax.ppermute(own, "seq", [(i, i + 1) for i in range(seq - 1)])
-    gain = swap(gain, gain_groups())
+    gain = add_up(swap(gain, gain_groups()), 1, 1)
+    one = jnp.where(odd, two, own)
+    one, table = lax.optimization_barrier((one, table))
+    one = lax.ppermute(one, "seq", [(i, i ^ 1) for i in range(seq)])
     q_grad, ret1, ret2, keep, parts = attend(q_first, do_first, query_raw[0], out_grad[0], own, one, two, (table, rows, gain), 64)
 
-    back2 = lax.ppermute(ret2, "seq", [(i + 2, i) for i in range(seq - 2)])
-    part = add_up(swap(parts, plane_groups()), 8)
-    ret1, part = lax.optimization_barrier((ret1, part))
-    back1 = lax.ppermute(ret1, "seq", [(i + 1, i) for i in range(seq - 1)])
+    near = lax.ppermute(ret1, "seq", [(i, i ^ 1) for i in range(seq)])
+    far, keep = merge(parity(odd, parts), near, ret2, keep)
+    far = lax.ppermute(far, "seq", [(i + 2, i) for i in range(seq - 2)])
+    part = add_up(swap(parts, plane_groups()), 8, 1)
     total = swap(part, column_groups())
-    k_grad, v_grad = finish(own, keep, back1, back2, table, gain)
+    k_grad, v_grad = finish(own, keep, far, table, gain)
     total, k_grad, v_grad = lax.optimization_barrier((total, k_grad, v_grad))
     total = jnp.sum(total, axis=0)
     shard_rows = total.reshape(2, shards, HEAD_DIM // shards)

time: 78.1 us -> 72.3 us (0.926)
  waiting for transfers between devices: 21.5 us -> 15.5 us
  Pallas kernels: 14.2 us -> 15.9 us
  starting transfers between devices: 39.1 us -> 38.2 us
    ppermute x3, waiting for transfers between devices: 5.28 us -> 1.24 us  [the longest x1 1.23 us: local(): far = lax.ppermute(far, 'seq', [(i + 2, i) for i in range(seq - 2)])]
    all_to_all x3, starting transfers between devices: 27.9 us -> 25.5 us  [swap(): lax.all_to_all(rows, AXES, 0, 0, axis_index_groups=groups, tiled=True)]
    pallas_call x1 -> x3, Pallas kernels: 1.75 us -> 3.73 us  [the longest x1 1.98 us: merge(): pl.pallas_call(merge_kernel, in_specs=[VMEM_IN, VMEM_IN, HBM_IN, VMEM_IN]...]
    all_to_all x3, waiting for transfers between devices: 16.2 us -> 14.3 us  [swap(): lax.all_to_all(rows, AXES, 0, 0, axis_index_groups=groups, tiled=True)]
    ppermute x1, starting transfers between devices: 3.15 us -> 3.98 us  [local(): two = lax.ppermute(own, 'seq', [(i, i + 2) for i in range(seq - 2)])]
  transfers between devices with their start and end apart: 7 -> 7, of which waited for: 3 -> 4; matrix products, arithmetic and copies ran while one was open for 0% -> 0% of each run, Pallas kernels for 5% -> 8%
where the time goes in v4:
time: 72.3 us; the launch traced here: 71.8 us
  starting transfers between devices  38.2 us (53%)
  Pallas kernels  15.9 us (22%)
  waiting for transfers between devices  15.5 us (21%)
  local copies, waits for them, and re-layouts  1.27 us (2%)
  between operations  0.79 us (1%)
    all_to_all x3, starting transfers between devices, swap(): lax.all_to_all(rows, AXES, 0, 0, axis_index_groups=groups, tiled=True)  25.5 us
    all_to_all x3, waiting for transfers between devices, swap(): lax.all_to_all(rows, AXES, 0, 0, axis_index_groups=groups, tiled=True)  14.3 us
    pallas_call x1, Pallas kernels, attend(): pl.pallas_call(attend_kernel, in_specs=[VMEM_IN] * 2 + [HBM_IN] * 2 + [VM...  8.14 us
    ppermute x1, starting transfers between devices, local(): near = lax.ppermute(ret1, 'seq', [(i, i ^ 1) for i in range(seq)])  4.28 us
    ppermute x1, starting transfers between devices, local(): two = lax.ppermute(own, 'seq', [(i, i + 2) for i in range(seq - 2)])  3.98 us
    ppermute x1, starting transfers between devices, local(): one = lax.ppermute(one, 'seq', [(i, i ^ 1) for i in range(seq)])  3.14 us
    pallas_call x1, Pallas kernels, merge(): pl.pallas_call(merge_kernel, in_specs=[VMEM_IN, VMEM_IN, HBM_IN, VMEM_IN]...  1.98 us
    pallas_call x1, Pallas kernels, pack(): pl.pallas_call(pack_kernel, in_specs=[HBM_IN] * 4 + [SMEM_IN], out_specs=...  1.77 us
  transfers between devices with their start and end apart: 7, of which 4 were waited for; matrix products, arithmetic and copies ran while one was open for 0% of the time, Pallas kernels for 8%

profile of v4, /device:TPU:1, one launch (start us, length us, event | category | flops | bytes accessed | tf_op | source)
XLA Modules:
  0.0 71.8 jit_solution(2653115039448042260)
XLA Ops:
  0.6 1.8 %pack.1 = (bf16[128,2048]{1,0:T(8,128)(2,1)S(1)}, f32[16,2,128]{2,1,0:T(2,128)}) custom-call(bf16[128,1024]{1,0:T(8,128)(2,1)} %bitcast.20, bf16[128,1024]{1,0:T(8,128)(2,1)} %bitcast.21, f32[8]{0:T(128)} %qg_in.1, f32[8]{0:T(128)} %kg_in.1, s32[1]{0:T(128)} %bitcast.6.shard_ref), custom_call_target="tpu_custom_call" | custom-call | tf_op jit(solution)/shard_map/pack/pallas_call | solution.py:160
  2.4 4.0 %collective-permute-start = (bf16[128,2048]{1,0:T(8,128)(2,1)S(1)}, bf16[128,2048]{1,0:T(8,128)(2,1)S(1)}, u32[]{:S(2)}, u32[]{:S(2)}) collective-permute-start(bf16[128,2048]{1,0:T(8,128)(2,1)S(1)} %get-tuple-element.27.own_ref), channel_id=1, source_target_pairs={{0,32},{16,48},{32,64},{48,80},{64,96},{80,112},{96,128},{112,144}... | collective-permute-start | bytes 1572872 | tf_op jit(solution)/shard_map/ppermute | solution.py:523
  6.4 13.8 %all-to-all-start = ((f32[16,2,128]{2,1,0:T(2,128)}), f32[16,2,128]{2,1,0:T(2,128)S(1)}, u32[]{:S(2)}, u32[]{:S(2)}) async-start(f32[16,2,128]{2,1,0:T(2,128)} %get-tuple-element.32), calls=%async_computation | async-start | bytes 32768 | tf_op jit(solution)/shard_map/all_to_all | solution.py:512
  20.2 0.0 copy-start
  20.3 0.0 copy-start.1
  20.3 0.6 copy-done
  20.9 0.0 copy-done.1
  20.9 1.6 %tables.1 = (f32[2,128,128]{2,1,0:T(8,128)S(1)}, f32[5,8,128]{2,1,0:T(8,128)S(1)}, bf16[128,1024]{1,0:T(8,128)(2,1)S(1)}, bf16[128,1024]{1,0:T(8,128)(2,1)S(1)}) custom-call(s32[48]{0:T(128)S(1)} %bitcast.15, s32[1]{0:T(128)} %bitcast.1.place_ref, f32[1,128]{1,0:T(1,128)S(1)} %copy-done.1, bf16[128,4096]{1,0:T(8,128)(2,1)} %bitcast.16, ...), custom_call_target="tpu_custom_call" | custom-call | tf_op jit(solution)/shard_map/tables/pallas_call | solution.py:115
  22.5 0.0 collective-permute-done.two_ref
  22.5 0.1 broadcast_select_fusion
  22.6 3.1 %collective-permute-start.1 = (bf16[128,2048]{1,0:T(8,128)(2,1)S(1)}, bf16[128,2048]{1,0:T(8,128)(2,1)S(1)}, u32[]{:S(2)}, u32[]{:S(2)}) collective-permute-start(bf16[128,2048]{1,0:T(8,128)(2,1)S(1)} %broadcast_select_fusion), channel_id=1, source_target_pairs={{0,16},{16,0},{32,48},{48,32},{64,80},{80,64},{96,112},{112,96},{1... | collective-permute-start | bytes 1572872 | tf_op jit(solution)/shard_map/ppermute | solution.py:527
  25.7 3.9 %all-to-all-done.parts_ref = f32[16,2,128]{2,1,0:T(2,128)S(1)} async-done(((f32[16,2,128]{2,1,0:T(2,128)}), f32[16,2,128]{2,1,0:T(2,128)S(1)}, u32[]{:S(2)}, u32[]{:S(2)}) %all-to-all-start) | async-done | bytes 16416 | tf_op jit(solution)/shard_map/all_to_all | solution.py:512
  29.7 0.0 collective-permute-done.1.one_ref
  29.7 8.1 %attend.1 = (bf16[128,4096]{1,0:T(8,128)(2,1)}, bf16[128,2048]{1,0:T(8,128)(2,1)}, bf16[128,2048]{1,0:T(8,128)(2,1)}, f32[128,2048]{1,0:T(8,128)S(1)}, f32[64,2,128]{2,1,0:T(2,128)}) custom-call(bf16[128,1024]{1,0:T(8,128)(2,1)S(1)} %get-tuple-element.25.q_first, bf16[128,1024]{1,0:T(8,128)(2,1)S(1)} %get-tuple-element.26.do_first, ...), custom_call_target="tpu_custom_call" | custom-call | tf_op jit(solution)/shard_map/attend/pallas_call | solution.py:342
  37.8 4.3 %collective-permute-start.2 = (bf16[128,2048]{1,0:T(8,128)(2,1)}, bf16[128,2048]{1,0:T(8,128)(2,1)S(1)}, u32[]{:S(2)}, u32[]{:S(2)}) collective-permute-start(bf16[128,2048]{1,0:T(8,128)(2,1)} %get-tuple-element.35), channel_id=1, source_target_pairs={{0,16},{16,0},{32,48},{48,32},{64,80},{80,64},{96,112},{112,96},{1... | collective-permute-start | bytes 1572872 | tf_op jit(solution)/shard_map/ppermute | solution.py:530
  42.1 6.3 %all-to-all-start.1 = ((f32[64,2,128]{2,1,0:T(2,128)}), f32[64,2,128]{2,1,0:T(2,128)S(1)}, u32[]{:S(2)}, u32[]{:S(2)}) async-start(f32[64,2,128]{2,1,0:T(2,128)} %get-tuple-element.34.parts_ref), calls=%async_computation.1 | async-start | bytes 131072 | tf_op jit(solution)/shard_map/all_to_all | solution.py:512
  48.5 0.0 collective-permute-done.2.near_ref
  48.5 2.0 %merge.1 = (bf16[128,2048]{1,0:T(8,128)(2,1)}, f32[128,2048]{1,0:T(8,128)S(1)}) custom-call(f32[8,128]{1,0:T(8,128)S(1)} %parity.1.odd_ref, bf16[128,2048]{1,0:T(8,128)(2,1)S(1)} %collective-permute-done.2.near_ref, bf16[128,2048]{1,0:T(8,128)(2,1)} %get-tuple-element.36.ret_in, ...), custom_call_target="tpu_custom_call", output_to_operand_aliasing={{1}: (3, {})} | custom-call | tf_op jit(solution)/shard_map/merge/pallas_call | solution.py:435
  50.4 1.3 %collective-permute-start.3 = (bf16[128,2048]{1,0:T(8,128)(2,1)}, bf16[128,2048]{1,0:T(8,128)(2,1)S(1)}, u32[]{:S(2)}, u32[]{:S(2)}) collective-permute-start(bf16[128,2048]{1,0:T(8,128)(2,1)} %get-tuple-element.39), channel_id=1, source_target_pairs={{32,0},{48,16},{64,32},{80,48},{96,64},{112,80},{128,96},{144,112}... | collective-permute-start | bytes 1572872 | tf_op jit(solution)/shard_map/ppermute | solution.py:532
  51.7 6.8 %all-to-all-done.1.parts_ref = f32[64,2,128]{2,1,0:T(2,128)S(1)} async-done(((f32[64,2,128]{2,1,0:T(2,128)}), f32[64,2,128]{2,1,0:T(2,128)S(1)}, u32[]{:S(2)}, u32[]{:S(2)}) %all-to-all-start.1) | async-done | bytes 65568 | tf_op jit(solution)/shard_map/all_to_all | solution.py:512
  58.5 0.7 add_up.3
  59.2 5.4 %all-to-all-start.2 = ((f32[8,2,128]{2,1,0:T(2,128)}), f32[8,2,128]{2,1,0:T(2,128)S(1)}, u32[]{:S(2)}, u32[]{:S(2)}) async-start(f32[8,2,128]{2,1,0:T(2,128)} %add_up.3), calls=%async_computation.2 | async-start | bytes 16384 | tf_op jit(solution)/shard_map/all_to_all | solution.py:512
  64.6 1.2 %collective-permute-done.3.far_ref = bf16[128,2048]{1,0:T(8,128)(2,1)S(1)} collective-permute-done((bf16[128,2048]{1,0:T(8,128)(2,1)}, bf16[128,2048]{1,0:T(8,128)(2,1)S(1)}, u32[]{:S(2)}, u32[]{:S(2)}) %collective-permute-start.3) | collective-permute-done | bytes 524320 | tf_op jit(solution)/shard_map/ppermute | solution.py:532
  65.8 1.7 %finish.1 = (bf16[128,1024]{1,0:T(8,128)(2,1)}, bf16[128,1024]{1,0:T(8,128)(2,1)}) custom-call(bf16[128,2048]{1,0:T(8,128)(2,1)S(1)} %get-tuple-element.27.own_ref, f32[128,2048]{1,0:T(8,128)S(1)} %get-tuple-element.38.keep_ref, bf16[128,2048]{1,0:T(8,128)(2,1)S(1)} %collective-permute-done.3.far_ref, f32[2,128,128]{2,1,0:T(8,128)S(1)} %get-tuple-element.30.table_ref, ...), custom_call_target="tpu_custom_call" | custom-call | tf_op jit(solution)/shard_map/finish/pallas_call | solution.py:475
  67.5 3.6 %all-to-all-done.2 = f32[8,2,128]{2,1,0:T(2,128)S(1)} async-done(((f32[8,2,128]{2,1,0:T(2,128)}), f32[8,2,128]{2,1,0:T(2,128)S(1)}, u32[]{:S(2)}, u32[]{:S(2)}) %all-to-all-start.2) | async-done | bytes 8224 | tf_op jit(solution)/shard_map/all_to_all | solution.py:512
  71.2 0.1 reshape.13
  71.2 0.5 dynamic-slice_bitcast_fusion
  (3 shorter events, 0.0 us)
Async XLA Ops:
  2.4 20.1 %collective-permute-start = (bf16[128,2048]{1,0:T(8,128)(2,1)S(1)}, bf16[128,2048]{1,0:T(8,128)(2,1)S(1)}, u32[]{:S(2)}, u32[]{:S(2)}) collective-permute-start(bf16[128,2048]{1,0:T(8,128)(2,1)S(1)} %get-tuple-element.27.own_ref), channel_id=1, source_target_pairs={{0,32},{16,48},{32,64},{48,80},{64,96},{80,112},{96,128},{112,144}... | collective-permute-start | bytes 1572872 | tf_op jit(solution)/shard_map/ppermute | solution.py:523
  6.4 23.3 %all-to-all-start = ((f32[16,2,128]{2,1,0:T(2,128)}), f32[16,2,128]{2,1,0:T(2,128)S(1)}, u32[]{:S(2)}, u32[]{:S(2)}) async-start(f32[16,2,128]{2,1,0:T(2,128)} %get-tuple-element.32), calls=%async_computation | async-start | bytes 32768 | tf_op jit(solution)/shard_map/all_to_all | solution.py:512
  20.2 0.7 copy-start
  20.3 0.7 copy-start.1
  22.6 7.1 %collective-permute-start.1 = (bf16[128,2048]{1,0:T(8,128)(2,1)S(1)}, bf16[128,2048]{1,0:T(8,128)(2,1)S(1)}, u32[]{:S(2)}, u32[]{:S(2)}) collective-permute-start(bf16[128,2048]{1,0:T(8,128)(2,1)S(1)} %broadcast_select_fusion), channel_id=1, source_target_pairs={{0,16},{16,0},{32,48},{48,32},{64,80},{80,64},{96,112},{112,96},{1... | collective-permute-start | bytes 1572872 | tf_op jit(solution)/shard_map/ppermute | solution.py:527
  37.8 10.6 %collective-permute-start.2 = (bf16[128,2048]{1,0:T(8,128)(2,1)}, bf16[128,2048]{1,0:T(8,128)(2,1)S(1)}, u32[]{:S(2)}, u32[]{:S(2)}) collective-permute-start(bf16[128,2048]{1,0:T(8,128)(2,1)} %get-tuple-element.35), channel_id=1, source_target_pairs={{0,16},{16,0},{32,48},{48,32},{64,80},{80,64},{96,112},{112,96},{1... | collective-permute-start | bytes 1572872 | tf_op jit(solution)/shard_map/ppermute | solution.py:530
  42.1 16.4 %all-to-all-start.1 = ((f32[64,2,128]{2,1,0:T(2,128)}), f32[64,2,128]{2,1,0:T(2,128)S(1)}, u32[]{:S(2)}, u32[]{:S(2)}) async-start(f32[64,2,128]{2,1,0:T(2,128)} %get-tuple-element.34.parts_ref), calls=%async_computation.1 | async-start | bytes 131072 | tf_op jit(solution)/shard_map/all_to_all | solution.py:512
  50.4 15.3 %collective-permute-start.3 = (bf16[128,2048]{1,0:T(8,128)(2,1)}, bf16[128,2048]{1,0:T(8,128)(2,1)S(1)}, u32[]{:S(2)}, u32[]{:S(2)}) collective-permute-start(bf16[128,2048]{1,0:T(8,128)(2,1)} %get-tuple-element.39), channel_id=1, source_target_pairs={{32,0},{48,16},{64,32},{80,48},{96,64},{112,80},{128,96},{144,112}... | collective-permute-start | bytes 1572872 | tf_op jit(solution)/shard_map/ppermute | solution.py:532
  59.2 11.9 %all-to-all-start.2 = ((f32[8,2,128]{2,1,0:T(2,128)}), f32[8,2,128]{2,1,0:T(2,128)S(1)}, u32[]{:S(2)}, u32[]{:S(2)}) async-start(f32[8,2,128]{2,1,0:T(2,128)} %add_up.3), calls=%async_computation.2 | async-start | bytes 16384 | tf_op jit(solution)/shard_map/all_to_all | solution.py:512

commit v5 on v4

--- a/solution.py
+++ b/solution.py
@@ -20,7 +20,6 @@
 OUT_HEADS = 2
 FIRST_HEADS = 2
 VMEM = 24 * 1024 * 1024
-FILL = 3
 
 NT = (((1,), (1,)), ((), ()))
 NN = (((1,), (0,)), ((), ()))
@@ -33,13 +32,6 @@
 
 def roll_half(x):
     return pltpu.roll(x, HALF, axis=1)
-
-
-def forward_norm(raw, gain, cosine, sine):
-    x = raw.astype(jnp.float32)
-    inverse = lax.rsqrt(jnp.mean(x * x, axis=-1, keepdims=True) + norm_epsilon)
-    y = x * inverse * gain
-    return x, inverse, (y * cosine + roll_half(y) * sine).astype(jnp.bfloat16)
 
 
 def unrotate(grad, cosine, sine):
@@ -128,7 +120,7 @@
     )(lengths, place, freqs, *in_hbm(q, do))
 
 
-def pack_kernel(k_ref, v_ref, qg_in, kg_in, shard_ref, own_ref, gain_ref, qg_ref, kg_ref, sems):
+def pack_kernel(k_ref, v_ref, qg_in, kg_in, shard_ref, own_ref, gain_out, gain_ref, qg_ref, kg_ref, sems):
     copies = [
         pltpu.make_async_copy(
             ref.at[:, pl.ds(h * HEAD_DIM, HEAD_DIM)],
@@ -152,6 +144,8 @@
     for i in range(width):
         both = jnp.where(lane == i, jnp.where(row == 0, qg_ref[i], kg_ref[i]), both)
     gain_ref[...] = jnp.broadcast_to(both[None], gain_ref.shape)
+    copies.append(pltpu.make_async_copy(gain_ref, gain_out, sems.at[2 * KV_HEADS + 2]))
+    copies[-1].start()
     for copy in copies:
         copy.wait()
 
@@ -160,15 +154,16 @@
     return pl.pallas_call(
         pack_kernel,
         in_specs=[HBM_IN] * 4 + [SMEM_IN],
-        out_specs=[VMEM_IN, VMEM_IN],
+        out_specs=[VMEM_IN, HBM_IN],
         out_shape=[
             pltpu.VMEM((ROWS, 2 * KV_HEADS * HEAD_DIM), jnp.bfloat16),
+            pltpu.HBM((shards, 2, HEAD_DIM), jnp.float32),
+        ],
+        scratch_shapes=[
             pltpu.VMEM((shards, 2, HEAD_DIM), jnp.float32),
-        ],
-        scratch_shapes=[
             pltpu.SMEM(q_gain.shape, jnp.float32),
             pltpu.SMEM(k_gain.shape, jnp.float32),
-            pltpu.SemaphoreType.DMA((2 * KV_HEADS + 2,)),
+            pltpu.SemaphoreType.DMA((2 * KV_HEADS + 3,)),
         ],
         compiler_params=pltpu.CompilerParams(vmem_limit_bytes=VMEM),
         name="pack",
@@ -388,34 +383,14 @@
     )(parts)
 
 
-def parity_kernel(odd_ref, parts_ref, mask_ref):
-    mask_ref[...] = jnp.zeros_like(mask_ref) + odd_ref[0].astype(jnp.float32)
-
-
-def parity(odd, parts):
-    return pl.pallas_call(
-        parity_kernel,
-        in_specs=[SMEM_IN, HBM_IN],
-        out_specs=VMEM_IN,
-        out_shape=jax.ShapeDtypeStruct((8, HEAD_DIM), jnp.float32),
-        compiler_params=pltpu.CompilerParams(vmem_limit_bytes=VMEM),
-        cost_estimate=hint(FILL),
-        name="parity",
-    )(odd.astype(jnp.int32)[None], *in_hbm(parts))
-
-
-def merge_kernel(odd_ref, near_ref, ret_in, keep_in, far_out, keep_ref, ret_ref, far_ref, in_sems, sems):
+def merge_kernel(odd_ref, near_ref, ret_in, keep_in, far_ref, keep_ref, ret_ref, sems):
     pieces = sems.shape[0]
     width = near_ref.shape[1] // pieces
-    odd = jnp.concatenate([odd_ref[0:1]] * (width // HEAD_DIM), axis=1)
+    odd = odd_ref[0].astype(jnp.float32)
 
     def fetch(n):
         at = pl.ds(n * width, width)
-        return pltpu.make_async_copy(ret_in.at[:, at], ret_ref.at[:, at], in_sems.at[n])
-
-    def out(n):
-        at = pl.ds(n * width, width)
-        return pltpu.make_async_copy(far_ref.at[:, at], far_out.at[:, at], sems.at[n])
+        return pltpu.make_async_copy(ret_in.at[:, at], ret_ref.at[:, at], sems.at[n])
 
     for n in range(pieces):
         fetch(n).start()
@@ -424,29 +399,24 @@
         near = near_ref[:, at].astype(jnp.float32)
         fetch(n).wait()
         far_ref[:, at] = (ret_ref[:, at] + near * odd).astype(jnp.bfloat16)
-        out(n).start()
         keep_ref[:, at] = keep_in[:, at] + near * (1.0 - odd)
-    for n in range(pieces):
-        out(n).wait()
 
 
 def merge(odd, near, ret, keep):
     pieces = 4
     return pl.pallas_call(
         merge_kernel,
-        in_specs=[VMEM_IN, VMEM_IN, HBM_IN, VMEM_IN],
-        out_specs=[HBM_IN, VMEM_IN],
-        out_shape=[pltpu.HBM(ret.shape, ret.dtype), pltpu.VMEM(keep.shape, keep.dtype)],
+        in_specs=[SMEM_IN, VMEM_IN, HBM_IN, VMEM_IN],
+        out_specs=[VMEM_IN] * 2,
+        out_shape=[pltpu.VMEM(ret.shape, ret.dtype), pltpu.VMEM(keep.shape, keep.dtype)],
         input_output_aliases={3: 1},
         scratch_shapes=[
             pltpu.VMEM(ret.shape, ret.dtype),
-            pltpu.VMEM(ret.shape, ret.dtype),
-            pltpu.SemaphoreType.DMA((pieces,)),
             pltpu.SemaphoreType.DMA((pieces,)),
         ],
         compiler_params=pltpu.CompilerParams(vmem_limit_bytes=VMEM),
         name="merge",
-    )(odd, near, *in_hbm(ret), keep)
+    )(odd.astype(jnp.int32)[None], near, *in_hbm(ret), keep)
 
 
 def finish_kernel(own_ref, keep_ref, far_ref, table_ref, gain_ref, dk_ref, dv_ref, stage, sems):
@@ -528,7 +498,7 @@
     q_grad, ret1, ret2, keep, parts = attend(q_first, do_first, query_raw[0], out_grad[0], own, one, two, (table, rows, gain), 64)
 
     near = lax.ppermute(ret1, "seq", [(i, i ^ 1) for i in range(seq)])
-    far, keep = merge(parity(odd, parts), near, ret2, keep)
+    far, keep = merge(odd, near, ret2, keep)
     far = lax.ppermute(far, "seq", [(i + 2, i) for i in range(seq - 2)])
     part = add_up(swap(parts, plane_groups()), 8, 1)
     total = swap(part, column_groups())

time: 72.3 us -> 72 us (level)
  Pallas kernels: 15.9 us -> 14.9 us
    all_to_all x3, waiting for transfers between devices: 14.3 us -> 15.7 us  [swap(): lax.all_to_all(rows, AXES, 0, 0, axis_index_groups=groups, tiled=True)]
    pallas_call x2 -> x1, Pallas kernels: 1.98 us -> 1.33 us  [merge(): pl.pallas_call(merge_kernel, in_specs=[SMEM_IN, VMEM_IN, HBM_IN, VMEM_IN]...]
  transfers between devices with their start and end apart: 7 -> 7, of which waited for: 4 -> 4; matrix products, arithmetic and copies ran while one was open for 0% -> 0% of each run, Pallas kernels for 8% -> 7%
where the time goes in v5:
time: 72 us; the launch traced here: 71.5 us
  starting transfers between devices  38.2 us (53%)
  waiting for transfers between devices  16.2 us (22%)
  Pallas kernels  14.9 us (21%)
  local copies, waits for them, and re-layouts  1.27 us (2%)
  between operations  0.79 us (1%)
    all_to_all x3, starting transfers between devices, swap(): lax.all_to_all(rows, AXES, 0, 0, axis_index_groups=groups, tiled=True)  25.5 us
    all_to_all x3, waiting for transfers between devices, swap(): lax.all_to_all(rows, AXES, 0, 0, axis_index_groups=groups, tiled=True)  15.7 us
    pallas_call x1, Pallas kernels, attend(): pl.pallas_call(attend_kernel, in_specs=[VMEM_IN] * 2 + [HBM_IN] * 2 + [VM...  8.14 us
    ppermute x1, starting transfers between devices, local(): near = lax.ppermute(ret1, 'seq', [(i, i ^ 1) for i in range(seq)])  4.29 us
    ppermute x1, starting transfers between devices, local(): two = lax.ppermute(own, 'seq', [(i, i + 2) for i in range(seq - 2)])  3.98 us
    ppermute x1, starting transfers between devices, local(): one = lax.ppermute(one, 'seq', [(i, i ^ 1) for i in range(seq)])  3.14 us
    pallas_call x1, Pallas kernels, finish(): pl.pallas_call(finish_kernel, in_specs=[VMEM_IN] * 5, out_specs=[HBM_IN]...  1.75 us
    pallas_call x1, Pallas kernels, block_tables(): pl.pallas_call(table_kernel, in_specs=[SMEM_IN, SMEM_IN, VMEM_IN, HBM_IN,...  1.59 us
  transfers between devices with their start and end apart: 7, of which 4 were waited for; matrix products, arithmetic and copies ran while one was open for 0% of the time, Pallas kernels for 7%

profile of v5, /device:TPU:1, one launch (start us, length us, event | category | flops | bytes accessed | tf_op | source)
XLA Modules:
  0.0 71.5 jit_solution(2859990827247485623)
XLA Ops:
  0.6 1.5 %pack.1 = (bf16[128,2048]{1,0:T(8,128)(2,1)S(1)}, f32[16,2,128]{2,1,0:T(2,128)}) custom-call(bf16[128,1024]{1,0:T(8,128)(2,1)} %bitcast.20, bf16[128,1024]{1,0:T(8,128)(2,1)} %bitcast.21, f32[8]{0:T(128)} %qg_in.1, f32[8]{0:T(128)} %kg_in.1, s32[1]{0:T(128)} %bitcast.6.shard_ref), custom_call_target="tpu_custom_call" | custom-call | tf_op jit(solution)/shard_map/pack/pallas_call | solution.py:154
  2.1 4.0 %collective-permute-start = (bf16[128,2048]{1,0:T(8,128)(2,1)S(1)}, bf16[128,2048]{1,0:T(8,128)(2,1)S(1)}, u32[]{:S(2)}, u32[]{:S(2)}) collective-permute-start(bf16[128,2048]{1,0:T(8,128)(2,1)S(1)} %get-tuple-element.27.own_ref), channel_id=1, source_target_pairs={{0,32},{16,48},{32,64},{48,80},{64,96},{80,112},{96,128},{112,144}... | collective-permute-start | bytes 1572872 | tf_op jit(solution)/shard_map/ppermute | solution.py:493
  6.1 13.8 %all-to-all-start = ((f32[16,2,128]{2,1,0:T(2,128)}), f32[16,2,128]{2,1,0:T(2,128)S(1)}, u32[]{:S(2)}, u32[]{:S(2)}) async-start(f32[16,2,128]{2,1,0:T(2,128)} %get-tuple-element.32), calls=%async_computation | async-start | bytes 32768 | tf_op jit(solution)/shard_map/all_to_all | solution.py:482
  19.9 0.0 copy-start
  19.9 0.0 copy-start.1
  19.9 0.6 copy-done
  20.6 0.0 copy-done.1
  20.6 1.6 %tables.1 = (f32[2,128,128]{2,1,0:T(8,128)S(1)}, f32[5,8,128]{2,1,0:T(8,128)S(1)}, bf16[128,1024]{1,0:T(8,128)(2,1)S(1)}, bf16[128,1024]{1,0:T(8,128)(2,1)S(1)}) custom-call(s32[48]{0:T(128)S(1)} %bitcast.15, s32[1]{0:T(128)} %bitcast.1.place_ref, f32[1,128]{1,0:T(1,128)S(1)} %copy-done.1, bf16[128,4096]{1,0:T(8,128)(2,1)} %bitcast.16, ...), custom_call_target="tpu_custom_call" | custom-call | tf_op jit(solution)/shard_map/tables/pallas_call | solution.py:107
  22.2 0.0 collective-permute-done.two_ref
  22.2 0.1 broadcast_select_fusion
  22.3 3.1 %collective-permute-start.1 = (bf16[128,2048]{1,0:T(8,128)(2,1)S(1)}, bf16[128,2048]{1,0:T(8,128)(2,1)S(1)}, u32[]{:S(2)}, u32[]{:S(2)}) collective-permute-start(bf16[128,2048]{1,0:T(8,128)(2,1)S(1)} %broadcast_select_fusion), channel_id=1, source_target_pairs={{0,16},{16,0},{32,48},{48,32},{64,80},{80,64},{96,112},{112,96},{1... | collective-permute-start | bytes 1572872 | tf_op jit(solution)/shard_map/ppermute | solution.py:497
  25.4 3.9 %all-to-all-done.parts_ref = f32[16,2,128]{2,1,0:T(2,128)S(1)} async-done(((f32[16,2,128]{2,1,0:T(2,128)}), f32[16,2,128]{2,1,0:T(2,128)S(1)}, u32[]{:S(2)}, u32[]{:S(2)}) %all-to-all-start) | async-done | bytes 16416 | tf_op jit(solution)/shard_map/all_to_all | solution.py:482
  29.4 0.0 collective-permute-done.1.one_ref
  29.4 8.1 %attend.1 = (bf16[128,4096]{1,0:T(8,128)(2,1)}, bf16[128,2048]{1,0:T(8,128)(2,1)}, bf16[128,2048]{1,0:T(8,128)(2,1)}, f32[128,2048]{1,0:T(8,128)S(1)}, f32[64,2,128]{2,1,0:T(2,128)}) custom-call(bf16[128,1024]{1,0:T(8,128)(2,1)S(1)} %get-tuple-element.25.q_first, bf16[128,1024]{1,0:T(8,128)(2,1)S(1)} %get-tuple-element.26.do_first, ...), custom_call_target="tpu_custom_call" | custom-call | tf_op jit(solution)/shard_map/attend/pallas_call | solution.py:337
  37.5 4.3 %collective-permute-start.2 = (bf16[128,2048]{1,0:T(8,128)(2,1)}, bf16[128,2048]{1,0:T(8,128)(2,1)S(1)}, u32[]{:S(2)}, u32[]{:S(2)}) collective-permute-start(bf16[128,2048]{1,0:T(8,128)(2,1)} %get-tuple-element.35), channel_id=1, source_target_pairs={{0,16},{16,0},{32,48},{48,32},{64,80},{80,64},{96,112},{112,96},{1... | collective-permute-start | bytes 1572872 | tf_op jit(solution)/shard_map/ppermute | solution.py:500
  41.8 6.3 %all-to-all-start.1 = ((f32[64,2,128]{2,1,0:T(2,128)}), f32[64,2,128]{2,1,0:T(2,128)S(1)}, u32[]{:S(2)}, u32[]{:S(2)}) async-start(f32[64,2,128]{2,1,0:T(2,128)} %get-tuple-element.34), calls=%async_computation.1 | async-start | bytes 131072 | tf_op jit(solution)/shard_map/all_to_all | solution.py:482
  48.1 0.0 collective-permute-done.2.near_ref
  48.1 1.3 %merge.1 = (bf16[128,2048]{1,0:T(8,128)(2,1)S(1)}, f32[128,2048]{1,0:T(8,128)S(1)}) custom-call(s32[1]{0:T(128)} %bitcast.8.odd_ref, bf16[128,2048]{1,0:T(8,128)(2,1)S(1)} %collective-permute-done.2.near_ref, bf16[128,2048]{1,0:T(8,128)(2,1)} %get-tuple-element.36.ret_in, f32[128,2048]{1,0:T(8,128)S(1)} %get-tuple-element.37.keep_in), custom_call_target="tpu_custom_call", output_to_operand_aliasing={{1}: (3, {})} | custom-call | tf_op jit(solution)/shard_map/merge/pallas_call | solution.py:407
  49.5 1.3 %collective-permute-start.3 = (bf16[128,2048]{1,0:T(8,128)(2,1)S(1)}, bf16[128,2048]{1,0:T(8,128)(2,1)S(1)}, u32[]{:S(2)}, u32[]{:S(2)}) collective-permute-start(bf16[128,2048]{1,0:T(8,128)(2,1)S(1)} %get-tuple-element.39), channel_id=1, source_target_pairs={{32,0},{48,16},{64,32},{80,48},{96,64},{112,80},{128,96},{144,112}... | collective-permute-start | bytes 1572872 | tf_op jit(solution)/shard_map/ppermute | solution.py:502
  50.8 7.4 %all-to-all-done.1.parts_ref = f32[64,2,128]{2,1,0:T(2,128)S(1)} async-done(((f32[64,2,128]{2,1,0:T(2,128)}), f32[64,2,128]{2,1,0:T(2,128)S(1)}, u32[]{:S(2)}, u32[]{:S(2)}) %all-to-all-start.1) | async-done | bytes 65568 | tf_op jit(solution)/shard_map/all_to_all | solution.py:482
  58.2 0.7 add_up.3
  58.9 5.4 %all-to-all-start.2 = ((f32[8,2,128]{2,1,0:T(2,128)}), f32[8,2,128]{2,1,0:T(2,128)S(1)}, u32[]{:S(2)}, u32[]{:S(2)}) async-start(f32[8,2,128]{2,1,0:T(2,128)} %add_up.3), calls=%async_computation.2 | async-start | bytes 16384 | tf_op jit(solution)/shard_map/all_to_all | solution.py:482
  64.2 0.5 collective-permute-done.3.far_ref
  64.8 1.7 %finish.1 = (bf16[128,1024]{1,0:T(8,128)(2,1)}, bf16[128,1024]{1,0:T(8,128)(2,1)}) custom-call(bf16[128,2048]{1,0:T(8,128)(2,1)S(1)} %get-tuple-element.27.own_ref, f32[128,2048]{1,0:T(8,128)S(1)} %get-tuple-element.38.keep_ref, bf16[128,2048]{1,0:T(8,128)(2,1)S(1)} %collective-permute-done.3.far_ref, f32[2,128,128]{2,1,0:T(8,128)S(1)} %get-tuple-element.30.table_ref, ...), custom_call_target="tpu_custom_call" | custom-call | tf_op jit(solution)/shard_map/finish/pallas_call | solution.py:445
  66.5 4.3 %all-to-all-done.2 = f32[8,2,128]{2,1,0:T(2,128)S(1)} async-done(((f32[8,2,128]{2,1,0:T(2,128)}), f32[8,2,128]{2,1,0:T(2,128)S(1)}, u32[]{:S(2)}, u32[]{:S(2)}) %all-to-all-start.2) | async-done | bytes 8224 | tf_op jit(solution)/shard_map/all_to_all | solution.py:482
  70.8 0.1 reshape.13
  70.9 0.5 dynamic-slice_bitcast_fusion
  (2 shorter events, 0.0 us)
Async XLA Ops:
  2.1 20.1 %collective-permute-start = (bf16[128,2048]{1,0:T(8,128)(2,1)S(1)}, bf16[128,2048]{1,0:T(8,128)(2,1)S(1)}, u32[]{:S(2)}, u32[]{:S(2)}) collective-permute-start(bf16[128,2048]{1,0:T(8,128)(2,1)S(1)} %get-tuple-element.27.own_ref), channel_id=1, source_target_pairs={{0,32},{16,48},{32,64},{48,80},{64,96},{80,112},{96,128},{112,144}... | collective-permute-start | bytes 1572872 | tf_op jit(solution)/shard_map/ppermute | solution.py:493
  6.1 23.3 %all-to-all-start = ((f32[16,2,128]{2,1,0:T(2,128)}), f32[16,2,128]{2,1,0:T(2,128)S(1)}, u32[]{:S(2)}, u32[]{:S(2)}) async-start(f32[16,2,128]{2,1,0:T(2,128)} %get-tuple-element.32), calls=%async_computation | async-start | bytes 32768 | tf_op jit(solution)/shard_map/all_to_all | solution.py:482
  19.9 0.7 copy-start
  19.9 0.7 copy-start.1
  22.3 7.1 %collective-permute-start.1 = (bf16[128,2048]{1,0:T(8,128)(2,1)S(1)}, bf16[128,2048]{1,0:T(8,128)(2,1)S(1)}, u32[]{:S(2)}, u32[]{:S(2)}) collective-permute-start(bf16[128,2048]{1,0:T(8,128)(2,1)S(1)} %broadcast_select_fusion), channel_id=1, source_target_pairs={{0,16},{16,0},{32,48},{48,32},{64,80},{80,64},{96,112},{112,96},{1... | collective-permute-start | bytes 1572872 | tf_op jit(solution)/shard_map/ppermute | solution.py:497
  37.5 10.6 %collective-permute-start.2 = (bf16[128,2048]{1,0:T(8,128)(2,1)}, bf16[128,2048]{1,0:T(8,128)(2,1)S(1)}, u32[]{:S(2)}, u32[]{:S(2)}) collective-permute-start(bf16[128,2048]{1,0:T(8,128)(2,1)} %get-tuple-element.35), channel_id=1, source_target_pairs={{0,16},{16,0},{32,48},{48,32},{64,80},{80,64},{96,112},{112,96},{1... | collective-permute-start | bytes 1572872 | tf_op jit(solution)/shard_map/ppermute | solution.py:500
  41.8 16.4 %all-to-all-start.1 = ((f32[64,2,128]{2,1,0:T(2,128)}), f32[64,2,128]{2,1,0:T(2,128)S(1)}, u32[]{:S(2)}, u32[]{:S(2)}) async-start(f32[64,2,128]{2,1,0:T(2,128)} %get-tuple-element.34), calls=%async_computation.1 | async-start | bytes 131072 | tf_op jit(solution)/shard_map/all_to_all | solution.py:482
  49.5 15.3 %collective-permute-start.3 = (bf16[128,2048]{1,0:T(8,128)(2,1)S(1)}, bf16[128,2048]{1,0:T(8,128)(2,1)S(1)}, u32[]{:S(2)}, u32[]{:S(2)}) collective-permute-start(bf16[128,2048]{1,0:T(8,128)(2,1)S(1)} %get-tuple-element.39), channel_id=1, source_target_pairs={{32,0},{48,16},{64,32},{80,48},{96,64},{112,80},{128,96},{144,112}... | collective-permute-start | bytes 1572872 | tf_op jit(solution)/shard_map/ppermute | solution.py:502
  58.9 11.9 %all-to-all-start.2 = ((f32[8,2,128]{2,1,0:T(2,128)}), f32[8,2,128]{2,1,0:T(2,128)S(1)}, u32[]{:S(2)}, u32[]{:S(2)}) async-start(f32[8,2,128]{2,1,0:T(2,128)} %add_up.3), calls=%async_computation.2 | async-start | bytes 16384 | tf_op jit(solution)/shard_map/all_to_all | solution.py:482

commit v6 on v5

--- a/solution.py
+++ b/solution.py
@@ -471,11 +471,11 @@
 
 
 def plane_groups():
-    return [[device_at(y, z, x, c) for z in range(8) for x in range(4) for c in range(2)] for y in range(8)]
+    return [[device_at(y, z, x, c) for y in range(8) for x in range(4) for c in range(2)] for z in range(8)]
 
 
 def column_groups():
-    return [[device_at(y, z, x, c) for y in range(8)] for z in range(8) for x in range(4) for c in range(2)]
+    return [[device_at(y, z, x, c) for z in range(8)] for y in range(8) for x in range(4) for c in range(2)]
 
 
 def swap(rows, groups):

time: 72 us -> 72 us (level)
  no operation moved by 1% of the time
where the time goes in v6:
time: 72 us; the launch traced here: 71.5 us
  starting transfers between devices  38.2 us (53%)
  waiting for transfers between devices  16.2 us (22%)
  Pallas kernels  14.9 us (21%)
  local copies, waits for them, and re-layouts  1.27 us (2%)
  between operations  0.79 us (1%)
    all_to_all x3, starting transfers between devices, swap(): lax.all_to_all(rows, AXES, 0, 0, axis_index_groups=groups, tiled=True)  25.5 us
    all_to_all x3, waiting for transfers between devices, swap(): lax.all_to_all(rows, AXES, 0, 0, axis_index_groups=groups, tiled=True)  15.6 us
    pallas_call x1, Pallas kernels, attend(): pl.pallas_call(attend_kernel, in_specs=[VMEM_IN] * 2 + [HBM_IN] * 2 + [VM...  8.14 us
    ppermute x1, starting transfers between devices, local(): near = lax.ppermute(ret1, 'seq', [(i, i ^ 1) for i in range(seq)])  4.29 us
    ppermute x1, starting transfers between devices, local(): two = lax.ppermute(own, 'seq', [(i, i + 2) for i in range(seq - 2)])  3.98 us
    ppermute x1, starting transfers between devices, local(): one = lax.ppermute(one, 'seq', [(i, i ^ 1) for i in range(seq)])  3.14 us
    pallas_call x1, Pallas kernels, finish(): pl.pallas_call(finish_kernel, in_specs=[VMEM_IN] * 5, out_specs=[HBM_IN]...  1.75 us
    pallas_call x1, Pallas kernels, block_tables(): pl.pallas_call(table_kernel, in_specs=[SMEM_IN, SMEM_IN, VMEM_IN, HBM_IN,...  1.59 us
  transfers between devices with their start and end apart: 7, of which 4 were waited for; matrix products, arithmetic and copies ran while one was open for 0% of the time, Pallas kernels for 7%

profile of v6, /device:TPU:1, one launch (start us, length us, event | category | flops | bytes accessed | tf_op | source)
XLA Modules:
  0.0 71.5 jit_solution(8829800966706418540)
XLA Ops:
  0.6 1.5 %pack.1 = (bf16[128,2048]{1,0:T(8,128)(2,1)S(1)}, f32[16,2,128]{2,1,0:T(2,128)}) custom-call(bf16[128,1024]{1,0:T(8,128)(2,1)} %bitcast.20, bf16[128,1024]{1,0:T(8,128)(2,1)} %bitcast.21, f32[8]{0:T(128)} %qg_in.1, f32[8]{0:T(128)} %kg_in.1, s32[1]{0:T(128)} %bitcast.6.shard_ref), custom_call_target="tpu_custom_call" | custom-call | tf_op jit(solution)/shard_map/pack/pallas_call | solution.py:154
  2.1 4.0 %collective-permute-start = (bf16[128,2048]{1,0:T(8,128)(2,1)S(1)}, bf16[128,2048]{1,0:T(8,128)(2,1)S(1)}, u32[]{:S(2)}, u32[]{:S(2)}) collective-permute-start(bf16[128,2048]{1,0:T(8,128)(2,1)S(1)} %get-tuple-element.27.own_ref), channel_id=1, source_target_pairs={{0,32},{16,48},{32,64},{48,80},{64,96},{80,112},{96,128},{112,144}... | collective-permute-start | bytes 1572872 | tf_op jit(solution)/shard_map/ppermute | solution.py:493
  6.1 13.8 %all-to-all-start = ((f32[16,2,128]{2,1,0:T(2,128)}), f32[16,2,128]{2,1,0:T(2,128)S(1)}, u32[]{:S(2)}, u32[]{:S(2)}) async-start(f32[16,2,128]{2,1,0:T(2,128)} %get-tuple-element.32), calls=%async_computation | async-start | bytes 32768 | tf_op jit(solution)/shard_map/all_to_all | solution.py:482
  19.9 0.0 copy-start
  19.9 0.0 copy-start.1
  19.9 0.6 copy-done
  20.6 0.0 copy-done.1
  20.6 1.6 %tables.1 = (f32[2,128,128]{2,1,0:T(8,128)S(1)}, f32[5,8,128]{2,1,0:T(8,128)S(1)}, bf16[128,1024]{1,0:T(8,128)(2,1)S(1)}, bf16[128,1024]{1,0:T(8,128)(2,1)S(1)}) custom-call(s32[48]{0:T(128)S(1)} %bitcast.15, s32[1]{0:T(128)} %bitcast.1.place_ref, f32[1,128]{1,0:T(1,128)S(1)} %copy-done.1, bf16[128,4096]{1,0:T(8,128)(2,1)} %bitcast.16, ...), custom_call_target="tpu_custom_call" | custom-call | tf_op jit(solution)/shard_map/tables/pallas_call | solution.py:107
  22.2 0.0 collective-permute-done.two_ref
  22.2 0.1 broadcast_select_fusion
  22.3 3.1 %collective-permute-start.1 = (bf16[128,2048]{1,0:T(8,128)(2,1)S(1)}, bf16[128,2048]{1,0:T(8,128)(2,1)S(1)}, u32[]{:S(2)}, u32[]{:S(2)}) collective-permute-start(bf16[128,2048]{1,0:T(8,128)(2,1)S(1)} %broadcast_select_fusion), channel_id=1, source_target_pairs={{0,16},{16,0},{32,48},{48,32},{64,80},{80,64},{96,112},{112,96},{1... | collective-permute-start | bytes 1572872 | tf_op jit(solution)/shard_map/ppermute | solution.py:497
  25.4 3.9 %all-to-all-done.parts_ref = f32[16,2,128]{2,1,0:T(2,128)S(1)} async-done(((f32[16,2,128]{2,1,0:T(2,128)}), f32[16,2,128]{2,1,0:T(2,128)S(1)}, u32[]{:S(2)}, u32[]{:S(2)}) %all-to-all-start) | async-done | bytes 16416 | tf_op jit(solution)/shard_map/all_to_all | solution.py:482
  29.4 0.0 collective-permute-done.1.one_ref
  29.4 8.1 %attend.1 = (bf16[128,4096]{1,0:T(8,128)(2,1)}, bf16[128,2048]{1,0:T(8,128)(2,1)}, bf16[128,2048]{1,0:T(8,128)(2,1)}, f32[128,2048]{1,0:T(8,128)S(1)}, f32[64,2,128]{2,1,0:T(2,128)}) custom-call(bf16[128,1024]{1,0:T(8,128)(2,1)S(1)} %get-tuple-element.25.q_first, bf16[128,1024]{1,0:T(8,128)(2,1)S(1)} %get-tuple-element.26.do_first, ...), custom_call_target="tpu_custom_call" | custom-call | tf_op jit(solution)/shard_map/attend/pallas_call | solution.py:337
  37.5 4.3 %collective-permute-start.2 = (bf16[128,2048]{1,0:T(8,128)(2,1)}, bf16[128,2048]{1,0:T(8,128)(2,1)S(1)}, u32[]{:S(2)}, u32[]{:S(2)}) collective-permute-start(bf16[128,2048]{1,0:T(8,128)(2,1)} %get-tuple-element.35), channel_id=1, source_target_pairs={{0,16},{16,0},{32,48},{48,32},{64,80},{80,64},{96,112},{112,96},{1... | collective-permute-start | bytes 1572872 | tf_op jit(solution)/shard_map/ppermute | solution.py:500
  41.8 6.4 %all-to-all-start.1 = ((f32[64,2,128]{2,1,0:T(2,128)}), f32[64,2,128]{2,1,0:T(2,128)S(1)}, u32[]{:S(2)}, u32[]{:S(2)}) async-start(f32[64,2,128]{2,1,0:T(2,128)} %get-tuple-element.34), calls=%async_computation.1 | async-start | bytes 131072 | tf_op jit(solution)/shard_map/all_to_all | solution.py:482
  48.2 0.0 collective-permute-done.2.near_ref
  48.2 1.3 %merge.1 = (bf16[128,2048]{1,0:T(8,128)(2,1)S(1)}, f32[128,2048]{1,0:T(8,128)S(1)}) custom-call(s32[1]{0:T(128)} %bitcast.8.odd_ref, bf16[128,2048]{1,0:T(8,128)(2,1)S(1)} %collective-permute-done.2.near_ref, bf16[128,2048]{1,0:T(8,128)(2,1)} %get-tuple-element.36.ret_in, f32[128,2048]{1,0:T(8,128)S(1)} %get-tuple-element.37.keep_in), custom_call_target="tpu_custom_call", output_to_operand_aliasing={{1}: (3, {})} | custom-call | tf_op jit(solution)/shard_map/merge/pallas_call | solution.py:407
  49.6 1.3 %collective-permute-start.3 = (bf16[128,2048]{1,0:T(8,128)(2,1)S(1)}, bf16[128,2048]{1,0:T(8,128)(2,1)S(1)}, u32[]{:S(2)}, u32[]{:S(2)}) collective-permute-start(bf16[128,2048]{1,0:T(8,128)(2,1)S(1)} %get-tuple-element.39), channel_id=1, source_target_pairs={{32,0},{48,16},{64,32},{80,48},{96,64},{112,80},{128,96},{144,112}... | collective-permute-start | bytes 1572872 | tf_op jit(solution)/shard_map/ppermute | solution.py:502
  50.9 7.4 %all-to-all-done.1.parts_ref = f32[64,2,128]{2,1,0:T(2,128)S(1)} async-done(((f32[64,2,128]{2,1,0:T(2,128)}), f32[64,2,128]{2,1,0:T(2,128)S(1)}, u32[]{:S(2)}, u32[]{:S(2)}) %all-to-all-start.1) | async-done | bytes 65568 | tf_op jit(solution)/shard_map/all_to_all | solution.py:482
  58.3 0.7 add_up.3
  59.0 5.3 %all-to-all-start.2 = ((f32[8,2,128]{2,1,0:T(2,128)}), f32[8,2,128]{2,1,0:T(2,128)S(1)}, u32[]{:S(2)}, u32[]{:S(2)}) async-start(f32[8,2,128]{2,1,0:T(2,128)} %add_up.3), calls=%async_computation.2 | async-start | bytes 16384 | tf_op jit(solution)/shard_map/all_to_all | solution.py:482
  64.2 0.6 collective-permute-done.3.far_ref
  64.9 1.7 %finish.1 = (bf16[128,1024]{1,0:T(8,128)(2,1)}, bf16[128,1024]{1,0:T(8,128)(2,1)}) custom-call(bf16[128,2048]{1,0:T(8,128)(2,1)S(1)} %get-tuple-element.27.own_ref, f32[128,2048]{1,0:T(8,128)S(1)} %get-tuple-element.38.keep_ref, bf16[128,2048]{1,0:T(8,128)(2,1)S(1)} %collective-permute-done.3.far_ref, f32[2,128,128]{2,1,0:T(8,128)S(1)} %get-tuple-element.30.table_ref, ...), custom_call_target="tpu_custom_call" | custom-call | tf_op jit(solution)/shard_map/finish/pallas_call | solution.py:445
  66.6 4.2 %all-to-all-done.2 = f32[8,2,128]{2,1,0:T(2,128)S(1)} async-done(((f32[8,2,128]{2,1,0:T(2,128)}), f32[8,2,128]{2,1,0:T(2,128)S(1)}, u32[]{:S(2)}, u32[]{:S(2)}) %all-to-all-start.2) | async-done | bytes 8224 | tf_op jit(solution)/shard_map/all_to_all | solution.py:482
  70.8 0.1 reshape.13
  70.9 0.5 dynamic-slice_bitcast_fusion
  (2 shorter events, 0.0 us)
Async XLA Ops:
  2.1 20.1 %collective-permute-start = (bf16[128,2048]{1,0:T(8,128)(2,1)S(1)}, bf16[128,2048]{1,0:T(8,128)(2,1)S(1)}, u32[]{:S(2)}, u32[]{:S(2)}) collective-permute-start(bf16[128,2048]{1,0:T(8,128)(2,1)S(1)} %get-tuple-element.27.own_ref), channel_id=1, source_target_pairs={{0,32},{16,48},{32,64},{48,80},{64,96},{80,112},{96,128},{112,144}... | collective-permute-start | bytes 1572872 | tf_op jit(solution)/shard_map/ppermute | solution.py:493
  6.1 23.3 %all-to-all-start = ((f32[16,2,128]{2,1,0:T(2,128)}), f32[16,2,128]{2,1,0:T(2,128)S(1)}, u32[]{:S(2)}, u32[]{:S(2)}) async-start(f32[16,2,128]{2,1,0:T(2,128)} %get-tuple-element.32), calls=%async_computation | async-start | bytes 32768 | tf_op jit(solution)/shard_map/all_to_all | solution.py:482
  19.9 0.7 copy-start
  19.9 0.7 copy-start.1
  22.3 7.1 %collective-permute-start.1 = (bf16[128,2048]{1,0:T(8,128)(2,1)S(1)}, bf16[128,2048]{1,0:T(8,128)(2,1)S(1)}, u32[]{:S(2)}, u32[]{:S(2)}) collective-permute-start(bf16[128,2048]{1,0:T(8,128)(2,1)S(1)} %broadcast_select_fusion), channel_id=1, source_target_pairs={{0,16},{16,0},{32,48},{48,32},{64,80},{80,64},{96,112},{112,96},{1... | collective-permute-start | bytes 1572872 | tf_op jit(solution)/shard_map/ppermute | solution.py:497
  37.5 10.7 %collective-permute-start.2 = (bf16[128,2048]{1,0:T(8,128)(2,1)}, bf16[128,2048]{1,0:T(8,128)(2,1)S(1)}, u32[]{:S(2)}, u32[]{:S(2)}) collective-permute-start(bf16[128,2048]{1,0:T(8,128)(2,1)} %get-tuple-element.35), channel_id=1, source_target_pairs={{0,16},{16,0},{32,48},{48,32},{64,80},{80,64},{96,112},{112,96},{1... | collective-permute-start | bytes 1572872 | tf_op jit(solution)/shard_map/ppermute | solution.py:500
  41.8 16.5 %all-to-all-start.1 = ((f32[64,2,128]{2,1,0:T(2,128)}), f32[64,2,128]{2,1,0:T(2,128)S(1)}, u32[]{:S(2)}, u32[]{:S(2)}) async-start(f32[64,2,128]{2,1,0:T(2,128)} %get-tuple-element.34), calls=%async_computation.1 | async-start | bytes 131072 | tf_op jit(solution)/shard_map/all_to_all | solution.py:482
  49.6 15.3 %collective-permute-start.3 = (bf16[128,2048]{1,0:T(8,128)(2,1)S(1)}, bf16[128,2048]{1,0:T(8,128)(2,1)S(1)}, u32[]{:S(2)}, u32[]{:S(2)}) collective-permute-start(bf16[128,2048]{1,0:T(8,128)(2,1)S(1)} %get-tuple-element.39), channel_id=1, source_target_pairs={{32,0},{48,16},{64,32},{80,48},{96,64},{112,80},{128,96},{144,112}... | collective-permute-start | bytes 1572872 | tf_op jit(solution)/shard_map/ppermute | solution.py:502
  59.0 11.9 %all-to-all-start.2 = ((f32[8,2,128]{2,1,0:T(2,128)}), f32[8,2,128]{2,1,0:T(2,128)S(1)}, u32[]{:S(2)}, u32[]{:S(2)}) async-start(f32[8,2,128]{2,1,0:T(2,128)} %add_up.3), calls=%async_computation.2 | async-start | bytes 16384 | tf_op jit(solution)/shard_map/all_to_all | solution.py:482
